TPU v7x, 32 devices: a whole 2x2x4 slice. The times are simulated.
32 devices in a mesh: groups: 2 (over y), tm: 4 (over z), space: 2 (over x), chan: 2 (over core).
Axes of the slice: x: 2, y: 2, z: 4, core: 2. Of those that a mesh axis runs over, the one named last changes fastest.
Arguments:
- activations: bfloat16 [256, 8, 16, 256], P(('groups', 'chan'), 'tm', 'space'), parts along dimension 0
- frame_clip: int32 [16], P(('groups', 'tm')), parts along dimension 0, may hold values from 0 to 3, as said below
- conv_weight: bfloat16 [3, 3, 3, 128, 128], replicated, may hold values from -0.109375 to 0.109375
- norm_gain: float32 [128], replicated, may hold values from 0.25 to 1.75
- norm_bias: float32 [128], replicated, may hold values from -3 to 3
- out_weight: bfloat16 [2, 2, 128, 32], replicated, may hold values from -0.25 to 0.25
- owner: int32 [4, 32, 1], P(('groups', 'space'), 'tm'), parts along dimension 0, may hold values from 0 to 3; in each aligned block of 8 rows (0 to 7, 8 to 15, ..., all dimensions but the last counted through in order) at most 4 rows name the same one
Outputs:
- owned: bfloat16 [4, 64, 32, 128], P(('groups', 'space'), 'tm', 'chan'), parts along dimension 0
There are 2 independent parts, one for each index of `groups`. A program takes and returns all parts, laid end to end along the dimension named above; an argument that names none is the same for every part. Nothing has to cross between parts.
Inputs may be any that keep to these rules, and one draw needn't show every extreme that they name: `frame_clip`: clip numbers never fall along the frames; each clip has 1 to 4 frames and one has exactly 4. Among the 8 rows of one tm index (aligned blocks), no owner is named more than 4 times; some owner is named exactly 4 times in some block.
All inputs are finite; a program needn't handle non-finite values.
Results may differ from a plain program's by a relative error of at most 0.012.
Values may be sent and summed in bfloat16 or wider, within the bound.
No kernel may reach another device: no remote copies, remote signals or barrier semaphores. Data moves between devices by JAX's collectives and lax.ppermute only.
A program may use at most 64 MiB of HBM per device.

v0:
```python
import jax
import jax.numpy as jnp
from jax import lax
from jax.sharding import PartitionSpec as P

CHANNELS = 128
GROUPS = 32
CLIPS = 4
MOMENTS = 32


def shifted(value, axis, steps):
    count = lax.axis_size(axis)
    leading, last = (max(0, -steps), min(count, count - steps))
    return lax.ppermute(value, axis, [(source, source + steps) for source in range(leading, last)])


def with_halo(block, sides, width):
    for axis, dim in sides:
        count = lax.axis_size(axis)
        forward = [(i, i + 1) for i in range(count - 1)]
        backward = [(target, source) for source, target in forward]
        low = lax.ppermute(
            lax.slice_in_dim(block, block.shape[dim] - width, None, axis=dim), axis, forward
        )
        high = lax.ppermute(lax.slice_in_dim(block, 0, width, axis=dim), axis, backward)
        block = jnp.concatenate([low, block, high], axis=dim)
    return block


def plane_conv(frames, kernel):
    return lax.conv_general_dilated(
        frames,
        kernel,
        (1, 1),
        ((0, 0), (1, 1)),
        dimension_numbers=("CNHW", "HWIO", "CNHW"),
        preferred_element_type=jnp.float32,
    )


def shards(activations, frame_clip, conv_weight, norm_gain, norm_bias, out_weight, owner):
    c_local, frames_here, rows_here, columns = activations.shape
    chan_index = lax.axis_index("chan")
    chan_first = chan_index * c_local
    trailing_ids = (frame_clip + 1).astype(jnp.bfloat16)
    previous, previous_ids = shifted((activations, trailing_ids), "tm", 1)
    extended = jnp.concatenate([previous, activations], axis=1)
    extended_ids = jnp.concatenate(
        [previous_ids.astype(jnp.float32), (frame_clip + 1).astype(jnp.float32)]
    )
    padded = with_halo(extended, (("space", 2),), 1)
    own_ids = extended_ids[2:]
    matches = [(extended_ids[m : m + frames_here] == own_ids).astype(jnp.int32) for m in range(3)]
    position = jnp.arange(frames_here, dtype=jnp.int32)
    tap_index = []
    for k in range(3):
        number = matches[k]
        for m in range(k + 1, 3):
            number = number + matches[m]
        tap_index.append(position + 3 - number)
    chan_count = lax.axis_size("chan")
    window = frames_here // chan_count
    windows = jnp.stack(
        [padded[:, w * window : w * window + window + 2] for w in range(chan_count)], axis=1
    )
    whole_window = lax.all_to_all(windows, "chan", split_axis=1, concat_axis=0, tiled=True)[:, 0]
    window_start = chan_index * window
    running = None
    for k in range(3):
        local_taps = lax.dynamic_slice_in_dim(tap_index[k], window_start, window) - window_start
        term = plane_conv(jnp.take(whole_window, local_taps, axis=1), conv_weight[k])
        running = term if running is None else running + term
    conv_window = running.astype(jnp.bfloat16)
    conv_full = lax.all_to_all(conv_window, "chan", split_axis=0, concat_axis=1, tiled=True).astype(
        jnp.float32
    )
    conv_value = conv_full.astype(jnp.bfloat16).astype(jnp.float32)
    group_size = CHANNELS // GROUPS
    local_groups = c_local // group_size
    onehot = (frame_clip[:, None] == jnp.arange(CLIPS, dtype=jnp.int32)[None, :]).astype(
        jnp.float32
    )
    sums_one = (
        jnp.sum(conv_value, axis=(2, 3)).reshape(local_groups, group_size, frames_here).sum(1)
    )
    sums_two = (
        jnp.sum(conv_value * conv_value, axis=(2, 3))
        .reshape(local_groups, group_size, frames_here)
        .sum(1)
    )
    sums_one = jnp.dot(sums_one, onehot, precision=lax.Precision.HIGHEST)
    sums_two = jnp.dot(sums_two, onehot, precision=lax.Precision.HIGHEST)
    counts_here = jnp.sum(onehot, axis=0) * (rows_here * columns * group_size)
    sums_one, sums_two, counts = lax.psum((sums_one, sums_two, counts_here), ("tm", "space"))
    mean = sums_one / counts
    rstd = lax.rsqrt(sums_two / counts - mean * mean + 1e-06)
    mean_frame = jnp.repeat(
        jnp.dot(mean, onehot.T, precision=lax.Precision.HIGHEST), group_size, axis=0
    )
    rstd_frame = jnp.repeat(
        jnp.dot(rstd, onehot.T, precision=lax.Precision.HIGHEST), group_size, axis=0
    )
    gain_here = lax.dynamic_slice_in_dim(norm_gain, chan_first, c_local)
    bias_here = lax.dynamic_slice_in_dim(norm_bias, chan_first, c_local)
    scaled = (conv_value - mean_frame[:, :, None, None]) * rstd_frame[:, :, None, None]
    normed = jax.nn.silu(
        scaled * gain_here[:, None, None, None] + bias_here[:, None, None, None]
    ).astype(jnp.bfloat16)
    patches = normed.reshape(c_local, frames_here, rows_here // 2, 2, columns // 2, 2)
    weight_here = lax.dynamic_slice(out_weight, (0, 0, chan_first, 0), (2, 2, c_local, MOMENTS))
    latent = lax.psum_scatter(
        jnp.einsum("cfrizj,ijco->ofrz", patches, weight_here, preferred_element_type=jnp.float32),
        "chan",
        scatter_dimension=0,
        tiled=True,
    ).astype(jnp.bfloat16)
    moments_here = latent.shape[0]
    send_rows = frames_here * (rows_here // 2)
    row_block = latent.reshape(moments_here, send_rows, columns // 2)
    tm_size = lax.axis_size("tm")
    capacity = max(2, 2 * send_rows // tm_size)
    targets = owner[0, :, 0]
    earlier = jnp.arange(send_rows)[None, :] < jnp.arange(send_rows)[:, None]
    equal = targets[:, None] == targets[None, :]
    order_rank = jnp.sum((equal & earlier).astype(jnp.int32), axis=1)
    slot_of_row = targets * capacity + order_rank
    selector = (
        slot_of_row[None, :] == jnp.arange(tm_size * capacity, dtype=jnp.int32)[:, None]
    ).astype(jnp.bfloat16)
    outgoing = jnp.einsum(
        "sr,crw->scw", selector, row_block, preferred_element_type=jnp.float32
    ).astype(jnp.bfloat16)
    arrived = lax.all_to_all(outgoing, "tm", split_axis=0, concat_axis=0, tiled=True)
    return arrived[None]


def solution(mesh):
    placed = (
        P(("groups", "chan"), "tm", "space", None),
        P(("groups", "tm")),
        P(),
        P(),
        P(),
        P(),
        P(("groups", "space"), "tm", None),
    )
    return jax.shard_map(
        shards,
        mesh=mesh,
        in_specs=placed,
        out_specs=P(("groups", "space"), "tm", "chan", None),
        check_vma=False,
    )
```

profile of v0, /device:TPU:0, one launch (start us, length us, event | category | flops | bytes accessed | tf_op | source)
XLA Modules:
  0.0 105.6 jit_solution(17287263570309921566)
XLA Ops:
  6.5 1.3 %copy.97 = bf16[64,2,8,256]{3,0,2,1:T(8,128)(2,1)S(1)} copy(bf16[64,2,8,256]{3,2,1,0:T(8,128)(2,1)} %param.9) | data formatting | bytes 1048576 | tf_op args[0]
  7.8 5.0 %collective-permute-start = (bf16[64,2,8,256]{3,0,2,1:T(8,128)(2,1)S(1)}, bf16[64,2,8,256]{3,0,2,1:T(8,128)(2,1)S(1)}, u32[]{:S(2)}, u32[]{:S(2)}) collective-permute-start(bf16[64,2,8,256]{3,0,2,1:T(8,128)(2,1)S(1)} %copy.97), channel_id=1, source_target_pairs={{0,4},{4,8},{8,12},{1,5},{5,9},{9,13},{2,6},{6,10},{10,14},{3,7},{... | collective-permute-start | bytes 1572872 | tf_op jit(solution)/shard_map/ppermute | solution.py:15
  12.8 0.7 add_convert_fusion.1
  13.5 3.4 %collective-permute-start.3 = (bf16[2]{0:T(256)(128)(2,1)S(1)}, bf16[2]{0:T(256)(128)(2,1)S(1)}, u32[]{:S(2)}, u32[]{:S(2)}) collective-permute-start(bf16[2]{0:T(256)(128)(2,1)S(1)} %get-tuple-element.32), channel_id=1, source_target_pairs={{0,4},{4,8},{8,12},{1,5},{5,9},{9,13},{2,6},{6,10},{10,14},{3,7},{... | collective-permute-start | bytes 20 | tf_op jit(solution)/shard_map/ppermute | solution.py:15
  16.9 0.7 dynamic_slice.23
  17.6 0.7 dynamic_slice.22
  18.4 0.7 convert_reduce_fusion.1
  19.1 4.9 %collective-permute-done.3 = bf16[2]{0:T(256)(128)(2,1)S(1)} collective-permute-done((bf16[2]{0:T(256)(128)(2,1)S(1)}, bf16[2]{0:T(256)(128)(2,1)S(1)}, u32[]{:S(2)}, u32[]{:S(2)}) %collective-permute-start.3) | collective-permute-done | bytes 36 | tf_op jit(solution)/shard_map/ppermute | solution.py:15
  24.3 1.3 %collective-permute-start.2 = (bf16[64,4,1,256]{3,0,2,1:T(8,128)(2,1)S(1)}, bf16[64,4,1,256]{3,0,2,1:T(8,128)(2,1)S(1)}, u32[]{:S(2)}, u32[]{:S(2)}) collective-permute-start(bf16[64,4,1,256]{3,0,2,1:T(8,128)(2,1)S(1)} %get-tuple-element.28), channel_id=1, source_target_pairs={{2,0},{3,1},{6,4},{7,5},{10,8},{11,9},{14,12},{15,13},{18,16},{19,... | collective-permute-start | bytes 393224 | tf_op jit(solution)/shard_map/ppermute | solution.py:26
  25.6 4.6 %collective-permute-start.1 = (bf16[64,4,1,256]{3,0,2,1:T(8,128)(2,1)S(1)}, bf16[64,4,1,256]{3,0,2,1:T(8,128)(2,1)S(1)}, u32[]{:S(2)}, u32[]{:S(2)}) collective-permute-start(bf16[64,4,1,256]{3,0,2,1:T(8,128)(2,1)S(1)} %get-tuple-element.27), channel_id=1, source_target_pairs={{0,2},{1,3},{4,6},{5,7},{8,10},{9,11},{12,14},{13,15},{16,18},{17,... | collective-permute-start | bytes 393224 | tf_op jit(solution)/shard_map/ppermute | solution.py:23
  31.6 0.7 dynamic_slice.20
  34.9 5.3 %all_to_all.29 = bf16[64,2,3,10,256]{4,0,3,2,1:T(8,128)(2,1)S(1)} all-to-all(bf16[64,2,3,10,256]{4,0,3,2,1:T(8,128)(2,1)S(1)} %pad_maximum_fusion), channel_id=1, replica_groups=mesh['groups'=2,'tm'=4,'space'=2,'chan'=2] {'chan'}, dimensions={1} | all-to-all | bytes 3932160 | tf_op jit(solution)/shard_map/all_to_all | solution.py:67
  42.4 0.8 copy-done.2
  44.4 0.7 copy-done.5
  45.2 1.5 %convolution_select_fusion.1 = f32[8,8,33,128]{3,1,2,0:T(8,128)S(1)} fusion(bf16[128,10,1,7,2]{0,3,4,1,2:T(8,128)(2,1)S(1)} %slice.52, bf16[128,10,1,8,33]{0,3,4,1,2:T(8,128)(2,1)S(1)} %copy.105, pred[8,33]{0,1:T(8,128)(4,1)S(1)} %copy-done.7, bf16[3,3,3,128,128]{4,3,2,1,0:T(8,128)(2,1)S(1)} %copy-done.5), kind=kOutput, calls=%fused_computation.6 | convolution fusion | flops 625274880 | bytes 2098176 | tf_op jit(solution)/shard_map/conv_general_dilated | solution.py:32
  46.6 1.5 %fusion.3 = f32[8,8,33,128]{3,1,2,0:T(8,128)S(1)} fusion(f32[8,8,33,128]{3,1,2,0:T(8,128)S(1)} %convolution_select_fusion.1, bf16[128,10,1,7,2]{0,3,4,1,2:T(8,128)(2,1)S(1)} %slice.51, bf16[128,10,1,8,33]{0,3,4,1,2:T(8,128)(2,1)S(1)} %copy-done.3, pred[8,33]{0,1:T(8,128)(4,1)S(1)} %copy-done.7, bf16[3,3,3,128,128]{4,3,2,1,0:T(8,128)(2,1)S(1)} %copy-done.5), kind=kOutput, calls=%fused_computation.8 | convolution fusion | flops 625545216 | bytes 3179520 | tf_op jit(solution)/shard_map/conv_general_dilated | solution.py:32
  48.1 1.5 %fusion.5 = bf16[8,8,33,128]{3,1,2,0:T(8,128)(2,1)S(1)} fusion(f32[8,8,33,128]{3,1,2,0:T(8,128)S(1)} %fusion.3, bf16[128,10,1,7,2]{0,3,4,1,2:T(8,128)(2,1)S(1)} %slice.53, bf16[128,10,1,8,33]{0,3,4,1,2:T(8,128)(2,1)S(1)} %copy.108, pred[8,33]{0,1:T(8,128)(4,1)S(1)} %copy-done.7, bf16[3,3,3,128,128]{4,3,2,1,0:T(8,128)(2,1)S(1)} %copy-done.5), kind=kOutput, calls=%fused_computation.11 | convolution fusion | flops 625815552 | bytes 2638848 | tf_op jit(solution)/shard_map/conv_general_dilated | solution.py:32
  50.3 4.2 %all_to_all.30 = bf16[128,1,8,256]{3,2,1,0:T(8,128)(2,1)S(1)} all-to-all(bf16[128,1,8,256]{3,2,1,0:T(8,128)(2,1)S(1)} %copy.110), channel_id=1, replica_groups=mesh['groups'=2,'tm'=4,'space'=2,'chan'=2] {'chan'}, dimensions={0} | all-to-all | bytes 1048576 | tf_op jit(solution)/shard_map/all_to_all | solution.py:75
  55.8 0.9 copy.113
  57.5 22.1 %all-reduce = (f32[16,4]{0,1:T(4,128)S(1)}, f32[4]{0:T(128)S(1)}, f32[16,4]{0,1:T(4,128)S(1)}) all-reduce(f32[16,4]{0,1:T(4,128)S(1)} %fusion.46, f32[4]{0:T(128)S(1)} %broadcast_multiply_fusion, f32[16,4]{0,1:T(4,128)S(1)} %fusion.48), channel_id=1, replica_groups=mesh['groups'=2,'tm'=4,'space'=2,'chan'=2] {'tm','space'}, use_global_device_ids=true, to_apply=%region_8.10 | all-reduce | flops 132 | bytes 1056 | tf_op jit(solution)/shard_map/psum | solution.py:95
  80.4 1.2 %convolution_bitcast_fusion = f32[32,2,4,128]{3,0,2,1:T(8,128)} fusion(f32[64,2,4,2,128,2]{4,0,5,3,2,1:T(8,128)S(1)} %copy.113, f32[64]{0:T(128)S(1)} %dynamic_slice.23, f32[64]{0:T(128)S(1)} %dynamic_slice.22, f32[64,2]{0,1:T(2,128)S(1)} %mul.50, f32[64,2]{0,1:T(2,128)S(1)} %sub.44, bf16[2,2,128,32]{2,3,1,0:T(8,128)(2,1)S(1)} %copy-done, s32[]{:T(128)S(6)} %select_n.25), kind=kOutput, calls=%fused_computation.12 | convolution fusion | flops 19136512 | bytes 1213956 | tf_op jit(solution)/shard_map/cfrizj,ijco->ofrz/dot_general | solution.py:113
  81.8 4.7 %reduce-scatter.2.cloned.1.call-done = f32[16,2,4,128]{3,0,2,1:T(8,128)} async-done(((f32[32,2,4,128]{3,0,2,1:T(8,128)}), f32[16,2,4,128]{3,0,2,1:T(8,128)}) %reduce-scatter.2.cloned.1.call-update) | async-done | bytes 65552 | tf_op jit(solution)/shard_map/reduce_scatter | solution.py:112
  86.6 0.8 convert_element_type.73
  87.7 10.4 %all_to_all.31 = bf16[16,16,128]{2,1,0:T(8,128)(2,1)S(1)} all-to-all(bf16[16,16,128]{2,1,0:T(8,128)(2,1)S(1)} %copy.115), channel_id=1, replica_groups=mesh['groups'=2,'tm'=4,'space'=2,'chan'=2] {'tm'}, dimensions={0} | all-to-all | bytes 131072 | tf_op jit(solution)/shard_map/all_to_all | solution.py:134
  (71 shorter events, 10.2 us)
Async XLA Ops:
  6.5 73.9 %copy-start = (bf16[2,2,128,32]{2,3,1,0:T(8,128)(2,1)S(1)}, bf16[2,2,128,32]{2,3,1,0:T(8,128)(2,1)}, u32[]{:S(2)}) copy-start(bf16[2,2,128,32]{2,3,1,0:T(8,128)(2,1)} %param.14) | copy-start | bytes 98308
  6.5 17.6 %copy-start.1 = (bf16[64,2,8,256]{3,2,1,0:T(8,128)(2,1)S(1)}, bf16[64,2,8,256]{3,2,1,0:T(8,128)(2,1)}, u32[]{:S(2)}) copy-start(bf16[64,2,8,256]{3,2,1,0:T(8,128)(2,1)} %param.9) | copy-start | bytes 1572868
  6.5 80.0 %reduce-scatter.2.cloned.1.call-start = ((), (), s32[]{:S(2)}) async-start(), calls=%async_computation.4 | async-start | bytes 196608 | tf_op jit(solution)/shard_map/reduce_scatter | solution.py:112
  7.8 22.4 %copy-start.4 = (s32[2]{0:T(128)S(1)}, s32[2]{0:T(128)}, u32[]{:S(2)}) copy-start(s32[2]{0:T(128)} %param.10) | copy-start | bytes 28
  7.8 16.2 %collective-permute-start = (bf16[64,2,8,256]{3,0,2,1:T(8,128)(2,1)S(1)}, bf16[64,2,8,256]{3,0,2,1:T(8,128)(2,1)S(1)}, u32[]{:S(2)}, u32[]{:S(2)}) collective-permute-start(bf16[64,2,8,256]{3,0,2,1:T(8,128)(2,1)S(1)} %copy.97), channel_id=1, source_target_pairs={{0,4},{4,8},{8,12},{1,5},{5,9},{9,13},{2,6},{6,10},{10,14},{3,7},{... | collective-permute-start | bytes 1572872 | tf_op jit(solution)/shard_map/ppermute | solution.py:15
  13.5 10.5 %collective-permute-start.3 = (bf16[2]{0:T(256)(128)(2,1)S(1)}, bf16[2]{0:T(256)(128)(2,1)S(1)}, u32[]{:S(2)}, u32[]{:S(2)}) collective-permute-start(bf16[2]{0:T(256)(128)(2,1)S(1)} %get-tuple-element.32), channel_id=1, source_target_pairs={{0,4},{4,8},{8,12},{1,5},{5,9},{9,13},{2,6},{6,10},{10,14},{3,7},{... | collective-permute-start | bytes 20 | tf_op jit(solution)/shard_map/ppermute | solution.py:15
  24.3 10.0 %collective-permute-start.2 = (bf16[64,4,1,256]{3,0,2,1:T(8,128)(2,1)S(1)}, bf16[64,4,1,256]{3,0,2,1:T(8,128)(2,1)S(1)}, u32[]{:S(2)}, u32[]{:S(2)}) collective-permute-start(bf16[64,4,1,256]{3,0,2,1:T(8,128)(2,1)S(1)} %get-tuple-element.28), channel_id=1, source_target_pairs={{2,0},{3,1},{6,4},{7,5},{10,8},{11,9},{14,12},{15,13},{18,16},{19,... | collective-permute-start | bytes 393224 | tf_op jit(solution)/shard_map/ppermute | solution.py:26
  25.6 8.7 %collective-permute-start.1 = (bf16[64,4,1,256]{3,0,2,1:T(8,128)(2,1)S(1)}, bf16[64,4,1,256]{3,0,2,1:T(8,128)(2,1)S(1)}, u32[]{:S(2)}, u32[]{:S(2)}) collective-permute-start(bf16[64,4,1,256]{3,0,2,1:T(8,128)(2,1)S(1)} %get-tuple-element.27), channel_id=1, source_target_pairs={{0,2},{1,3},{4,6},{5,7},{8,10},{9,11},{12,14},{13,15},{16,18},{17,... | collective-permute-start | bytes 393224 | tf_op jit(solution)/shard_map/ppermute | solution.py:23
  42.4 0.9 copy-start.2
  43.8 0.7 copy-start.7
  44.0 1.2 %copy-start.5 = (bf16[3,3,3,128,128]{4,3,2,1,0:T(8,128)(2,1)S(1)}, bf16[3,3,3,128,128]{4,3,2,1,0:T(8,128)(2,1)}, u32[]{:S(2)}) copy-start(bf16[3,3,3,128,128]{4,3,2,1,0:T(8,128)(2,1)} %param.11) | copy-start | bytes 2654212
  45.2 1.5 %copy-start.3 = (bf16[128,10,1,8,33]{0,3,4,1,2:T(8,128)(2,1)S(1)}, bf16[128,10,1,8,33]{0,3,4,1,2:T(8,128)(2,1)}, u32[]{:S(2)}) copy-start(bf16[128,10,1,8,33]{0,3,4,1,2:T(8,128)(2,1)} %copy-done.2) | copy-start | bytes 2027524
  80.4 1.2 %copy-start.6 = (s32[1,8,1]{1,2,0:T(1,128)S(1)}, s32[1,8,1]{1,2,0:T(1,128)}, u32[]{:S(2)}) copy-start(s32[1,8,1]{1,2,0:T(1,128)} %param.15) | copy-start | bytes 100
Sparse Core Ops, SparseCore 0:
  81.8 4.7 reduce-scatter.1
where the time goes:
time: 106 us
  blocking collectives  42 us (40%)
  between operations  15.9 us (15%)
  starting transfers between devices  14.3 us (13%)
  local copies, waits for them, and re-layouts  13.1 us (12%)
  waiting for transfers between devices  9.62 us (9%)
  matrix products  6.8 us (6%)
  other arithmetic  3.95 us (4%)
    psum x1, blocking collectives, shards(): lax.psum((sums_one, sums_two, counts_here), ('tm', 'space'))  22.1 us
    all_to_all x1, blocking collectives, shards(): lax.all_to_all(outgoing, 'tm', split_axis=0, concat_axis=0, tiled=True)  10.4 us
    ppermute x2, starting transfers between devices, shifted(): lax.ppermute(value, axis, [(source, source + steps) for source in range(l...  8.4 us
    all_to_all x1, blocking collectives, shards(): lax.all_to_all(windows, 'chan', split_axis=1, concat_axis=0, tiled=True)  5.31 us
    unnamed x22, local copies, waits for them, and re-layouts  4.86 us
    ppermute x2, waiting for transfers between devices, shifted(): lax.ppermute(value, axis, [(source, source + steps) for source in range(l...  4.86 us
    reduce_scatter x1, waiting for transfers between devices, shards(): lax.psum_scatter(jnp.einsum('cfrizj,ijco->ofrz', patches, weight_here, pr...  4.74 us
    ppermute x1, starting transfers between devices, with_halo(): lax.ppermute(lax.slice_in_dim(block, block.shape[dim] - width, None, axis...  4.56 us
  transfers between devices with their start and end apart: 5, of which 2 were waited for; matrix products, arithmetic and copies ran while one was open for 5% of the time, Pallas kernels for 0%

commit v1 on v0

--- a/solution.py
+++ b/solution.py
@@ -71,68 +71,67 @@
         local_taps = lax.dynamic_slice_in_dim(tap_index[k], window_start, window) - window_start
         term = plane_conv(jnp.take(whole_window, local_taps, axis=1), conv_weight[k])
         running = term if running is None else running + term
-    conv_window = running.astype(jnp.bfloat16)
-    conv_full = lax.all_to_all(conv_window, "chan", split_axis=0, concat_axis=1, tiled=True).astype(
-        jnp.float32
-    )
-    conv_value = conv_full.astype(jnp.bfloat16).astype(jnp.float32)
+    conv_value = running.astype(jnp.bfloat16).astype(jnp.float32)
+    tm_size = lax.axis_size("tm")
+    parts = tm_size * lax.axis_size("space") * chan_count
     group_size = CHANNELS // GROUPS
-    local_groups = c_local // group_size
-    onehot = (frame_clip[:, None] == jnp.arange(CLIPS, dtype=jnp.int32)[None, :]).astype(
-        jnp.float32
-    )
-    sums_one = (
-        jnp.sum(conv_value, axis=(2, 3)).reshape(local_groups, group_size, frames_here).sum(1)
-    )
-    sums_two = (
-        jnp.sum(conv_value * conv_value, axis=(2, 3))
-        .reshape(local_groups, group_size, frames_here)
-        .sum(1)
-    )
-    sums_one = jnp.dot(sums_one, onehot, precision=lax.Precision.HIGHEST)
-    sums_two = jnp.dot(sums_two, onehot, precision=lax.Precision.HIGHEST)
-    counts_here = jnp.sum(onehot, axis=0) * (rows_here * columns * group_size)
-    sums_one, sums_two, counts = lax.psum((sums_one, sums_two, counts_here), ("tm", "space"))
-    mean = sums_one / counts
-    rstd = lax.rsqrt(sums_two / counts - mean * mean + 1e-06)
-    mean_frame = jnp.repeat(
-        jnp.dot(mean, onehot.T, precision=lax.Precision.HIGHEST), group_size, axis=0
-    )
-    rstd_frame = jnp.repeat(
-        jnp.dot(rstd, onehot.T, precision=lax.Precision.HIGHEST), group_size, axis=0
-    )
-    gain_here = lax.dynamic_slice_in_dim(norm_gain, chan_first, c_local)
-    bias_here = lax.dynamic_slice_in_dim(norm_bias, chan_first, c_local)
+    send_rows = frames_here * (rows_here // 2)
+    sums_one = jnp.sum(conv_value, axis=(2, 3)).reshape(GROUPS, group_size, window).sum(1)
+    sums_two = jnp.sum(conv_value * conv_value, axis=(2, 3)).reshape(GROUPS, group_size, window).sum(1)
+    own_clip = lax.dynamic_slice_in_dim(frame_clip, window_start, window).astype(jnp.float32)
+    pieces = [sums_one.reshape(-1), sums_two.reshape(-1), own_clip, owner.reshape(-1).astype(jnp.float32)]
+    message = jnp.concatenate(pieces)
+    size = message.shape[0]
+    message = jnp.pad(message, (0, -size % 128)).reshape(1, -1, 128)
+    gathered = lax.all_to_all(
+        jnp.broadcast_to(message, (parts,) + message.shape[1:]),
+        ("tm", "space", "chan"),
+        split_axis=0,
+        concat_axis=0,
+        tiled=True,
+    ).reshape(parts, -1)
+    first = GROUPS * window
+    all_one = gathered[:, :first].reshape(parts, GROUPS, window)
+    all_two = gathered[:, first : 2 * first].reshape(parts, GROUPS, window)
+    all_clip = gathered[:, 2 * first : 2 * first + window]
+    all_owner = gathered[:, 2 * first + window : 2 * first + window + send_rows].astype(jnp.int32)
+    same = (all_clip[:, None, :] == own_clip[None, :, None]).astype(jnp.float32)
+    total_one = jnp.einsum("pgw,pvw->gv", all_one, same, precision=lax.Precision.HIGHEST)
+    total_two = jnp.einsum("pgw,pvw->gv", all_two, same, precision=lax.Precision.HIGHEST)
+    counts = jnp.sum(same, axis=(0, 2)) * (rows_here * columns * group_size)
+    mean = total_one / counts
+    rstd = lax.rsqrt(total_two / counts - mean * mean + 1e-06)
+    mean_frame = jnp.repeat(mean, group_size, axis=0)
+    rstd_frame = jnp.repeat(rstd, group_size, axis=0)
     scaled = (conv_value - mean_frame[:, :, None, None]) * rstd_frame[:, :, None, None]
     normed = jax.nn.silu(
-        scaled * gain_here[:, None, None, None] + bias_here[:, None, None, None]
+        scaled * norm_gain[:, None, None, None] + norm_bias[:, None, None, None]
     ).astype(jnp.bfloat16)
-    patches = normed.reshape(c_local, frames_here, rows_here // 2, 2, columns // 2, 2)
-    weight_here = lax.dynamic_slice(out_weight, (0, 0, chan_first, 0), (2, 2, c_local, MOMENTS))
-    latent = lax.psum_scatter(
-        jnp.einsum("cfrizj,ijco->ofrz", patches, weight_here, preferred_element_type=jnp.float32),
-        "chan",
-        scatter_dimension=0,
-        tiled=True,
+    patches = normed.reshape(CHANNELS, window, rows_here // 2, 2, columns // 2, 2)
+    latent = jnp.einsum(
+        "cfrizj,ijco->froz",
+        patches,
+        out_weight,
+        preferred_element_type=jnp.float32,
     ).astype(jnp.bfloat16)
-    moments_here = latent.shape[0]
-    send_rows = frames_here * (rows_here // 2)
-    row_block = latent.reshape(moments_here, send_rows, columns // 2)
-    tm_size = lax.axis_size("tm")
+    half = MOMENTS // chan_count
+    rows = latent.reshape(window * (rows_here // 2), chan_count, half, columns // 2)
+    outgoing = jnp.broadcast_to(
+        rows.transpose(1, 0, 2, 3)[None], (tm_size,) + (chan_count, rows.shape[0], half, columns // 2)
+    ).reshape((tm_size * chan_count,) + (rows.shape[0], half, columns // 2))
+    arrived = lax.all_to_all(outgoing, ("tm", "chan"), split_axis=0, concat_axis=0, tiled=True)
+    arrived = arrived.reshape(tm_size * send_rows, half * (columns // 2))
     capacity = max(2, 2 * send_rows // tm_size)
-    targets = owner[0, :, 0]
+    own_space = all_owner.reshape(tm_size, -1, chan_count, send_rows)
+    own_space = lax.dynamic_index_in_dim(own_space, lax.axis_index("space"), 1, keepdims=False)[:, 0]
     earlier = jnp.arange(send_rows)[None, :] < jnp.arange(send_rows)[:, None]
-    equal = targets[:, None] == targets[None, :]
-    order_rank = jnp.sum((equal & earlier).astype(jnp.int32), axis=1)
-    slot_of_row = targets * capacity + order_rank
-    selector = (
-        slot_of_row[None, :] == jnp.arange(tm_size * capacity, dtype=jnp.int32)[:, None]
-    ).astype(jnp.bfloat16)
-    outgoing = jnp.einsum(
-        "sr,crw->scw", selector, row_block, preferred_element_type=jnp.float32
-    ).astype(jnp.bfloat16)
-    arrived = lax.all_to_all(outgoing, "tm", split_axis=0, concat_axis=0, tiled=True)
-    return arrived[None]
+    equal = own_space[:, :, None] == own_space[:, None, :]
+    rank = jnp.sum((equal & earlier[None]).astype(jnp.int32), axis=2)
+    slot = jnp.arange(tm_size)[:, None] * capacity + rank
+    slot = jnp.where(own_space == lax.axis_index("tm"), slot, -1).reshape(-1)
+    selector = (slot[None, :] == jnp.arange(tm_size * capacity)[:, None]).astype(jnp.bfloat16)
+    owned = jnp.dot(selector, arrived, preferred_element_type=jnp.float32).astype(jnp.bfloat16)
+    return owned.reshape(1, tm_size * capacity, half, columns // 2)
 
 
 def solution(mesh):

time: 106 us -> 71.7 us (0.68)
  blocking collectives: 42 us -> 5.31 us
  between operations: 15.9 us -> 3.72 us
  starting transfers between devices: 14.3 us -> 24 us
  waiting for transfers between devices: 9.62 us -> 15.9 us
  matrix products: 6.8 us -> 5.13 us
    psum x1 -> x0, blocking collectives: 22.1 us -> none  [shards(): lax.psum((sums_one, sums_two, counts_here), ('tm', 'space'))]
    all_to_all x2 -> x0, blocking collectives: 14.5 us -> none  [the longest x1 10.4 us: shards(): lax.all_to_all(outgoing, 'tm', split_axis=0, concat_axis=0, tiled=True)]
    all_to_all x0 -> x2, waiting for transfers between devices: none -> 12.5 us  [the longest x1 6.31 us: shards(): lax.all_to_all(jnp.broadcast_to(message, (parts,) + message.shape[1:]), (...]
    all_to_all x0 -> x2, starting transfers between devices: none -> 9.7 us  [the longest x1 6.33 us: shards(): lax.all_to_all(jnp.broadcast_to(message, (parts,) + message.shape[1:]), (...]
    reduce_scatter x1 -> x0, waiting for transfers between devices: 4.74 us -> none  [shards(): lax.psum_scatter(jnp.einsum('cfrizj,ijco->ofrz', patches, weight_here, pr...]
    convert_element_type x6 -> x2, local copies, waits for them, and re-layouts: 2.23 us -> 0.11 us  [shards(): normed = jax.nn.silu(scaled * norm_gain[:, None, None, None] + norm_bias[...]
    dot_general x6 -> x4, matrix products: 2.38 us -> 0.72 us  [the longest x1 0.26 us: shards(): jnp.einsum('cfrizj,ijco->froz', patches, out_weight, preferred_element_ty...]
    broadcast_in_dim x2 -> x6, local copies, waits for them, and re-layouts: 0.14 us -> 1.66 us  [the longest x1 0.67 us: shards(): jnp.broadcast_to(rows.transpose(1, 0, 2, 3)[None], (tm_size,) + (chan_cou...]
  transfers between devices with their start and end apart: 5 -> 6, of which waited for: 2 -> 3; matrix products, arithmetic and copies ran while one was open for 5% -> 9% of each run, Pallas kernels for 0% -> 0%
where the time goes in v1:
time: 71.7 us; the launch traced here: 71.3 us
  starting transfers between devices  24 us (33%)
  waiting for transfers between devices  15.9 us (22%)
  local copies, waits for them, and re-layouts  12.3 us (17%)
  blocking collectives  5.31 us (7%)
  matrix products  5.13 us (7%)
  other arithmetic  4.96 us (7%)
  between operations  3.72 us (5%)
    ppermute x2, starting transfers between devices, shifted(): lax.ppermute(value, axis, [(source, source + steps) for source in range(l...  8.4 us
    all_to_all x1, starting transfers between devices, shards(): lax.all_to_all(jnp.broadcast_to(message, (parts,) + message.shape[1:]), (...  6.33 us
    all_to_all x1, waiting for transfers between devices, shards(): lax.all_to_all(jnp.broadcast_to(message, (parts,) + message.shape[1:]), (...  6.31 us
    all_to_all x1, waiting for transfers between devices, shards(): lax.all_to_all(outgoing, ('tm', 'chan'), split_axis=0, concat_axis=0, til...  6.18 us
    all_to_all x1, blocking collectives, shards(): lax.all_to_all(windows, 'chan', split_axis=1, concat_axis=0, tiled=True)  5.31 us
    unnamed x28, local copies, waits for them, and re-layouts  4.81 us
    ppermute x1, starting transfers between devices, with_halo(): lax.ppermute(lax.slice_in_dim(block, block.shape[dim] - width, None, axis...  4.56 us
    conv_general_dilated x3, matrix products, plane_conv(): lax.conv_general_dilated(frames, kernel, (1, 1), ((0, 0), (1, 1)), dimens...  4.41 us
  transfers between devices with their start and end apart: 6, of which 3 were waited for; matrix products, arithmetic and copies ran while one was open for 9% of the time, Pallas kernels for 0%

profile of v1, /device:TPU:0, one launch (start us, length us, event | category | flops | bytes accessed | tf_op | source)
XLA Modules:
  0.0 71.3 jit_solution(2218596778311375268)
XLA Ops:
  0.0 1.3 %copy.50 = bf16[64,2,8,256]{3,0,2,1:T(8,128)(2,1)S(1)} copy(bf16[64,2,8,256]{3,2,1,0:T(8,128)(2,1)} %param.9) | data formatting | bytes 1048576 | tf_op args[0]
  1.3 5.0 %collective-permute-start = (bf16[64,2,8,256]{3,0,2,1:T(8,128)(2,1)S(1)}, bf16[64,2,8,256]{3,0,2,1:T(8,128)(2,1)S(1)}, u32[]{:S(2)}, u32[]{:S(2)}) collective-permute-start(bf16[64,2,8,256]{3,0,2,1:T(8,128)(2,1)S(1)} %copy.50), channel_id=1, source_target_pairs={{0,4},{4,8},{8,12},{1,5},{5,9},{9,13},{2,6},{6,10},{10,14},{3,7},{... | collective-permute-start | bytes 1572872 | tf_op jit(solution)/shard_map/ppermute | solution.py:15
  6.2 0.7 add_convert_fusion.1
  6.9 3.4 %collective-permute-start.3 = (bf16[2]{0:T(256)(128)(2,1)S(1)}, bf16[2]{0:T(256)(128)(2,1)S(1)}, u32[]{:S(2)}, u32[]{:S(2)}) collective-permute-start(bf16[2]{0:T(256)(128)(2,1)S(1)} %get-tuple-element.31), channel_id=1, source_target_pairs={{0,4},{4,8},{8,12},{1,5},{5,9},{9,13},{2,6},{6,10},{10,14},{3,7},{... | collective-permute-start | bytes 20 | tf_op jit(solution)/shard_map/ppermute | solution.py:15
  10.4 1.3 %dynamic_slice.19 = s32[1]{0:T(128)} dynamic-slice(s32[2]{0:T(128)} %param.10, s32[]{:T(128)S(6)} %select_n.33), dynamic_slice_sizes={1} | dynamic-slice | bytes 12 | tf_op jit(solution)/shard_map/dynamic_slice | solution.py:81
  12.9 1.1 %convert_bitcast_fusion = f32[8]{0:T(128)} fusion(s32[1,8,1]{1,2,0:T(1,128)} %param.15), kind=kLoop, calls=%fused_computation.99 | loop fusion | flops 8 | bytes 64 | tf_op jit(solution)/shard_map/convert_element_type | solution.py:82
  14.0 3.4 %collective-permute-done.3 = bf16[2]{0:T(256)(128)(2,1)S(1)} collective-permute-done((bf16[2]{0:T(256)(128)(2,1)S(1)}, bf16[2]{0:T(256)(128)(2,1)S(1)}, u32[]{:S(2)}, u32[]{:S(2)}) %collective-permute-start.3) | collective-permute-done | bytes 36 | tf_op jit(solution)/shard_map/ppermute | solution.py:15
  17.8 1.3 %collective-permute-start.2 = (bf16[64,4,1,256]{3,0,2,1:T(8,128)(2,1)S(1)}, bf16[64,4,1,256]{3,0,2,1:T(8,128)(2,1)S(1)}, u32[]{:S(2)}, u32[]{:S(2)}) collective-permute-start(bf16[64,4,1,256]{3,0,2,1:T(8,128)(2,1)S(1)} %get-tuple-element.27), channel_id=1, source_target_pairs={{2,0},{3,1},{6,4},{7,5},{10,8},{11,9},{14,12},{15,13},{18,16},{19,... | collective-permute-start | bytes 393224 | tf_op jit(solution)/shard_map/ppermute | solution.py:26
  19.1 4.6 %collective-permute-start.1 = (bf16[64,4,1,256]{3,0,2,1:T(8,128)(2,1)S(1)}, bf16[64,4,1,256]{3,0,2,1:T(8,128)(2,1)S(1)}, u32[]{:S(2)}, u32[]{:S(2)}) collective-permute-start(bf16[64,4,1,256]{3,0,2,1:T(8,128)(2,1)S(1)} %get-tuple-element.26), channel_id=1, source_target_pairs={{0,2},{1,3},{4,6},{5,7},{8,10},{9,11},{12,14},{13,15},{16,18},{17,... | collective-permute-start | bytes 393224 | tf_op jit(solution)/shard_map/ppermute | solution.py:23
  23.7 0.6 dynamic_slice.18
  25.0 0.7 dynamic_slice.17
  28.2 5.3 %all_to_all.25 = bf16[64,2,3,10,256]{4,0,3,2,1:T(8,128)(2,1)S(1)} all-to-all(bf16[64,2,3,10,256]{4,0,3,2,1:T(8,128)(2,1)S(1)} %pad_maximum_fusion), channel_id=1, replica_groups=mesh['groups'=2,'tm'=4,'space'=2,'chan'=2] {'chan'}, dimensions={1} | all-to-all | bytes 3932160 | tf_op jit(solution)/shard_map/all_to_all | solution.py:67
  35.6 0.8 %copy-done.2 = bf16[128,10,1,8,33]{0,3,4,1,2:T(8,128)(2,1)} copy-done((bf16[128,10,1,8,33]{0,3,4,1,2:T(8,128)(2,1)}, bf16[128,10,1,8,33]{0,3,4,1,2:T(8,128)(2,1)S(1)}, u32[]{:S(2)}) %copy-start.2) | copy-done | bytes 675864
  37.3 1.0 %copy-done.9 = bf16[3,3,3,128,128]{4,3,2,1,0:T(8,128)(2,1)S(1)} copy-done((bf16[3,3,3,128,128]{4,3,2,1,0:T(8,128)(2,1)S(1)}, bf16[3,3,3,128,128]{4,3,2,1,0:T(8,128)(2,1)}, u32[]{:S(2)}) %copy-start.9) | copy-done | bytes 884760
  38.4 1.4 %convolution_select_fusion.1 = f32[8,8,33,128]{3,1,2,0:T(8,128)S(1)} fusion(bf16[128,10,1,7,2]{0,3,4,1,2:T(8,128)(2,1)S(1)} %slice.72, bf16[128,10,1,8,33]{0,3,4,1,2:T(8,128)(2,1)S(1)} %copy.58, pred[8,33]{0,1:T(8,128)(4,1)S(1)} %copy-done.10, bf16[3,3,3,128,128]{4,3,2,1,0:T(8,128)(2,1)S(1)} %copy-done.9), kind=kOutput, calls=%fused_computation.10 | convolution fusion | flops 625274880 | bytes 2098176 | tf_op jit(solution)/shard_map/conv_general_dilated | solution.py:32
  39.8 1.4 %fusion.3 = f32[8,8,33,128]{3,1,2,0:T(8,128)S(1)} fusion(f32[8,8,33,128]{3,1,2,0:T(8,128)S(1)} %convolution_select_fusion.1, bf16[128,10,1,7,2]{0,3,4,1,2:T(8,128)(2,1)S(1)} %slice.71, bf16[128,10,1,8,33]{0,3,4,1,2:T(8,128)(2,1)S(1)} %copy-done.3, pred[8,33]{0,1:T(8,128)(4,1)S(1)} %copy-done.10, bf16[3,3,3,128,128]{4,3,2,1,0:T(8,128)(2,1)S(1)} %copy-done.9), kind=kOutput, calls=%fused_computation.12 | convolution fusion | flops 625545216 | bytes 3179520 | tf_op jit(solution)/shard_map/conv_general_dilated | solution.py:32
  41.3 1.5 %fusion.13 = (f32[128]{0:T(128)S(1)}, f32[128]{0:T(128)S(1)}, bf16[8,8,33,128]{3,1,2,0:T(8,128)(2,1)S(1)}) fusion(pred[8,33]{0,1:T(8,128)(4,1)S(1)} %copy-done.10, f32[8,8,33,128]{3,1,2,0:T(8,128)S(1)} %fusion.3, bf16[3,3,3,128,128]{4,3,2,1,0:T(8,128)(2,1)S(1)} %copy-done.9, bf16[128,10,1,7,2]{0,3,4,1,2:T(8,128)(2,1)S(1)} %slice.73, ...), kind=kOutput, calls=%fused_computation.26 | convolution fusion | flops 627437312 | bytes 2639872 | tf_op jit(solution)/shard_map/conv_general_dilated | solution.py:32
  44.0 6.3 %all-to-all-start.1 = ((f32[16,1,128]{2,1,0:T(1,128)}), f32[16,1,128]{2,1,0:T(1,128)S(1)}, u32[]{:S(2)}, u32[]{:S(2)}) async-start(f32[16,1,128]{2,1,0:T(1,128)} %broadcast_in_dim.24), calls=%async_computation.1 | async-start | bytes 16384 | tf_op jit(solution)/shard_map/all_to_all | solution.py:86
  50.3 6.3 %all-to-all-done.1 = f32[16,1,128]{2,1,0:T(1,128)S(1)} async-done(((f32[16,1,128]{2,1,0:T(1,128)}), f32[16,1,128]{2,1,0:T(1,128)S(1)}, u32[]{:S(2)}, u32[]{:S(2)}) %all-to-all-start.1) | async-done | bytes 8224 | tf_op jit(solution)/shard_map/all_to_all | solution.py:86
  56.7 0.7 convert_reduce_fusion.1
  59.7 0.7 broadcast_in_dim.51
  60.4 3.4 %all-to-all-start.2 = ((bf16[8,4,16,128]{3,2,1,0:T(8,128)(2,1)}), bf16[8,4,16,128]{3,2,1,0:T(8,128)(2,1)S(1)}, u32[]{:S(2)}, u32[]{:S(2)}) async-start(bf16[8,4,16,128]{3,2,1,0:T(8,128)(2,1)} %bitcast.42), calls=%async_computation.2 | async-start | bytes 262144 | tf_op jit(solution)/shard_map/all_to_all | solution.py:122
  64.3 6.2 %all-to-all-done.2 = bf16[8,4,16,128]{3,2,1,0:T(8,128)(2,1)S(1)} async-done(((bf16[8,4,16,128]{3,2,1,0:T(8,128)(2,1)}), bf16[8,4,16,128]{3,2,1,0:T(8,128)(2,1)S(1)}, u32[]{:S(2)}, u32[]{:S(2)}) %all-to-all-start.2) | async-done | bytes 131104 | tf_op jit(solution)/shard_map/all_to_all | solution.py:122
  70.6 0.6 copy.73
  (80 shorter events, 8.5 us)
Async XLA Ops:
  0.0 59.4 %copy-start = (bf16[2,2,128,32]{2,3,1,0:T(8,128)(2,1)S(1)}, bf16[2,2,128,32]{2,3,1,0:T(8,128)(2,1)}, u32[]{:S(2)}) copy-start(bf16[2,2,128,32]{2,3,1,0:T(8,128)(2,1)} %param.14) | copy-start | bytes 98308
  0.0 17.6 %copy-start.1 = (bf16[64,2,8,256]{3,2,1,0:T(8,128)(2,1)S(1)}, bf16[64,2,8,256]{3,2,1,0:T(8,128)(2,1)}, u32[]{:S(2)}) copy-start(bf16[64,2,8,256]{3,2,1,0:T(8,128)(2,1)} %param.9) | copy-start | bytes 1572868
  1.3 16.2 %collective-permute-start = (bf16[64,2,8,256]{3,0,2,1:T(8,128)(2,1)S(1)}, bf16[64,2,8,256]{3,0,2,1:T(8,128)(2,1)S(1)}, u32[]{:S(2)}, u32[]{:S(2)}) collective-permute-start(bf16[64,2,8,256]{3,0,2,1:T(8,128)(2,1)S(1)} %copy.50), channel_id=1, source_target_pairs={{0,4},{4,8},{8,12},{1,5},{5,9},{9,13},{2,6},{6,10},{10,14},{3,7},{... | collective-permute-start | bytes 1572872 | tf_op jit(solution)/shard_map/ppermute | solution.py:15
  6.9 10.5 %collective-permute-start.3 = (bf16[2]{0:T(256)(128)(2,1)S(1)}, bf16[2]{0:T(256)(128)(2,1)S(1)}, u32[]{:S(2)}, u32[]{:S(2)}) collective-permute-start(bf16[2]{0:T(256)(128)(2,1)S(1)} %get-tuple-element.31), channel_id=1, source_target_pairs={{0,4},{4,8},{8,12},{1,5},{5,9},{9,13},{2,6},{6,10},{10,14},{3,7},{... | collective-permute-start | bytes 20 | tf_op jit(solution)/shard_map/ppermute | solution.py:15
  17.5 6.1 %copy-start.8 = (s32[2]{0:T(128)S(1)}, s32[2]{0:T(128)}, u32[]{:S(2)}) copy-start(s32[2]{0:T(128)} %param.10) | copy-start | bytes 28
  17.8 9.8 %collective-permute-start.2 = (bf16[64,4,1,256]{3,0,2,1:T(8,128)(2,1)S(1)}, bf16[64,4,1,256]{3,0,2,1:T(8,128)(2,1)S(1)}, u32[]{:S(2)}, u32[]{:S(2)}) collective-permute-start(bf16[64,4,1,256]{3,0,2,1:T(8,128)(2,1)S(1)} %get-tuple-element.27), channel_id=1, source_target_pairs={{2,0},{3,1},{6,4},{7,5},{10,8},{11,9},{14,12},{15,13},{18,16},{19,... | collective-permute-start | bytes 393224 | tf_op jit(solution)/shard_map/ppermute | solution.py:26
  19.1 8.5 %collective-permute-start.1 = (bf16[64,4,1,256]{3,0,2,1:T(8,128)(2,1)S(1)}, bf16[64,4,1,256]{3,0,2,1:T(8,128)(2,1)S(1)}, u32[]{:S(2)}, u32[]{:S(2)}) collective-permute-start(bf16[64,4,1,256]{3,0,2,1:T(8,128)(2,1)S(1)} %get-tuple-element.26), channel_id=1, source_target_pairs={{0,2},{1,3},{4,6},{5,7},{8,10},{9,11},{12,14},{13,15},{16,18},{17,... | collective-permute-start | bytes 393224 | tf_op jit(solution)/shard_map/ppermute | solution.py:23
  35.6 0.8 %copy-start.2 = (bf16[128,10,1,8,33]{0,3,4,1,2:T(8,128)(2,1)}, bf16[128,10,1,8,33]{0,3,4,1,2:T(8,128)(2,1)S(1)}, u32[]{:S(2)}) copy-start(bf16[128,10,1,8,33]{0,3,4,1,2:T(8,128)(2,1)S(1)} %copy.55) | copy-start | bytes 2027524
  37.2 1.2 %copy-start.9 = (bf16[3,3,3,128,128]{4,3,2,1,0:T(8,128)(2,1)S(1)}, bf16[3,3,3,128,128]{4,3,2,1,0:T(8,128)(2,1)}, u32[]{:S(2)}) copy-start(bf16[3,3,3,128,128]{4,3,2,1,0:T(8,128)(2,1)} %param.11) | copy-start | bytes 2654212
  37.2 1.2 %copy-start.10 = (pred[8,33]{0,1:T(8,128)(4,1)S(1)}, pred[8,33]{0,1:T(8,128)(4,1)}, u32[]{:S(2)}) copy-start(pred[8,33]{0,1:T(8,128)(4,1)} %constant.89) | copy-start | bytes 796
  38.4 1.4 %copy-start.3 = (bf16[128,10,1,8,33]{0,3,4,1,2:T(8,128)(2,1)S(1)}, bf16[128,10,1,8,33]{0,3,4,1,2:T(8,128)(2,1)}, u32[]{:S(2)}) copy-start(bf16[128,10,1,8,33]{0,3,4,1,2:T(8,128)(2,1)} %copy-done.2) | copy-start | bytes 2027524
  41.2 2.0 %copy-start.7 = (f32[8]{0:T(128)S(1)}, f32[8]{0:T(128)}, u32[]{:S(2)}) copy-start(f32[8]{0:T(128)} %convert_bitcast_fusion) | copy-start | bytes 100
  41.3 17.6 %copy-start.5 = (f32[128]{0:T(128)S(1)}, f32[128]{0:T(128)}, u32[]{:S(2)}) copy-start(f32[128]{0:T(128)} %param.13) | copy-start | bytes 1540
  41.3 17.6 %copy-start.6 = (f32[128]{0:T(128)S(1)}, f32[128]{0:T(128)}, u32[]{:S(2)}) copy-start(f32[128]{0:T(128)} %param.12) | copy-start | bytes 1540
  44.0 12.7 %all-to-all-start.1 = ((f32[16,1,128]{2,1,0:T(1,128)}), f32[16,1,128]{2,1,0:T(1,128)S(1)}, u32[]{:S(2)}, u32[]{:S(2)}) async-start(f32[16,1,128]{2,1,0:T(1,128)} %broadcast_in_dim.24), calls=%async_computation.1 | async-start | bytes 16384 | tf_op jit(solution)/shard_map/all_to_all | solution.py:86
  59.4 4.4 %copy-start.4 = (pred[8,8]{1,0:T(8,128)(4,1)S(1)}, pred[8,8]{1,0:T(8,128)(4,1)}, u32[]{:S(2)}) copy-start(pred[8,8]{1,0:T(8,128)(4,1)} %iota_compare_fusion.3) | copy-start | bytes 196
  60.4 10.1 %all-to-all-start.2 = ((bf16[8,4,16,128]{3,2,1,0:T(8,128)(2,1)}), bf16[8,4,16,128]{3,2,1,0:T(8,128)(2,1)S(1)}, u32[]{:S(2)}, u32[]{:S(2)}) async-start(bf16[8,4,16,128]{3,2,1,0:T(8,128)(2,1)} %bitcast.42), calls=%async_computation.2 | async-start | bytes 262144 | tf_op jit(solution)/shard_map/all_to_all | solution.py:122

commit v2 on v0

v2 whole, which is shorter than its diff:
```python
import jax
import jax.numpy as jnp
import numpy as np
from jax import lax
from jax.experimental import pallas as pl
from jax.experimental.pallas import tpu as pltpu
from jax.sharding import PartitionSpec as P

CHANNELS = 128
GROUPS = 32
MOMENTS = 32
ID_ROWS = 16
BF16 = jnp.bfloat16
F32 = jnp.float32
VMEM = pl.BlockSpec(memory_space=pltpu.VMEM)
SMEM = pl.BlockSpec(memory_space=pltpu.SMEM)
PARAMS = pltpu.CompilerParams(vmem_limit_bytes=40 * 1024 * 1024)
PART = ("tm", "space", "chan")


def flat_pairs(sizes, pairs):
    _, spaces, chans = sizes
    return [
        ((a[0] * spaces + a[1]) * chans + a[2], (b[0] * spaces + b[1]) * chans + b[2])
        for a, b in pairs
    ]


def space_swap(value, sizes, odd):
    slabs, spaces, chans = sizes
    pairs = []
    for low in range(odd, spaces - 1, 2):
        for t in range(slabs):
            for c in range(chans):
                pairs += [((t, low, c), (t, low + 1, c)), ((t, low + 1, c), (t, low, c))]
    return lax.ppermute(value, PART, flat_pairs(sizes, pairs))


def slab_swap(value, sizes, cross):
    slabs, spaces, _ = sizes
    pairs = []
    for t in range(slabs - 1):
        for s in range(spaces):
            if cross:
                pairs += [((t, s, 0), (t + 1, s, 1)), ((t + 1, s, 1), (t, s, 0))]
            else:
                pairs += [((t, s, 1), (t + 1, s, 1)), ((t + 1, s, 0), (t, s, 0))]
    return lax.ppermute(value, PART, flat_pairs(sizes, pairs))


def whole_call(kernel, out_shape, specs, args):
    return pl.pallas_call(
        kernel,
        out_shape=out_shape,
        in_specs=specs,
        out_specs=jax.tree.map(lambda _: VMEM, out_shape),
        compiler_params=PARAMS,
    )(*args)


def pack_kernel(halos, where_ref, ids_ref, frames_ref, *refs):
    halo_refs, (cross_ref, same_ref) = refs[:halos], refs[halos:]
    chan = where_ref[2]
    _, rows, half, columns = frames_ref.shape
    source = lax.broadcasted_iota(jnp.int32, (columns, columns), 0)
    target = lax.broadcasted_iota(jnp.int32, (columns, columns), 1)
    wanted = jnp.where(target < columns // 2, 2 * target, 2 * target - columns + 1)
    split = jnp.where(source == wanted, 1.0, 0.0).astype(BF16)

    def parted(value):
        return jnp.dot(value, split, preferred_element_type=F32).astype(BF16)

    for out_ref, frame in ((cross_ref, 1 - chan), (same_ref, chan)):
        for r in range(rows):
            out_ref[r * half : (r + 1) * half, :] = parted(frames_ref[frame, r])
        for h in range(halos):
            first = (rows + h) * half
            out_ref[first : first + half, :] = parted(halo_refs[h][frame])
        number = (ids_ref[frame] + 1).astype(F32)
        out_ref[(rows + halos) * half :, :] = jnp.full((ID_ROWS, columns), number, F32).astype(BF16)


def weights_kernel(where_ref, ids_ref, weight_ref, local_ref, late_ref, sum_ref):
    chan = where_ref[2]
    half = CHANNELS // 2
    zero = jnp.float32(0.0)
    one = jnp.float32(1.0)
    first = chan == 0
    joined = ids_ref[0] == ids_ref[1]
    flag = jnp.where(joined, one, zero)
    on_first = jnp.where(first, one, zero)
    on_second = one - on_first
    near = (
        on_first * (one - flag),
        on_first + on_second * flag,
        zero,
    )
    far = (
        on_first * flag + on_second * (one - flag),
        on_second * (one - flag),
        on_second,
    )
    late_same = (on_second * flag, zero, on_first)
    late_apart = (on_first + on_second * flag, on_first, on_first)
    own = pl.multiple_of(chan * half, half)
    other = pl.multiple_of((1 - chan) * half, half)
    for j in range(3):
        for i in range(3):
            taps = []
            for k in range(3):
                block = jnp.concatenate(
                    [weight_ref[k, i, j, pl.ds(own, half), :], weight_ref[k, i, j, pl.ds(other, half), :]],
                    axis=0,
                )
                taps.append(block.astype(F32).T)

            def mixed(scale):
                return (taps[0] * scale[0] + taps[1] * scale[1] + taps[2] * scale[2]).astype(BF16)

            rows = slice(j * CHANNELS, (j + 1) * CHANNELS)
            columns = slice(i * CHANNELS, (i + 1) * CHANNELS)
            shifted = slice((3 + i) * CHANNELS, (4 + i) * CHANNELS)
            local_ref[rows, columns] = mixed(near)
            local_ref[rows, shifted] = mixed(far)
            late_ref[0, rows, columns] = mixed(late_same)
            late_ref[1, rows, columns] = mixed(late_apart)
            sum_ref[rows, columns] = mixed((one, one, one))


def image_row(own_ref, other_ref, rows, halos, odd, r):
    half = CHANNELS // 2

    def slab(ref, n):
        return ref[n * half : (n + 1) * half, :]

    pieces = []
    for ref in (own_ref, other_ref):
        if 0 <= r < rows:
            pieces.append(slab(ref, r))
            continue
        first = slab(ref, rows)
        second = slab(ref, rows + 1) if halos > 1 else jnp.zeros_like(first)
        on_first = odd if r < 0 else jnp.logical_not(odd)
        pieces.append(jnp.where(on_first, first, second))
    return jnp.concatenate(pieces, axis=0)


def joined_columns(product):
    half = product.shape[1] // 2
    left = product[:CHANNELS, :]
    middle = product[CHANNELS : 2 * CHANNELS, :]
    right = product[2 * CHANNELS :, :]
    lane = lax.broadcasted_iota(jnp.int32, (CHANNELS, half), 1)
    from_left = jnp.where(lane == 0, 0.0, pltpu.roll(left[:, half:], 1, 1))
    from_right = jnp.where(lane == half - 1, 0.0, pltpu.roll(right[:, :half], half - 1, 1))
    even = from_left + middle[:, :half] + right[:, half:]
    odd = left[:, :half] + middle[:, half:] + from_right
    return even, odd


def lane_totals(first, second):
    rows = [jnp.sum(value.T, axis=0, keepdims=True) for value in (first, second)]
    return rows


def local_kernel(
    rows, halos, where_ref, weight_ref, sum_ref, cross_ref, same_ref, cross_other_ref, same_other_ref,
    conv_ref, extra_ref, sums_ref,
):
    odd = lax.rem(where_ref[1], 2) == 1
    chan = where_ref[2]
    near = [image_row(cross_ref, same_other_ref, rows, halos, odd, r) for r in range(-1, rows + 1)]
    far = [image_row(same_ref, cross_other_ref, rows, halos, odd, r) for r in range(-1, rows + 1)]
    half = near[0].shape[1] // 2
    for r in range(rows):
        image = jnp.concatenate(near[r : r + 3] + far[r : r + 3], axis=0)
        product = jnp.dot(weight_ref[...], image, preferred_element_type=F32)
        even, late = joined_columns(product)
        conv_ref[r, :, :half] = even
        conv_ref[r, :, half:] = late
    sums_ref[...] = jnp.zeros_like(sums_ref)

    @pl.when(where_ref[0] > 0)
    def _():
        extra_ref[...] = jnp.zeros_like(extra_ref)

    for c in range(2):

        @pl.when((where_ref[0] == 0) & (chan == c))
        def _():
            totals = [jnp.zeros((CHANNELS, half), F32)] * 2
            start = c * (rows // 2)
            for r in range(rows // 2):
                images = far if c == 0 else near
                image = jnp.concatenate(images[start + r : start + r + 3], axis=0)
                product = jnp.dot(sum_ref[...], image, preferred_element_type=F32)
                for side, value in enumerate(joined_columns(product)):
                    value = value.astype(BF16)
                    extra_ref[r, :, side * half : (side + 1) * half] = value
                    value = value.astype(F32)
                    totals = [totals[0] + value, totals[1] + value * value]
            one, two = lane_totals(*totals)
            sums_ref[0:1, :] = one
            sums_ref[1:2, :] = two


def late_kernel(
    rows, halos, slabs, where_ref, ids_ref, owner_ref, weight_ref, part_ref, cross_ref, same_other_ref,
    late_own_ref, late_other_ref, sums_ref, conv_ref, message_ref,
):
    odd = lax.rem(where_ref[1], 2) == 1
    slab = where_ref[0]
    chan = where_ref[2]
    half = part_ref.shape[2] // 2
    tail = (rows + halos) * (CHANNELS // 2)
    number = jnp.max(late_own_ref[tail:, :].astype(F32)).astype(jnp.int32) - 1
    first = chan == 0
    same = jnp.where(first, number == ids_ref[1], number == ids_ref[0])
    keep = jnp.where(jnp.logical_or(same, jnp.logical_not(first)), 1.0, 0.0)
    use_late = jnp.logical_or(same, first)
    choice = jnp.where(same, 0, 1)
    weight = weight_ref[choice]
    images = []
    for r in range(-1, rows + 1):
        late = image_row(late_own_ref, late_other_ref, rows, halos, odd, r)
        here = image_row(cross_ref, same_other_ref, rows, halos, odd, r)
        images.append(jnp.where(use_late, late, here))
    totals = [jnp.zeros((CHANNELS, half), F32)] * 2
    for r in range(rows):
        image = jnp.concatenate(images[r : r + 3], axis=0)
        product = jnp.dot(weight, image, preferred_element_type=F32)
        for side, value in enumerate(joined_columns(product)):
            lanes = slice(side * half, (side + 1) * half)
            value = (value + keep * part_ref[r, :, lanes]).astype(BF16)
            conv_ref[r, :, lanes] = value
            value = value.astype(F32)
            totals = [totals[0] + value, totals[1] + value * value]
    one, two = lane_totals(*totals)
    absent = jnp.logical_and(first, slab == slabs - 1)
    main_id = jnp.where(first, jnp.where(absent, -1, number), ids_ref[1]).astype(F32)
    extra_id = jnp.where(slab == 0, ids_ref[0], -1).astype(F32)
    line = lax.broadcasted_iota(jnp.int32, (8, CHANNELS), 0)
    message = jnp.where(line == 0, one, 0.0)
    message = jnp.where(line == 1, two, message)
    message = jnp.where(line == 2, sums_ref[0:1, :], message)
    message = jnp.where(line == 3, sums_ref[1:2, :], message)
    message = jnp.where(line == 4, main_id, message)
    message = jnp.where(line == 5, extra_id, message)
    message = jnp.where(line == 6, owner_ref[0:1, :], message)
    for p in range(message_ref.shape[0]):
        message_ref[p] = message


def norm_kernel(
    count, where_ref, message_ref, gathered_ref, affine_ref, out_weight_ref, conv_ref, extra_ref, latent_ref
):
    rows, _, columns = conv_ref.shape
    half = columns // 2
    main = gathered_ref[:, 4, :]
    extra = gathered_ref[:, 5, :]
    lines = []
    for number in (message_ref[0, 4:5, :], message_ref[0, 5:6, :]):
        on_main = main == number
        on_extra = extra == number
        for n in range(2):
            picked = jnp.where(on_main, gathered_ref[:, n, :], 0.0) + jnp.where(
                on_extra, gathered_ref[:, 2 + n, :], 0.0
            )
            lines.append(jnp.sum(picked, axis=0, keepdims=True))
        held = jnp.where(on_main, float(count), 0.0) + jnp.where(on_extra, float(count // 2), 0.0)
        lines.append(jnp.sum(held, axis=0, keepdims=True))
    lines += [jnp.zeros((1, CHANNELS), F32)] * 2
    size = CHANNELS // GROUPS
    group_row = lax.broadcasted_iota(jnp.int32, (CHANNELS, CHANNELS), 0) // size
    group_column = lax.broadcasted_iota(jnp.int32, (CHANNELS, CHANNELS), 1) // size
    member = jnp.where(group_row == group_column, 1.0, 0.0)
    totals = jnp.dot(
        jnp.concatenate(lines, axis=0), member, preferred_element_type=F32, precision=lax.Precision.HIGHEST
    )

    def factors(first):
        counts = totals[first + 2 : first + 3, :]
        mean = totals[first : first + 1, :] / counts
        var = totals[first + 1 : first + 2, :] / counts - mean * mean
        scale = lax.rsqrt(var + 1e-06) * affine_ref[0:1, :]
        offset = affine_ref[1:2, :] - mean * scale
        return [jnp.broadcast_to(value, (CHANNELS, CHANNELS)).T for value in (scale, offset)]

    def project(source_ref, scale, offset):
        images = []
        for r in range(source_ref.shape[0] // 2):
            pieces = []
            for i in range(2):
                for j in range(2):
                    value = source_ref[2 * r + i, :, j * half : (j + 1) * half].astype(F32)
                    value = value * scale + offset
                    pieces.append((value / (1.0 + jnp.exp(-value))).astype(BF16))
            images.append(jnp.concatenate(pieces, axis=0))
        image = jnp.concatenate(images, axis=1)
        return jnp.dot(out_weight_ref[...], image, preferred_element_type=F32).astype(BF16)

    places, chans = latent_ref.shape[0] // 2, 2
    part = MOMENTS // chans

    def store(latent, first):
        for r in range(latent.shape[1] // half):
            for c in range(chans):
                block = latent[c * part : (c + 1) * part, r * half : (r + 1) * half]
                for t in range(places):
                    latent_ref[t * chans + c, first + r] = block

    store(project(conv_ref, *factors(0)), 0)

    @pl.when(where_ref[0] == 0)
    def _():
        store(project(extra_ref, *factors(3)), rows // 2)

    @pl.when(where_ref[0] > 0)
    def _():
        for r in range(rows // 4):
            for p in range(latent_ref.shape[0]):
                latent_ref[p, rows // 2 + r] = jnp.zeros((part, half), BF16)


def shards(activations, frame_clip, conv_weight, norm_gain, norm_bias, out_weight, owner):
    half, frames, rows, columns = activations.shape
    sizes = tuple(lax.axis_size(name) for name in PART)
    slabs, spaces, chans = sizes
    assert (frames, chans, half * chans) == (2, 2, CHANNELS)
    parts = slabs * spaces * chans
    halos = 1 if spaces <= 2 else 2
    space = lax.axis_index("space")
    where = jnp.stack([lax.axis_index(name) for name in PART]).astype(jnp.int32)
    edge_low = activations[:, :, 0, :].transpose(1, 0, 2)
    edge_high = activations[:, :, rows - 1, :].transpose(1, 0, 2)
    odd = space % 2 == 1
    swapped = [space_swap(jnp.where(odd, edge_low, edge_high), sizes, 0)]
    if halos > 1:
        swapped.append(space_swap(jnp.where(odd, edge_high, edge_low), sizes, 1))
    planes = activations.transpose(1, 2, 0, 3)
    depth = (rows + halos) * half + ID_ROWS
    payload = jax.ShapeDtypeStruct((depth, columns), BF16)
    cross, same = whole_call(
        lambda *refs: pack_kernel(halos, *refs),
        (payload, payload),
        [SMEM, SMEM] + [VMEM] * (1 + halos),
        (where, frame_clip, planes, *swapped),
    )
    late_other = slab_swap(cross, sizes, True)
    late_own = slab_swap(same, sizes, False)
    turn = [(0, 1), (1, 0)]
    cross_other = lax.ppermute(cross, "chan", turn)
    same_other = lax.ppermute(same, "chan", turn)
    local_weight, late_weight, sum_weight = whole_call(
        weights_kernel,
        (
            jax.ShapeDtypeStruct((3 * CHANNELS, 6 * CHANNELS), BF16),
            jax.ShapeDtypeStruct((2, 3 * CHANNELS, 3 * CHANNELS), BF16),
            jax.ShapeDtypeStruct((3 * CHANNELS, 3 * CHANNELS), BF16),
        ),
        [SMEM, SMEM, VMEM],
        (where, frame_clip, conv_weight),
    )
    part, extra, extra_sums = whole_call(
        lambda *refs: local_kernel(rows, halos, *refs),
        (
            jax.ShapeDtypeStruct((rows, CHANNELS, columns), F32),
            jax.ShapeDtypeStruct((rows // 2, CHANNELS, columns), BF16),
            jax.ShapeDtypeStruct((8, CHANNELS), F32),
        ),
        [SMEM] + [VMEM] * 6,
        (where, local_weight, sum_weight, cross, same, cross_other, same_other),
    )
    send_rows = frames * (rows // 2)
    owner_line = jnp.pad(owner.reshape(1, send_rows).astype(F32), ((0, 0), (0, CHANNELS - send_rows)))
    conv, message = whole_call(
        lambda *refs: late_kernel(rows, halos, slabs, *refs),
        (
            jax.ShapeDtypeStruct((rows, CHANNELS, columns), BF16),
            jax.ShapeDtypeStruct((parts, 8, CHANNELS), F32),
        ),
        [SMEM, SMEM] + [VMEM] * 8,
        (where, frame_clip, owner_line, late_weight, part, cross, same_other, late_own, late_other, extra_sums),
    )
    gathered = lax.all_to_all(message, PART, split_axis=0, concat_axis=0, tiled=True)
    affine = jnp.stack([norm_gain, norm_bias])
    out_matrix = out_weight.reshape(4 * CHANNELS, MOMENTS).T
    kept = rows // 2 + rows // 4
    latent = whole_call(
        lambda *refs: norm_kernel(rows * columns, *refs),
        jax.ShapeDtypeStruct((slabs * chans, kept, MOMENTS // chans, columns // 2), BF16),
        [SMEM] + [VMEM] * 6,
        (where, message, gathered, affine, out_matrix, conv, extra),
    )
    arrived = lax.all_to_all(latent, ("tm", "chan"), split_axis=0, concat_axis=0, tiled=True)
    owners = gathered.reshape(slabs, spaces, chans, 8, CHANNELS)[:, :, 0, 6, :send_rows]
    owners = lax.dynamic_index_in_dim(owners, space, 1, keepdims=False).astype(jnp.int32)
    capacity = max(2, 2 * send_rows // slabs)
    earlier = jnp.arange(send_rows)[None, :] < jnp.arange(send_rows)[:, None]
    equal = owners[:, :, None] == owners[:, None, :]
    rank = jnp.sum((equal & earlier[None]).astype(jnp.int32), axis=2)
    slot = jnp.arange(slabs)[:, None] * capacity + rank
    slot = jnp.where(owners == lax.axis_index("tm"), slot, -1)
    by_frame = slot.reshape(slabs * frames, rows // 2)
    none = jnp.full((1, rows // 2), -1, jnp.int32)
    main_slot = jnp.stack([jnp.concatenate([by_frame[2::2], none]), by_frame[1::2]], axis=1)
    extra_slot = jnp.concatenate(
        [by_frame[0].reshape(1, chans, rows // 4), jnp.full((slabs - 1, chans, rows // 4), -1, jnp.int32)]
    )
    slots = jnp.concatenate([main_slot, extra_slot], axis=2).reshape(-1)
    selector = (slots[None, :] == jnp.arange(slabs * capacity)[:, None]).astype(BF16)
    block = arrived.reshape(slots.shape[0], -1)
    owned = jnp.dot(selector, block, preferred_element_type=F32).astype(BF16)
    return owned.reshape(1, slabs * capacity, MOMENTS // chans, columns // 2)


def solution(mesh):
    placed = (
        P(("groups", "chan"), "tm", "space", None),
        P(("groups", "tm")),
        P(),
        P(),
        P(),
        P(),
        P(("groups", "space"), "tm", None),
    )
    return jax.shard_map(
        shards,
        mesh=mesh,
        in_specs=placed,
        out_specs=P(("groups", "space"), "tm", "chan", None),
        check_vma=False,
    )
```

time: 106 us -> 50.9 us (0.48)
  blocking collectives: 42 us -> 0 us
  between operations: 15.9 us -> 0.21 us
  Pallas kernels: 0 us -> 10.3 us
  local copies, waits for them, and re-layouts: 13.1 us -> 4.19 us
  matrix products: 6.8 us -> 0.15 us
  waiting for transfers between devices: 9.62 us -> 16.2 us
  starting transfers between devices: 14.3 us -> 18.9 us
  other arithmetic: 3.95 us -> 0.5 us
    psum x1 -> x0, blocking collectives: 22.1 us -> none  [shards(): lax.psum((sums_one, sums_two, counts_here), ('tm', 'space'))]
    all_to_all x3 -> x0, blocking collectives: 19.8 us -> none  [the longest x1 10.4 us: shards(): lax.all_to_all(outgoing, 'tm', split_axis=0, concat_axis=0, tiled=True)]
    all_to_all x0 -> x2, waiting for transfers between devices: none -> 13.8 us  [the longest x1 7.86 us: shards(): lax.all_to_all(latent, ('tm', 'chan'), split_axis=0, concat_axis=0, tiled...]
    pallas_call x0 -> x5, Pallas kernels: none -> 10.3 us  [whole_call(): pl.pallas_call(kernel, out_shape=out_shape, in_specs=specs, out_specs=jax...]
    all_to_all x0 -> x2, starting transfers between devices: none -> 8.48 us  [the longest x1 5.09 us: shards(): lax.all_to_all(message, PART, split_axis=0, concat_axis=0, tiled=True)]
    reduce_scatter x1 -> x0, waiting for transfers between devices: 4.74 us -> none  [shards(): lax.psum_scatter(jnp.einsum('cfrizj,ijco->ofrz', patches, weight_here, pr...]
    conv_general_dilated x3 -> x0, matrix products: 4.42 us -> none  [plane_conv(): lax.conv_general_dilated(frames, kernel, (1, 1), ((0, 0), (1, 1)), dimens...]
    ppermute x4 -> x5, starting transfers between devices: 14.2 us -> 10.5 us  [the longest x2 4.38 us: slab_swap(): return lax.ppermute(value, PART, flat_pairs(sizes, pairs))]
  transfers between devices with their start and end apart: 5 -> 7, of which waited for: 2 -> 4; matrix products, arithmetic and copies ran while one was open for 5% -> 2% of each run, Pallas kernels for 0% -> 8%
where the time goes in v2:
time: 50.9 us; the launch traced here: 50.5 us
  starting transfers between devices  18.9 us (37%)
  waiting for transfers between devices  16.2 us (32%)
  Pallas kernels  10.3 us (20%)
  local copies, waits for them, and re-layouts  4.19 us (8%)
    pallas_call x5, Pallas kernels, whole_call(): pl.pallas_call(kernel, out_shape=out_shape, in_specs=specs, out_specs=jax...  10.3 us
    all_to_all x1, waiting for transfers between devices, shards(): lax.all_to_all(latent, ('tm', 'chan'), split_axis=0, concat_axis=0, tiled...  7.86 us
    all_to_all x1, waiting for transfers between devices, shards(): lax.all_to_all(message, PART, split_axis=0, concat_axis=0, tiled=True)  5.99 us
    all_to_all x1, starting transfers between devices, shards(): lax.all_to_all(message, PART, split_axis=0, concat_axis=0, tiled=True)  5.09 us
    ppermute x2, starting transfers between devices, slab_swap(): return lax.ppermute(value, PART, flat_pairs(sizes, pairs))  4.38 us
    all_to_all x1, starting transfers between devices, shards(): lax.all_to_all(latent, ('tm', 'chan'), split_axis=0, concat_axis=0, tiled...  3.39 us
    ppermute x1, starting transfers between devices, shards(): cross_other = lax.ppermute(cross, 'chan', turn)  3.01 us
    ppermute x1, starting transfers between devices, space_swap(): return lax.ppermute(value, PART, flat_pairs(sizes, pairs))  3 us
  transfers between devices with their start and end apart: 7, of which 4 were waited for; matrix products, arithmetic and copies ran while one was open for 2% of the time, Pallas kernels for 8%

profile of v2, /device:TPU:0, one launch (start us, length us, event | category | flops | bytes accessed | tf_op | source)
XLA Modules:
  0.0 50.5 jit_solution(7258668525352993869)
XLA Ops:
  0.0 1.5 %fusion.5 = (bf16[64,2,1,256]{3,2,1,0:T(2,128)(2,1)S(1)}, bf16[64,2,1,256]{3,2,1,0:T(2,128)(2,1)S(1)}) fusion(bf16[64,2,8,256]{3,2,1,0:T(8,128)(2,1)} %param.7), kind=kLoop, calls=%fused_computation.23 | loop fusion | bytes 262144 | tf_op jit(solution)/shard_map/slice | solution.py:334
  1.6 3.0 %collective-permute-start = (bf16[2,64,256]{2,1,0:T(8,128)(2,1)S(1)}, bf16[2,64,256]{2,1,0:T(8,128)(2,1)S(1)}, u32[]{:S(2)}, u32[]{:S(2)}) collective-permute-start(bf16[2,64,256]{2,1,0:T(8,128)(2,1)S(1)} %fusion.3), channel_id=1, source_target_pairs={{0,2},{2,0},{1,3},{3,1},{4,6},{6,4},{5,7},{7,5},{8,10},{10,8},{9,1... | collective-permute-start | bytes 196616 | tf_op jit(solution)/shard_map/ppermute | solution.py:36
  4.6 0.2 copy.44
  4.8 0.6 %copy-done.1 = s32[2]{0:T(128)S(1)} copy-done((s32[2]{0:T(128)S(1)}, s32[2]{0:T(128)}, u32[]{:S(2)}) %copy-start.1) | copy-done | bytes 32
  5.4 1.2 %shard_map.73 = (bf16[384,768]{1,0:T(8,128)(2,1)S(1)}, bf16[2,384,384]{2,1,0:T(8,128)(2,1)S(1)}, bf16[384,384]{1,0:T(8,128)(2,1)S(1)}) custom-call(s32[3]{0:T(128)S(1)} %pad_add_fusion.where_ref.refs_0_, s32[2]{0:T(128)S(1)} %copy-done.1, bf16[3,3,3,128,128]{4,3,2,1,0:T(8,128)(2,1)S(1)} %copy-done), custom_call_target="tpu_custom_call" | custom-call | tf_op jit(solution)/shard_map/pallas_call | solution.py:52
  6.6 0.2 collective-permute-done.refs_3_
  6.8 1.1 %shard_map.74 = (bf16[592,256]{1,0:T(8,128)(2,1)S(1)}, bf16[592,256]{1,0:T(8,128)(2,1)S(1)}) custom-call(s32[3]{0:T(128)S(1)} %pad_add_fusion.where_ref.refs_0_, s32[2]{0:T(128)S(1)} %copy-done.1, bf16[2,8,64,256]{3,2,1,0:T(8,128)(2,1)S(1)} %bitcast.36, bf16[2,64,256]{2,1,0:T(8,128)(2,1)S(1)} %collective-permute-done.refs_3_), custom_call_target="tpu_custom_call" | custom-call | tf_op jit(solution)/shard_map/pallas_call | solution.py:52
  8.0 1.3 %collective-permute-start.3 = (bf16[592,256]{1,0:T(8,128)(2,1)S(1)}, bf16[592,256]{1,0:T(8,128)(2,1)S(1)}, u32[]{:S(2)}, u32[]{:S(2)}) collective-permute-start(bf16[592,256]{1,0:T(8,128)(2,1)S(1)} %get-tuple-element.19.refs_4_), channel_id=1, source_target_pairs={{1,5},{4,0},{3,7},{6,2},{5,9},{8,4},{7,11},{10,6},{9,13},{12,8},{1... | collective-permute-start | bytes 909320 | tf_op jit(solution)/shard_map/ppermute | solution.py:48
  9.3 3.0 %collective-permute-start.1 = (bf16[592,256]{1,0:T(8,128)(2,1)S(1)}, bf16[592,256]{1,0:T(8,128)(2,1)S(1)}, u32[]{:S(2)}, u32[]{:S(2)}) collective-permute-start(bf16[592,256]{1,0:T(8,128)(2,1)S(1)} %get-tuple-element.18.refs_3_.refs_5_), channel_id=1, source_target_pairs={{0,1},{1,0},{2,3},{3,2},{4,5},{5,4},{6,7},{7,6},{8,9},{9,8},{10,11... | collective-permute-start | bytes 909320 | tf_op jit(solution)/shard_map/ppermute | solution.py:352
  12.3 3.1 %collective-permute-start.4 = (bf16[592,256]{1,0:T(8,128)(2,1)S(1)}, bf16[592,256]{1,0:T(8,128)(2,1)S(1)}, u32[]{:S(2)}, u32[]{:S(2)}) collective-permute-start(bf16[592,256]{1,0:T(8,128)(2,1)S(1)} %get-tuple-element.18.refs_3_.refs_5_), channel_id=1, source_target_pairs={{0,5},{5,0},{2,7},{7,2},{4,9},{9,4},{6,11},{11,6},{8,13},{13,8},{1... | collective-permute-start | bytes 909320 | tf_op jit(solution)/shard_map/ppermute | solution.py:48
  15.4 2.8 %shard_map.75 = (f32[8,128,256]{2,1,0:T(8,128)S(1)}, bf16[4,128,256]{2,1,0:T(8,128)(2,1)S(1)}, f32[8,128]{1,0:T(8,128)S(1)}) custom-call(s32[3]{0:T(128)S(1)} %pad_add_fusion.where_ref.refs_0_, bf16[384,768]{1,0:T(8,128)(2,1)S(1)} %get-tuple-element.16.refs_1_, bf16[384,384]{1,0:T(8,128)(2,1)S(1)} %get-tuple-element.17.refs_2_, ...), custom_call_target="tpu_custom_call" | custom-call | tf_op jit(solution)/shard_map/pallas_call | solution.py:52
  18.2 2.2 %collective-permute-done.4.refs_8_ = bf16[592,256]{1,0:T(8,128)(2,1)S(1)} collective-permute-done((bf16[592,256]{1,0:T(8,128)(2,1)S(1)}, bf16[592,256]{1,0:T(8,128)(2,1)S(1)}, u32[]{:S(2)}, u32[]{:S(2)}) %collective-permute-start.4) | collective-permute-done | bytes 303136 | tf_op jit(solution)/shard_map/ppermute | solution.py:48
  20.4 2.5 %shard_map.76 = (bf16[8,128,256]{2,1,0:T(8,128)(2,1)S(1)}, f32[16,8,128]{2,1,0:T(8,128)}) custom-call(s32[3]{0:T(128)S(1)} %pad_add_fusion.where_ref.refs_0_, s32[2]{0:T(128)S(1)} %copy-done.1, f32[1,128]{1,0:T(1,128)S(1)} %pad.6.refs_2_, bf16[2,384,384]{2,1,0:T(8,128)(2,1)S(1)} %get-tuple-element.15.refs_3_, f32[8,128,256]{2,1,0:T(8,128)S(1)} %get-tuple-element.20.refs_4_, ...), custom_call_target="tpu_custom_call" | custom-call | tf_op jit(solution)/shard_map/pallas_call | solution.py:52
  22.9 5.1 %all-to-all-start = ((f32[16,8,128]{2,1,0:T(8,128)}), f32[16,8,128]{2,1,0:T(8,128)S(1)}, u32[]{:S(2)}, u32[]{:S(2)}) async-start(f32[16,8,128]{2,1,0:T(8,128)} %get-tuple-element.22.refs_1_), calls=%async_computation | async-start | bytes 131072 | tf_op jit(solution)/shard_map/all_to_all | solution.py:385
  28.0 0.1 add.30
  28.2 0.6 %copy-done.4 = f32[128]{0:T(128)S(1)} copy-done((f32[128]{0:T(128)S(1)}, f32[128]{0:T(128)}, u32[]{:S(2)}) %copy-start.4) | copy-done | bytes 536
  28.9 6.0 %all-to-all-done.refs_2_ = f32[16,8,128]{2,1,0:T(8,128)S(1)} async-done(((f32[16,8,128]{2,1,0:T(8,128)}), f32[16,8,128]{2,1,0:T(8,128)S(1)}, u32[]{:S(2)}, u32[]{:S(2)}) %all-to-all-start) | async-done | bytes 65568 | tf_op jit(solution)/shard_map/all_to_all | solution.py:385
  34.9 0.2 convert_reduce_fusion
  35.3 2.7 %shard_map.77 = bf16[8,6,16,128]{3,2,1,0:T(8,128)(2,1)} custom-call(s32[3]{0:T(128)S(1)} %pad_add_fusion.where_ref.refs_0_, f32[16,8,128]{2,1,0:T(8,128)} %get-tuple-element.22.refs_1_, f32[16,8,128]{2,1,0:T(8,128)S(1)} %all-to-all-done.refs_2_, f32[2,128]{1,0:T(2,128)S(1)} %pad_maximum_fusion.refs_3_, bf16[32,512]{1,0:T(8,128)(2,1)S(1)} %bitcast.38, ...), custom_call_target="tpu_custom_call" | custom-call | tf_op jit(solution)/shard_map/pallas_call | solution.py:52
  38.0 3.4 %all-to-all-start.1 = ((bf16[8,6,16,128]{3,2,1,0:T(8,128)(2,1)}), bf16[8,6,16,128]{3,2,1,0:T(8,128)(2,1)S(1)}, u32[]{:S(2)}, u32[]{:S(2)}) async-start(bf16[8,6,16,128]{3,2,1,0:T(8,128)(2,1)} %shard_map.77), calls=%async_computation.1 | async-start | bytes 393216 | tf_op jit(solution)/shard_map/all_to_all | solution.py:395
  41.7 0.1 eq.50
  41.8 7.9 %all-to-all-done.1 = bf16[8,6,16,128]{3,2,1,0:T(8,128)(2,1)S(1)} async-done(((bf16[8,6,16,128]{3,2,1,0:T(8,128)(2,1)}), bf16[8,6,16,128]{3,2,1,0:T(8,128)(2,1)S(1)}, u32[]{:S(2)}, u32[]{:S(2)}) %all-to-all-start.1) | async-done | bytes 196640 | tf_op jit(solution)/shard_map/all_to_all | solution.py:395
  49.7 0.2 fusion
  49.8 0.6 %copy.34 = bf16[2,8,16,128]{3,2,1,0:T(8,128)(2,1)} copy(bf16[2,8,16,128]{3,1,2,0:T(8,128)(2,1)S(1)} %fusion) | data formatting | bytes 131072
  (40 shorter events, 0.9 us)
Async XLA Ops:
  0.0 4.6 %copy-start.2 = (bf16[64,2,8,256]{3,2,1,0:T(8,128)(2,1)S(1)}, bf16[64,2,8,256]{3,2,1,0:T(8,128)(2,1)}, u32[]{:S(2)}) copy-start(bf16[64,2,8,256]{3,2,1,0:T(8,128)(2,1)} %param.7) | copy-start | bytes 1572868
  0.0 4.8 %copy-start = (bf16[3,3,3,128,128]{4,3,2,1,0:T(8,128)(2,1)S(1)}, bf16[3,3,3,128,128]{4,3,2,1,0:T(8,128)(2,1)}, u32[]{:S(2)}) copy-start(bf16[3,3,3,128,128]{4,3,2,1,0:T(8,128)(2,1)} %weight_ref.1) | copy-start | bytes 2654212
  1.6 5.2 %collective-permute-start = (bf16[2,64,256]{2,1,0:T(8,128)(2,1)S(1)}, bf16[2,64,256]{2,1,0:T(8,128)(2,1)S(1)}, u32[]{:S(2)}, u32[]{:S(2)}) collective-permute-start(bf16[2,64,256]{2,1,0:T(8,128)(2,1)S(1)} %fusion.3), channel_id=1, source_target_pairs={{0,2},{2,0},{1,3},{3,1},{4,6},{6,4},{5,7},{7,5},{8,10},{10,8},{9,1... | collective-permute-start | bytes 196616 | tf_op jit(solution)/shard_map/ppermute | solution.py:36
  4.7 0.7 %copy-start.1 = (s32[2]{0:T(128)S(1)}, s32[2]{0:T(128)}, u32[]{:S(2)}) copy-start(s32[2]{0:T(128)} %refs_1_.3) | copy-start | bytes 28
  7.9 7.5 %copy-start.6 = (s32[1,8,1]{1,2,0:T(1,128)S(1)}, s32[1,8,1]{1,2,0:T(1,128)}, u32[]{:S(2)}) copy-start(s32[1,8,1]{1,2,0:T(1,128)} %param.13) | copy-start | bytes 100
  7.9 7.5 %collective-permute-start.2 = (bf16[592,256]{1,0:T(8,128)(2,1)S(1)}, bf16[592,256]{1,0:T(8,128)(2,1)S(1)}, u32[]{:S(2)}, u32[]{:S(2)}) collective-permute-start(bf16[592,256]{1,0:T(8,128)(2,1)S(1)} %get-tuple-element.19.refs_4_), channel_id=1, source_target_pairs={{0,1},{1,0},{2,3},{3,2},{4,5},{5,4},{6,7},{7,6},{8,9},{9,8},{10,11... | collective-permute-start | bytes 909320 | tf_op jit(solution)/shard_map/ppermute | solution.py:353
  8.0 10.2 %collective-permute-start.3 = (bf16[592,256]{1,0:T(8,128)(2,1)S(1)}, bf16[592,256]{1,0:T(8,128)(2,1)S(1)}, u32[]{:S(2)}, u32[]{:S(2)}) collective-permute-start(bf16[592,256]{1,0:T(8,128)(2,1)S(1)} %get-tuple-element.19.refs_4_), channel_id=1, source_target_pairs={{1,5},{4,0},{3,7},{6,2},{5,9},{8,4},{7,11},{10,6},{9,13},{12,8},{1... | collective-permute-start | bytes 909320 | tf_op jit(solution)/shard_map/ppermute | solution.py:48
  9.3 6.2 %collective-permute-start.1 = (bf16[592,256]{1,0:T(8,128)(2,1)S(1)}, bf16[592,256]{1,0:T(8,128)(2,1)S(1)}, u32[]{:S(2)}, u32[]{:S(2)}) collective-permute-start(bf16[592,256]{1,0:T(8,128)(2,1)S(1)} %get-tuple-element.18.refs_3_.refs_5_), channel_id=1, source_target_pairs={{0,1},{1,0},{2,3},{3,2},{4,5},{5,4},{6,7},{7,6},{8,9},{9,8},{10,11... | collective-permute-start | bytes 909320 | tf_op jit(solution)/shard_map/ppermute | solution.py:352
  12.3 8.1 %collective-permute-start.4 = (bf16[592,256]{1,0:T(8,128)(2,1)S(1)}, bf16[592,256]{1,0:T(8,128)(2,1)S(1)}, u32[]{:S(2)}, u32[]{:S(2)}) collective-permute-start(bf16[592,256]{1,0:T(8,128)(2,1)S(1)} %get-tuple-element.18.refs_3_.refs_5_), channel_id=1, source_target_pairs={{0,5},{5,0},{2,7},{7,2},{4,9},{9,4},{6,11},{11,6},{8,13},{13,8},{1... | collective-permute-start | bytes 909320 | tf_op jit(solution)/shard_map/ppermute | solution.py:48
  22.9 5.3 %copy-start.3 = (bf16[2,2,128,32]{2,3,1,0:T(8,128)(2,1)S(1)}, bf16[2,2,128,32]{2,3,1,0:T(8,128)(2,1)}, u32[]{:S(2)}) copy-start(bf16[2,2,128,32]{2,3,1,0:T(8,128)(2,1)} %param.12) | copy-start | bytes 98308
  22.9 12.0 %all-to-all-start = ((f32[16,8,128]{2,1,0:T(8,128)}), f32[16,8,128]{2,1,0:T(8,128)S(1)}, u32[]{:S(2)}, u32[]{:S(2)}) async-start(f32[16,8,128]{2,1,0:T(8,128)} %get-tuple-element.22.refs_1_), calls=%async_computation | async-start | bytes 131072 | tf_op jit(solution)/shard_map/all_to_all | solution.py:385
  28.2 0.7 %copy-start.4 = (f32[128]{0:T(128)S(1)}, f32[128]{0:T(128)}, u32[]{:S(2)}) copy-start(f32[128]{0:T(128)} %param.11) | copy-start | bytes 1540
  28.2 0.7 %copy-start.5 = (f32[128]{0:T(128)S(1)}, f32[128]{0:T(128)}, u32[]{:S(2)}) copy-start(f32[128]{0:T(128)} %param.10) | copy-start | bytes 1540
  38.0 11.7 %all-to-all-start.1 = ((bf16[8,6,16,128]{3,2,1,0:T(8,128)(2,1)}), bf16[8,6,16,128]{3,2,1,0:T(8,128)(2,1)S(1)}, u32[]{:S(2)}, u32[]{:S(2)}) async-start(bf16[8,6,16,128]{3,2,1,0:T(8,128)(2,1)} %shard_map.77), calls=%async_computation.1 | async-start | bytes 393216 | tf_op jit(solution)/shard_map/all_to_all | solution.py:395

commit v3 on v2

v3 whole, which is shorter than its diff:
```python
import jax
import jax.numpy as jnp
import numpy as np
from jax import lax
from jax.experimental import pallas as pl
from jax.experimental.pallas import tpu as pltpu
from jax.sharding import PartitionSpec as P

CHANNELS = 128
GROUPS = 32
MOMENTS = 32
SEND_ROWS = 8
ID_ROWS = 16
BF16 = jnp.bfloat16
F32 = jnp.float32
VMEM = pl.BlockSpec(memory_space=pltpu.VMEM)
PARAMS = pltpu.CompilerParams(vmem_limit_bytes=40 * 1024 * 1024)
PART = ("tm", "space", "chan")


def flat_pairs(sizes, pairs):
    _, spaces, chans = sizes
    return [
        ((a[0] * spaces + a[1]) * chans + a[2], (b[0] * spaces + b[1]) * chans + b[2])
        for a, b in pairs
    ]


def space_swap(value, sizes, start):
    slabs, spaces, chans = sizes
    pairs = []
    for low in range(start, spaces - 1, 2):
        for t in range(slabs):
            for c in range(chans):
                pairs += [((t, low, c), (t, low + 1, c)), ((t, low + 1, c), (t, low, c))]
    return lax.ppermute(value, PART, flat_pairs(sizes, pairs))


def slab_swap(value, sizes, cross):
    slabs, spaces, _ = sizes
    last = slabs - 1
    pairs = []
    for s in range(spaces):
        for t in range(last):
            if cross:
                pairs += [((t, s, 0), (t + 1, s, 1)), ((t + 1, s, 1), (t, s, 0))]
            else:
                pairs += [((t, s, 1), (t + 1, s, 1)), ((t + 1, s, 0), (t, s, 0))]
        if spaces % 2 == 0 and cross:
            pairs += [((0, s, 1), (0, s ^ 1, 1)), ((last, s, 0), (last, s ^ 1, 0))]
        elif spaces % 2 == 0:
            pairs += [((last, s, 1), (last, s, 0)), ((0, s, 0), (0, s, 1))]
    return lax.ppermute(value, PART, flat_pairs(sizes, pairs))


def whole_call(kernel, out_shape, args, scratch=(), specs=None, flops=0):
    return pl.pallas_call(
        kernel,
        out_shape=out_shape,
        in_specs=specs or [VMEM] * len(args),
        out_specs=jax.tree.map(lambda _: VMEM, out_shape),
        scratch_shapes=scratch,
        compiler_params=PARAMS,
        cost_estimate=pl.CostEstimate(flops=flops, bytes_accessed=flops // 400, transcendentals=0),
    )(*args)


def number_at(small_ref, n):
    lane = lax.broadcasted_iota(jnp.int32, (1, CHANNELS), 1)
    return jnp.sum(jnp.where(lane == n, small_ref[2:3, :], 0.0))


def edge_kernel(frames_ref, split_ref, *edge_refs):
    chan = lax.axis_index("chan")
    odd = lax.axis_index("space") % 2 == 1
    _, rows, half, columns = frames_ref.shape
    source = lax.broadcasted_iota(jnp.int32, (columns, columns), 0)
    target = lax.broadcasted_iota(jnp.int32, (1, columns), 1)
    wanted = jnp.where(target < columns // 2, 2 * target, 2 * target - columns + 1)
    split_ref[...] = jnp.where(source == wanted, 1.0, 0.0).astype(BF16)
    for h, edge_ref in enumerate(edge_refs):
        to_low = odd if h == 0 else jnp.logical_not(odd)
        line = jnp.where(to_low, 0, rows - 1)
        image = jnp.concatenate([frames_ref[1 - chan, line], frames_ref[chan, line]], axis=0)
        edge_ref[...] = jnp.dot(image, split_ref[...], preferred_element_type=F32).astype(BF16)


def interior_kernel(frames_ref, split_ref, cross_ref, same_ref, both_ref):
    chan = lax.axis_index("chan")
    _, rows, half, columns = frames_ref.shape
    inside = rows * half
    for out_ref, frame, n in ((cross_ref, 1 - chan, 0), (same_ref, chan, 1)):
        image = frames_ref[frame].reshape(inside, columns)
        value = jnp.dot(image, split_ref[...], preferred_element_type=F32).astype(BF16)
        out_ref[...] = value
        both_ref[n * inside : (n + 1) * inside, :] = value


def halo_kernel(halos, capacity, small_ref, *refs):
    halo_refs, kept_refs, (cross_ref, same_ref) = refs[:halos], refs[halos : 2 * halos], refs[2 * halos :]
    for halo_ref, kept_ref in zip(halo_refs, kept_refs):
        kept_ref[...] = halo_ref[...]
    chan = lax.axis_index("chan")
    half, columns = CHANNELS // 2, cross_ref.shape[1]
    count = SEND_ROWS
    line = lax.broadcasted_iota(jnp.int32, (ID_ROWS, CHANNELS), 0)
    lane = lax.broadcasted_iota(jnp.int32, (ID_ROWS, CHANNELS), 1)
    owners = jnp.broadcast_to(small_ref[3:4, :], (ID_ROWS, CHANNELS))
    mine = jnp.sum(jnp.where(line == lane, owners, 0.0), axis=1, keepdims=True)
    rank = jnp.sum(jnp.where((owners == mine) & (lane < line), 1.0, 0.0), axis=1, keepdims=True)
    keys = mine * float(capacity) + rank + 1.0
    place = lax.broadcasted_iota(jnp.int32, (ID_ROWS, columns), 0)
    tail = jnp.where(place < count, keys, 0.0)
    ids = [number_at(small_ref, n) for n in range(2)]
    for n, (out_ref, frame) in enumerate(((cross_ref, 1 - chan), (same_ref, chan))):
        for h in range(halos):
            out_ref[h * half : (h + 1) * half, :] = halo_refs[h][n * half : (n + 1) * half, :]
        number = jnp.where(frame == 0, ids[0], ids[1])
        out_ref[halos * half :, :] = jnp.where(place == count, number + 1.0, tail).astype(BF16)


def weights_kernel(
    ids_any, owner_any, gain_any, bias_any, out_weight_any, weight_ref, _, local_ref, late_ref, sum_ref, small_ref,
    out_matrix_ref, ids_ref, owner_ref, gain_ref, bias_ref, out_weight_ref, taps_ref, copies
):
    chan = lax.axis_index("chan")
    fetched = [
        pltpu.make_async_copy(source, target, copies.at[n])
        for n, (source, target) in enumerate(
            (
                (ids_any, ids_ref),
                (owner_any, owner_ref),
                (gain_any, gain_ref),
                (bias_any, bias_ref),
                (out_weight_any, out_weight_ref),
            )
        )
    ]
    for copy in fetched:
        copy.start()
    half = CHANNELS // 2
    own = pl.multiple_of(chan * half, half)
    other = pl.multiple_of((1 - chan) * half, half)
    for j in range(3):
        for i in range(3):
            for k in range(3):
                block = jnp.concatenate(
                    [weight_ref[k, i, j, pl.ds(own, half), :], weight_ref[k, i, j, pl.ds(other, half), :]],
                    axis=0,
                )
                taps_ref[k, i, j] = block.T
    for copy in fetched:
        copy.wait()
    small_ref[...] = jnp.zeros_like(small_ref)
    small_ref[0:1, :] = gain_ref[...]
    small_ref[1:2, :] = bias_ref[...]
    small_ref[2:3, : ids_ref.shape[1]] = ids_ref[...].astype(F32)
    small_ref[3:4, :SEND_ROWS] = owner_ref[...].astype(F32)
    for i in range(2):
        for j in range(2):
            first = (2 * i + j) * CHANNELS
            out_matrix_ref[:, first : first + CHANNELS] = out_weight_ref[i, j]
    zero = jnp.float32(0.0)
    one = jnp.float32(1.0)
    first = chan == 0
    joined = number_at(small_ref, 0) == number_at(small_ref, 1)
    flag = jnp.where(joined, one, zero)
    on_first = jnp.where(first, one, zero)
    on_second = one - on_first
    near = (
        on_first * (one - flag),
        on_first + on_second * flag,
        zero,
    )
    far = (
        on_first * flag + on_second * (one - flag),
        on_second * (one - flag),
        on_second,
    )
    late_same = (on_second * flag, zero, on_first)
    late_apart = (on_first + on_second * flag, on_first, on_first)
    for j in range(3):
        for i in range(3):
            taps = [taps_ref[k, i, j].astype(F32) for k in range(3)]

            def mixed(scale):
                return (taps[0] * scale[0] + taps[1] * scale[1] + taps[2] * scale[2]).astype(BF16)

            rows = slice(j * CHANNELS, (j + 1) * CHANNELS)
            columns = slice(i * CHANNELS, (i + 1) * CHANNELS)
            shifted = slice((3 + i) * CHANNELS, (4 + i) * CHANNELS)
            local_ref[rows, columns] = mixed(near)
            local_ref[rows, shifted] = mixed(far)
            late_ref[0, rows, columns] = mixed(late_same)
            late_ref[1, rows, columns] = mixed(late_apart)
            sum_ref[rows, columns] = mixed((one, one, one))


def image_row(sources, rows, odd, r):
    half = CHANNELS // 2
    pieces = []
    for ref, start, halos in sources:
        if 0 <= r < rows:
            pieces.append(ref[start + r * half : start + (r + 1) * half, :])
            continue
        edges = [halo_ref[first : first + half, :] for halo_ref, first in halos]
        edges.append(jnp.zeros_like(edges[0]))
        on_first = odd if r < 0 else jnp.logical_not(odd)
        pieces.append(jnp.where(on_first, edges[0], edges[1]))
    return jnp.concatenate(pieces, axis=0)


def local_sources(rows, cross_ref, same_ref, other_ref, own_halos, other_halos):
    half = CHANNELS // 2
    inside = rows * half
    near = (
        (cross_ref, 0, [(ref, 0) for ref in own_halos]),
        (other_ref, inside, [(ref, half) for ref in other_halos]),
    )
    far = (
        (same_ref, 0, [(ref, half) for ref in own_halos]),
        (other_ref, 0, [(ref, 0) for ref in other_halos]),
    )
    return near, far


def joined_columns(product):
    half = product.shape[1] // 2
    left = product[:CHANNELS, :]
    middle = product[CHANNELS : 2 * CHANNELS, :]
    right = product[2 * CHANNELS :, :]
    lane = lax.broadcasted_iota(jnp.int32, (CHANNELS, half), 1)
    from_left = jnp.where(lane == 0, 0.0, pltpu.roll(left[:, half:], 1, 1))
    from_right = jnp.where(lane == half - 1, 0.0, pltpu.roll(right[:, :half], half - 1, 1))
    even = from_left + middle[:, :half] + right[:, half:]
    odd = left[:, :half] + middle[:, half:] + from_right
    return even, odd


def lane_totals(first, second):
    rows = [jnp.sum(value.T, axis=0, keepdims=True) for value in (first, second)]
    return rows


def local_kernel(rows, halos, weight_ref, sum_ref, *refs):
    conv_ref, extra_ref, sums_ref, images_ref = refs[3 + 2 * halos :]
    near, far = local_sources(rows, *refs[:3], refs[3 : 3 + halos], refs[3 + halos : 3 + 2 * halos])
    odd = lax.axis_index("space") % 2 == 1
    chan = lax.axis_index("chan")
    half = conv_ref.shape[2] // 2
    for r in range(rows):
        image = jnp.concatenate(
            [image_row(frame, rows, odd, r + i) for frame in (near, far) for i in (-1, 0, 1)], axis=0
        )
        product = jnp.dot(weight_ref[...], image, preferred_element_type=F32)
        for side, value in enumerate(joined_columns(product)):
            conv_ref[r, :, side * half : (side + 1) * half] = value
    sums_ref[...] = jnp.zeros_like(sums_ref)

    @pl.when(lax.axis_index("tm") == 0)
    def _():
        rows_here = rows // 2
        for n in range(rows_here + 2):
            upper = image_row(far, rows, odd, n - 1)
            lower = image_row(near, rows, odd, rows_here + n - 1)
            images_ref[n] = jnp.where(chan == 0, upper, lower)
        totals = [jnp.zeros((CHANNELS, half), F32)] * 2
        for r in range(rows_here):
            image = jnp.concatenate([images_ref[r + i] for i in range(3)], axis=0)
            product = jnp.dot(sum_ref[...], image, preferred_element_type=F32)
            for side, value in enumerate(joined_columns(product)):
                value = value.astype(BF16)
                extra_ref[r, :, side * half : (side + 1) * half] = value
                value = value.astype(F32)
                totals = [totals[0] + value, totals[1] + value * value]
        one, two = lane_totals(*totals)
        sums_ref[0:1, :] = one
        sums_ref[1:2, :] = two


def late_kernel(rows, halos, slabs, small_ref, weight_ref, part_ref, sums_ref, own_edge_ref, *refs):
    near, _ = local_sources(rows, *refs[:3], refs[3 : 3 + halos], refs[3 + halos : 3 + 2 * halos])
    refs = refs[3 + 2 * halos :]
    late_own_ref, late_other_ref, own_halo_ref, other_halo_ref = refs[:4]
    conv_ref, message_ref, keys_ref, images_ref = refs[4:]
    extent = CHANNELS // 2
    arrived = (
        (late_own_ref, 0, [(own_halo_ref, h * extent) for h in range(halos)]),
        (late_other_ref, 0, [(other_halo_ref, h * extent) for h in range(halos)]),
    )
    odd = lax.axis_index("space") % 2 == 1
    slab = lax.axis_index("tm")
    first = lax.axis_index("chan") == 0
    half = part_ref.shape[2] // 2
    kept = rows // 2
    tail = halos * extent
    absent = slab == jnp.where(first, slabs - 1, 0)
    late_tail = jnp.where(absent, 0.0, own_halo_ref[tail:, :CHANNELS].astype(F32))
    own_tail = own_edge_ref[tail:, :CHANNELS].astype(F32)
    number = jnp.max(late_tail[2 * kept : 2 * kept + 1, :]) - 1.0
    ids = [number_at(small_ref, n) for n in range(2)]
    same = number == jnp.where(first, ids[1], ids[0])
    keep = jnp.where(jnp.logical_or(same, jnp.logical_not(first)), 1.0, 0.0)
    use_late = jnp.logical_or(same, first)
    choice = jnp.where(same, 0, 1)
    for r in range(-1, rows + 1):
        late = image_row(arrived, rows, odd, r)
        here = image_row(near, rows, odd, r)
        images_ref[r + 1] = jnp.where(use_late, late, here)
    totals = [jnp.zeros((CHANNELS, half), F32)] * 2
    for r in range(rows):
        image = jnp.concatenate([images_ref[r + i] for i in range(3)], axis=0)
        product = jnp.dot(weight_ref[choice], image, preferred_element_type=F32)
        for side, value in enumerate(joined_columns(product)):
            lanes = slice(side * half, (side + 1) * half)
            value = (value + keep * part_ref[r, :, lanes]).astype(BF16)
            conv_ref[r, :, lanes] = value
            value = value.astype(F32)
            totals = [totals[0] + value, totals[1] + value * value]
    one, two = lane_totals(*totals)
    main_id = jnp.where(first, number, ids[1])
    extra_id = jnp.where(slab == 0, ids[0], -1.0)
    line = lax.broadcasted_iota(jnp.int32, (8, CHANNELS), 0)
    message = jnp.where(line == 0, one, 0.0)
    message = jnp.where(line == 1, two, message)
    message = jnp.where(line == 2, sums_ref[0:1, :], message)
    message = jnp.where(line == 3, sums_ref[1:2, :], message)
    message = jnp.where(line == 4, main_id, message)
    message = jnp.where(line == 5, extra_id, message)
    for p in range(message_ref.shape[0]):
        message_ref[p] = message
    keys = jnp.zeros((8, CHANNELS), F32)
    for n in range(kept):
        main_key = jnp.where(first, late_tail[n : n + 1, :], own_tail[kept + n : kept + n + 1, :])
        keys = jnp.where(line == n, main_key, keys)
    quarter = kept // 2
    for n in range(quarter):
        extra_key = jnp.where(first, own_tail[n : n + 1, :], own_tail[quarter + n : quarter + n + 1, :])
        keys = jnp.where(line == kept + n, jnp.where(slab == 0, extra_key, 0.0), keys)
    keys_ref[...] = keys


def norm_kernel(
    count, capacity, message_ref, keys_ref, gathered_ref, small_ref, out_matrix_ref, conv_ref, extra_ref, latent_ref
):
    rows, _, columns = conv_ref.shape
    half = columns // 2
    main = gathered_ref[:, 4, :]
    extra = gathered_ref[:, 5, :]
    lines = []
    for number in (message_ref[0, 4:5, :], message_ref[0, 5:6, :]):
        on_main = main == number
        on_extra = extra == number
        for n in range(2):
            picked = jnp.where(on_main, gathered_ref[:, n, :], 0.0) + jnp.where(
                on_extra, gathered_ref[:, 2 + n, :], 0.0
            )
            lines.append(jnp.sum(picked, axis=0, keepdims=True))
        held = jnp.where(on_main, float(count), 0.0) + jnp.where(on_extra, float(count // 2), 0.0)
        lines.append(jnp.sum(held, axis=0, keepdims=True))
    lines += [jnp.zeros((1, CHANNELS), F32)] * 2
    size = CHANNELS // GROUPS
    group_row = lax.broadcasted_iota(jnp.int32, (CHANNELS, CHANNELS), 0) // size
    group_column = lax.broadcasted_iota(jnp.int32, (CHANNELS, CHANNELS), 1) // size
    member = jnp.where(group_row == group_column, 1.0, 0.0)
    totals = jnp.dot(
        jnp.concatenate(lines, axis=0), member, preferred_element_type=F32, precision=lax.Precision.HIGHEST
    )

    def factors(first):
        counts = totals[first + 2 : first + 3, :]
        mean = totals[first : first + 1, :] / counts
        var = totals[first + 1 : first + 2, :] / counts - mean * mean
        scale = lax.rsqrt(var + 1e-06) * small_ref[0:1, :]
        offset = small_ref[1:2, :] - mean * scale
        return [jnp.broadcast_to(value, (CHANNELS, CHANNELS)).T for value in (scale, offset)]

    def project(source_ref, scale, offset):
        images = []
        for r in range(source_ref.shape[0] // 2):
            pieces = []
            for i in range(2):
                for j in range(2):
                    value = source_ref[2 * r + i, :, j * half : (j + 1) * half].astype(F32)
                    value = value * scale + offset
                    pieces.append((value / (1.0 + jnp.exp(-value))).astype(BF16))
            images.append(jnp.concatenate(pieces, axis=0))
        image = jnp.concatenate(images, axis=1)
        return jnp.dot(out_matrix_ref[...], image, preferred_element_type=F32)

    slots, places, chans = latent_ref.shape[1], latent_ref.shape[0] // 2, 2
    part = MOMENTS // chans

    def place(latent, first_key, wanted, slot):
        for c in range(chans):
            blocks = [
                latent[c * part : (c + 1) * part, r * half : (r + 1) * half] for r in range(latent.shape[1] // half)
            ]
            for t in range(places):
                for j in range(wanted):
                    value = jnp.zeros((part, half), F32)
                    for n, block in enumerate(blocks):
                        key = keys_ref[first_key + n : first_key + n + 1, :]
                        value = jnp.where(key == float(t * capacity + j + 1), block, value)
                    yield t * chans + c, slot + j, value

    kept = rows // 2
    for p, j, value in place(project(conv_ref, *factors(0)), 0, capacity, 0):
        latent_ref[p, j] = value.astype(BF16)
    for p in range(latent_ref.shape[0]):
        for j in range(capacity, slots):
            latent_ref[p, j] = jnp.zeros((part, half), BF16)

    @pl.when(lax.axis_index("tm") == 0)
    def _():
        latent = project(extra_ref, *factors(3))

        @pl.when(lax.axis_index("chan") == 0)
        def _():
            for p, j, value in place(latent, kept, slots - capacity, capacity):
                latent_ref[p, j] = value.astype(BF16)

        @pl.when(lax.axis_index("chan") == 1)
        def _():
            for p, j, value in place(latent, kept, capacity, 0):
                latent_ref[p, j] = (latent_ref[p, j].astype(F32) + value).astype(BF16)


def shards(activations, frame_clip, conv_weight, norm_gain, norm_bias, out_weight, owner):
    half, frames, rows, columns = activations.shape
    sizes = tuple(lax.axis_size(name) for name in PART)
    slabs, spaces, chans = sizes
    assert (frames, chans, half * chans) == (2, 2, CHANNELS)
    parts = slabs * spaces * chans
    halos = 1 if spaces <= 2 else 2
    send_rows = frames * (rows // 2)
    capacity = max(2, 2 * send_rows // slabs)
    kept = rows // 2
    assert send_rows == SEND_ROWS
    payload = jax.ShapeDtypeStruct((rows * half, columns), BF16)
    pair = jax.ShapeDtypeStruct((2 * half, columns), BF16)
    planes = activations.transpose(1, 2, 0, 3)
    split, *edges = whole_call(
        edge_kernel, (jax.ShapeDtypeStruct((columns, columns), BF16),) + (pair,) * halos, (planes,)
    )
    own_halos = [space_swap(edge, sizes, start) for start, edge in enumerate(edges)]
    cross, same, both = whole_call(
        interior_kernel,
        (payload, payload, jax.ShapeDtypeStruct((2 * rows * half, columns), BF16)),
        (planes, split),
        flops=300_000_000,
    )
    late_own = slab_swap(same, sizes, False)
    late_other = slab_swap(cross, sizes, True)
    turn = [(0, 1), (1, 0)]
    other = lax.ppermute(both, "chan", turn)
    local_weight, late_weight, sum_weight, small, out_matrix = whole_call(
        weights_kernel,
        (
            jax.ShapeDtypeStruct((3 * CHANNELS, 6 * CHANNELS), BF16),
            jax.ShapeDtypeStruct((2, 3 * CHANNELS, 3 * CHANNELS), BF16),
            jax.ShapeDtypeStruct((3 * CHANNELS, 3 * CHANNELS), BF16),
            jax.ShapeDtypeStruct((8, CHANNELS), F32),
            jax.ShapeDtypeStruct((MOMENTS, 4 * CHANNELS), BF16),
        ),
        (
            frame_clip.reshape(1, frames), owner.reshape(1, send_rows), norm_gain.reshape(1, CHANNELS),
            norm_bias.reshape(1, CHANNELS), out_weight.transpose(0, 1, 3, 2), conv_weight, both,
        ),
        [
            pltpu.VMEM((1, frames), jnp.int32),
            pltpu.VMEM((1, send_rows), jnp.int32),
            pltpu.VMEM((1, CHANNELS), F32),
            pltpu.VMEM((1, CHANNELS), F32),
            pltpu.VMEM((2, 2, MOMENTS, CHANNELS), BF16),
            pltpu.VMEM((3, 3, 3, CHANNELS, CHANNELS), BF16),
            pltpu.SemaphoreType.DMA((5,)),
        ],
        [pl.BlockSpec(memory_space=pl.ANY)] * 5 + [VMEM] * 2,
        1_200_000_000,
    )
    message_halo = jax.ShapeDtypeStruct((halos * half + ID_ROWS, columns), BF16)
    *own_halos, cross_halo, same_halo = whole_call(
        lambda *refs: halo_kernel(halos, capacity, *refs),
        (pair,) * halos + (message_halo, message_halo),
        (small, *own_halos),
    )
    other_halos = [lax.ppermute(halo, "chan", turn) for halo in own_halos]
    late_own_halo = slab_swap(same_halo, sizes, False)
    late_other_halo = slab_swap(cross_halo, sizes, True)
    here = (cross, same, other, *own_halos, *other_halos)
    part, extra, extra_sums = whole_call(
        lambda *refs: local_kernel(rows, halos, *refs),
        (
            jax.ShapeDtypeStruct((rows, CHANNELS, columns), F32),
            jax.ShapeDtypeStruct((rows // 2, CHANNELS, columns), BF16),
            jax.ShapeDtypeStruct((8, CHANNELS), F32),
        ),
        (local_weight, sum_weight, *here),
        [pltpu.VMEM((rows // 2 + 2, CHANNELS, columns), BF16)],
        flops=1_800_000_000,
    )
    conv, message, keys = whole_call(
        lambda *refs: late_kernel(rows, halos, slabs, *refs),
        (
            jax.ShapeDtypeStruct((rows, CHANNELS, columns), BF16),
            jax.ShapeDtypeStruct((parts, 8, CHANNELS), F32),
            jax.ShapeDtypeStruct((8, CHANNELS), F32),
        ),
        (
            small, late_weight, part, extra_sums, cross_halo, *here, late_own, late_other, late_own_halo, late_other_halo,
        ),
        [pltpu.VMEM((rows + 2, CHANNELS, columns), BF16)],
        flops=1_500_000_000,
    )
    gathered = lax.all_to_all(message, PART, split_axis=0, concat_axis=0, tiled=True)
    slots = capacity + kept // 2
    latent = whole_call(
        lambda *refs: norm_kernel(rows * columns, capacity, *refs),
        jax.ShapeDtypeStruct((slabs * chans, slots, MOMENTS // chans, columns // 2), BF16),
        (message, keys, gathered, small, out_matrix, conv, extra),
    )
    arrived = lax.all_to_all(latent, ("tm", "chan"), split_axis=0, concat_axis=0, tiled=True)
    arrived = arrived.reshape((slabs, chans) + arrived.shape[1:])
    later = arrived[:, 1, :capacity]
    begin = jnp.pad(arrived[:1, 0, capacity:], ((0, 0), (0, 2 * capacity - slots), (0, 0), (0, 0)))
    sooner = jnp.concatenate([begin, arrived[:-1, 0, :capacity]])
    return (later + sooner).reshape(1, slabs * capacity, MOMENTS // chans, columns // 2)


def solution(mesh):
    placed = (
        P(("groups", "chan"), "tm", "space", None),
        P(("groups", "tm")),
        P(),
        P(),
        P(),
        P(),
        P(("groups", "space"), "tm", None),
    )
    return jax.shard_map(
        shards,
        mesh=mesh,
        in_specs=placed,
        out_specs=P(("groups", "space"), "tm", "chan", None),
        check_vma=False,
    )
```

time: 50.9 us -> 39.6 us (0.78)
  blocking collectives: 0 us -> 21 us
  waiting for transfers between devices: 16.2 us -> 1.78 us
  starting transfers between devices: 18.9 us -> 7.45 us
  Pallas kernels: 10.3 us -> 6.47 us
  local copies, waits for them, and re-layouts: 4.19 us -> 1.89 us
    all_to_all x0 -> x2, blocking collectives: none -> 21 us  [the longest x1 10.7 us: shards(): lax.all_to_all(latent, ('tm', 'chan'), split_axis=0, concat_axis=0, tiled...]
    all_to_all x2 -> x0, waiting for transfers between devices: 13.8 us -> none  [the longest x1 7.86 us: shards(): lax.all_to_all(latent, ('tm', 'chan'), split_axis=0, concat_axis=0, tiled...]
    all_to_all x2 -> x0, starting transfers between devices: 8.48 us -> none  [the longest x1 5.09 us: shards(): lax.all_to_all(message, PART, split_axis=0, concat_axis=0, tiled=True)]
    pallas_call x5 -> x7, Pallas kernels: 10.3 us -> 6.47 us  [whole_call(): pl.pallas_call(kernel, out_shape=out_shape, in_specs=specs or [VMEM] * le...]
    ppermute x2, starting transfers between devices: 3.08 us -> 0.57 us  [the longest x1 0.52 us: shards(): other = lax.ppermute(both, 'chan', turn)]
    slice x5 -> x1, local copies, waits for them, and re-layouts: 1.58 us -> 0.01 us  [shards(): later = arrived[:, 1, :capacity]]
    add x0 -> x1, other arithmetic: none -> 0.64 us  [shards(): later + sooner]
    ppermute x2 -> x4, waiting for transfers between devices: 2.19 us -> 1.77 us  [slab_swap(): return lax.ppermute(value, PART, flat_pairs(sizes, pairs))]
  transfers between devices with their start and end apart: 7 -> 7, of which waited for: 4 -> 2; matrix products, arithmetic and copies ran while one was open for 2% -> 0% of each run, Pallas kernels for 8% -> 9%
where the time goes in v3:
time: 39.6 us; the launch traced here: 39.4 us
  blocking collectives  21 us (53%)
  starting transfers between devices  7.45 us (19%)
  Pallas kernels  6.47 us (16%)
  local copies, waits for them, and re-layouts  1.89 us (5%)
  waiting for transfers between devices  1.78 us (4%)
  other arithmetic  0.65 us (2%)
    all_to_all x1, blocking collectives, shards(): lax.all_to_all(latent, ('tm', 'chan'), split_axis=0, concat_axis=0, tiled...  10.7 us
    all_to_all x1, blocking collectives, shards(): lax.all_to_all(message, PART, split_axis=0, concat_axis=0, tiled=True)  10.3 us
    pallas_call x7, Pallas kernels, whole_call(): pl.pallas_call(kernel, out_shape=out_shape, in_specs=specs or [VMEM] * le...  6.47 us
    ppermute x4, starting transfers between devices, slab_swap(): return lax.ppermute(value, PART, flat_pairs(sizes, pairs))  4.31 us
    ppermute x1, starting transfers between devices, space_swap(): return lax.ppermute(value, PART, flat_pairs(sizes, pairs))  2.56 us
    unnamed x13, local copies, waits for them, and re-layouts  1.88 us
    ppermute x4, waiting for transfers between devices, slab_swap(): return lax.ppermute(value, PART, flat_pairs(sizes, pairs))  1.77 us
  transfers between devices with their start and end apart: 7, of which 2 were waited for; matrix products, arithmetic and copies ran while one was open for 0% of the time, Pallas kernels for 9%

profile of v3, /device:TPU:0, one launch (start us, length us, event | category | flops | bytes accessed | tf_op | source)
XLA Modules:
  0.0 39.4 jit_solution(1566200514892151522)
XLA Ops:
  0.0 1.2 %copy.10 = bf16[64,2,8,256]{3,0,2,1:T(8,128)(2,1)S(1)} copy(bf16[64,2,8,256]{3,2,1,0:T(8,128)(2,1)} %param.7) | data formatting | bytes 1048576 | tf_op args[0]
  1.2 0.0 copy-start
  1.2 0.2 shard_map.73
  1.4 0.0 copy-start.5
  1.4 0.3 shard_map.74
  1.7 0.5 %collective-permute-start = (bf16[1024,256]{1,0:T(8,128)(2,1)S(1)}, bf16[1024,256]{1,0:T(8,128)(2,1)S(1)}, u32[]{:S(2)}, u32[]{:S(2)}) collective-permute-start(bf16[1024,256]{1,0:T(8,128)(2,1)S(1)} %get-tuple-element.25._), channel_id=1, source_target_pairs={{0,1},{1,0},{2,3},{3,2},{4,5},{5,4},{6,7},{7,6},{8,9},{9,8},{10,11... | collective-permute-start | bytes 1572872 | tf_op jit(solution)/shard_map/ppermute | solution.py:456
  2.2 2.6 %collective-permute-start.1 = (bf16[128,256]{1,0:T(8,128)(2,1)S(1)}, bf16[128,256]{1,0:T(8,128)(2,1)S(1)}, u32[]{:S(2)}, u32[]{:S(2)}) collective-permute-start(bf16[128,256]{1,0:T(8,128)(2,1)S(1)} %get-tuple-element.32), channel_id=1, source_target_pairs={{0,2},{2,0},{1,3},{3,1},{4,6},{6,4},{5,7},{7,5},{8,10},{10,8},{9,1... | collective-permute-start | bytes 196616 | tf_op jit(solution)/shard_map/ppermute | solution.py:36
  4.8 0.2 collective-permute-start.3
  5.0 2.5 %collective-permute-start.4 = (bf16[512,256]{1,0:T(8,128)(2,1)S(1)}, bf16[512,256]{1,0:T(8,128)(2,1)S(1)}, u32[]{:S(2)}, u32[]{:S(2)}) collective-permute-start(bf16[512,256]{1,0:T(8,128)(2,1)S(1)} %get-tuple-element.30.refs_2_.refs_5_), channel_id=1, source_target_pairs={{0,5},{5,0},{4,9},{9,4},{8,13},{13,8},{1,3},{12,14},{2,7},{7,2},{6... | collective-permute-start | bytes 786440 | tf_op jit(solution)/shard_map/ppermute | solution.py:53
  7.5 0.6 %copy-done.2 = s32[2]{0:T(128)S(1)} copy-done((s32[2]{0:T(128)S(1)}, s32[2]{0:T(128)}, u32[]{:S(2)}) %copy-start.2) | copy-done | bytes 32
  8.1 0.0 copy-done.3
  8.1 0.0 copy-done.4
  8.1 1.1 %shard_map.75 = (bf16[384,768]{1,0:T(8,128)(2,1)S(1)}, bf16[2,384,384]{2,1,0:T(8,128)(2,1)S(1)}, bf16[384,384]{1,0:T(8,128)(2,1)S(1)}, f32[8,128]{1,0:T(8,128)S(1)}, bf16[32,512]{1,0:T(8,128)(2,1)S(1)}) custom-call(s32[1,2]{1,0:T(1,128)S(1)} %bitcast.20, s32[1,8]{1,0:T(1,128)S(1)} %bitcast.21, f32[1,128]{1,0:T(1,128)S(1)} %bitcast.22, ...), custom_call_target="tpu_custom_call" | custom-call | flops 1200000000 | bytes 3000000 | tf_op jit(solution)/shard_map/pallas_call | solution.py:57
  9.2 0.2 shard_map.76
  9.4 0.0 collective-permute-start.2
  9.5 1.7 %collective-permute-start.6 = (bf16[80,256]{1,0:T(8,128)(2,1)S(1)}, bf16[80,256]{1,0:T(8,128)(2,1)S(1)}, u32[]{:S(2)}, u32[]{:S(2)}) collective-permute-start(bf16[80,256]{1,0:T(8,128)(2,1)S(1)} %get-tuple-element.36.refs_4_), channel_id=1, source_target_pairs={{0,5},{5,0},{4,9},{9,4},{8,13},{13,8},{1,3},{12,14},{2,7},{7,2},{6... | collective-permute-start | bytes 122888 | tf_op jit(solution)/shard_map/ppermute | solution.py:53
  11.1 2.2 %shard_map.77 = (f32[8,128,256]{2,1,0:T(8,128)S(1)}, bf16[4,128,256]{2,1,0:T(8,128)(2,1)S(1)}, f32[8,128]{1,0:T(8,128)S(1)}) custom-call(bf16[384,768]{1,0:T(8,128)(2,1)S(1)} %get-tuple-element.28.refs_0_, bf16[384,384]{1,0:T(8,128)(2,1)S(1)} %get-tuple-element.29.refs_1_, bf16[512,256]{1,0:T(8,128)(2,1)S(1)} %get-tuple-element.30.refs_2_.refs_5_, ...), custom_call_target="tpu_custom_call" | custom-call | flops 1800000000 | bytes 4500000 | tf_op jit(solution)/shard_map/pallas_call | solution.py:57
  13.4 1.1 %collective-permute-done.6.refs_13_ = bf16[80,256]{1,0:T(8,128)(2,1)S(1)} collective-permute-done((bf16[80,256]{1,0:T(8,128)(2,1)S(1)}, bf16[80,256]{1,0:T(8,128)(2,1)S(1)}, u32[]{:S(2)}, u32[]{:S(2)}) %collective-permute-start.6) | collective-permute-done | bytes 40992 | tf_op jit(solution)/shard_map/ppermute | solution.py:53
  14.4 0.7 %collective-permute-done.5.refs_12_ = bf16[80,256]{1,0:T(8,128)(2,1)S(1)} collective-permute-done((bf16[80,256]{1,0:T(8,128)(2,1)S(1)}, bf16[80,256]{1,0:T(8,128)(2,1)S(1)}, u32[]{:S(2)}, u32[]{:S(2)}) %collective-permute-start.5) | collective-permute-done | bytes 40992 | tf_op jit(solution)/shard_map/ppermute | solution.py:53
  15.1 1.3 %shard_map.78 = (bf16[8,128,256]{2,1,0:T(8,128)(2,1)S(1)}, f32[16,8,128]{2,1,0:T(8,128)S(1)}, f32[8,128]{1,0:T(8,128)S(1)}) custom-call(f32[8,128]{1,0:T(8,128)S(1)} %get-tuple-element.26.refs_0_.refs_3_, bf16[2,384,384]{2,1,0:T(8,128)(2,1)S(1)} %get-tuple-element.27.refs_1_, f32[8,128,256]{2,1,0:T(8,128)S(1)} %get-tuple-element.34.refs_2_, ...), custom_call_target="tpu_custom_call" | custom-call | flops 1500000000 | bytes 3750000 | tf_op jit(solution)/shard_map/pallas_call | solution.py:57
  16.5 10.3 %all_to_all.10.refs_2_ = f32[16,8,128]{2,1,0:T(8,128)S(1)} all-to-all(f32[16,8,128]{2,1,0:T(8,128)S(1)} %get-tuple-element.38.refs_0_), channel_id=1, replica_groups=mesh['groups'=2,'tm'=4,'space'=2,'chan'=2] {'tm','space','chan'}, dimensions={0} | all-to-all | bytes 131072 | tf_op jit(solution)/shard_map/all_to_all | solution.py:516
  26.7 1.2 %shard_map.79 = bf16[8,6,16,128]{3,2,1,0:T(8,128)(2,1)S(1)} custom-call(f32[16,8,128]{2,1,0:T(8,128)S(1)} %get-tuple-element.38.refs_0_, f32[8,128]{1,0:T(8,128)S(1)} %get-tuple-element.39.refs_1_, f32[16,8,128]{2,1,0:T(8,128)S(1)} %all_to_all.10.refs_2_, f32[8,128]{1,0:T(8,128)S(1)} %get-tuple-element.26.refs_0_.refs_3_, ...), custom_call_target="tpu_custom_call" | custom-call | tf_op jit(solution)/shard_map/pallas_call | solution.py:57
  28.0 10.7 %all_to_all.11 = bf16[8,6,16,128]{3,2,1,0:T(8,128)(2,1)S(1)} all-to-all(bf16[8,6,16,128]{3,2,1,0:T(8,128)(2,1)S(1)} %shard_map.79), channel_id=1, replica_groups=mesh['groups'=2,'tm'=4,'space'=2,'chan'=2] {'tm','chan'}, dimensions={0} | all-to-all | bytes 393216 | tf_op jit(solution)/shard_map/all_to_all | solution.py:523
  38.7 0.6 %bitcast_add_fusion = bf16[1,16,16,128]{3,2,1,0:T(8,128)(2,1)} fusion(bf16[1,16,16,128]{3,2,1,0:T(8,128)(2,1)S(1)} %bitcast.27, bf16[1,16,16,128]{3,2,1,0:T(8,128)(2,1)S(1)} %bitcast.28), kind=kLoop, calls=%fused_computation.4 | loop fusion | flops 32768 | bytes 196608 | tf_op jit(solution)/shard_map/add | solution.py:528
  (17 shorter events, 0.0 us)
Async XLA Ops:
  1.2 6.2 %copy-start = (bf16[3,3,3,128,128]{4,3,2,1,0:T(8,128)(2,1)S(1)}, bf16[3,3,3,128,128]{4,3,2,1,0:T(8,128)(2,1)}, u32[]{:S(2)}) copy-start(bf16[3,3,3,128,128]{4,3,2,1,0:T(8,128)(2,1)} %weight_ref.1) | copy-start | bytes 2654212
  1.4 6.1 %copy-start.1 = (bf16[2,2,128,32]{2,3,1,0:T(8,128)(2,1)S(1)}, bf16[2,2,128,32]{2,3,1,0:T(8,128)(2,1)}, u32[]{:S(2)}) copy-start(bf16[2,2,128,32]{2,3,1,0:T(8,128)(2,1)} %param.12) | copy-start | bytes 98308
  1.4 6.1 %copy-start.5 = (f32[128]{0:T(128)S(1)}, f32[128]{0:T(128)}, u32[]{:S(2)}) copy-start(f32[128]{0:T(128)} %param.11) | copy-start | bytes 1540
  1.7 9.4 %collective-permute-start = (bf16[1024,256]{1,0:T(8,128)(2,1)S(1)}, bf16[1024,256]{1,0:T(8,128)(2,1)S(1)}, u32[]{:S(2)}, u32[]{:S(2)}) collective-permute-start(bf16[1024,256]{1,0:T(8,128)(2,1)S(1)} %get-tuple-element.25._), channel_id=1, source_target_pairs={{0,1},{1,0},{2,3},{3,2},{4,5},{5,4},{6,7},{7,6},{8,9},{9,8},{10,11... | collective-permute-start | bytes 1572872 | tf_op jit(solution)/shard_map/ppermute | solution.py:456
  2.2 7.0 %collective-permute-start.1 = (bf16[128,256]{1,0:T(8,128)(2,1)S(1)}, bf16[128,256]{1,0:T(8,128)(2,1)S(1)}, u32[]{:S(2)}, u32[]{:S(2)}) collective-permute-start(bf16[128,256]{1,0:T(8,128)(2,1)S(1)} %get-tuple-element.32), channel_id=1, source_target_pairs={{0,2},{2,0},{1,3},{3,1},{4,6},{6,4},{5,7},{7,5},{8,10},{10,8},{9,1... | collective-permute-start | bytes 196616 | tf_op jit(solution)/shard_map/ppermute | solution.py:36
  4.8 10.3 %collective-permute-start.3 = (bf16[512,256]{1,0:T(8,128)(2,1)S(1)}, bf16[512,256]{1,0:T(8,128)(2,1)S(1)}, u32[]{:S(2)}, u32[]{:S(2)}) collective-permute-start(bf16[512,256]{1,0:T(8,128)(2,1)S(1)} %get-tuple-element.31.refs_3_.refs_6_), channel_id=1, source_target_pairs={{1,5},{4,0},{5,9},{8,4},{9,13},{12,8},{13,12},{0,1},{3,7},{6,2},{7... | collective-permute-start | bytes 786440 | tf_op jit(solution)/shard_map/ppermute | solution.py:53
  5.0 10.2 %collective-permute-start.4 = (bf16[512,256]{1,0:T(8,128)(2,1)S(1)}, bf16[512,256]{1,0:T(8,128)(2,1)S(1)}, u32[]{:S(2)}, u32[]{:S(2)}) collective-permute-start(bf16[512,256]{1,0:T(8,128)(2,1)S(1)} %get-tuple-element.30.refs_2_.refs_5_), channel_id=1, source_target_pairs={{0,5},{5,0},{4,9},{9,4},{8,13},{13,8},{1,3},{12,14},{2,7},{7,2},{6... | collective-permute-start | bytes 786440 | tf_op jit(solution)/shard_map/ppermute | solution.py:53
  7.4 0.7 %copy-start.2 = (s32[2]{0:T(128)S(1)}, s32[2]{0:T(128)}, u32[]{:S(2)}) copy-start(s32[2]{0:T(128)} %param.8) | copy-start | bytes 28
  7.4 0.7 %copy-start.3 = (s32[1,8,1]{1,2,0:T(1,128)S(1)}, s32[1,8,1]{1,2,0:T(1,128)}, u32[]{:S(2)}) copy-start(s32[1,8,1]{1,2,0:T(1,128)} %param.13) | copy-start | bytes 100
  7.4 0.7 %copy-start.4 = (f32[128]{0:T(128)S(1)}, f32[128]{0:T(128)}, u32[]{:S(2)}) copy-start(f32[128]{0:T(128)} %param.10) | copy-start | bytes 1540
  9.4 1.7 %collective-permute-start.2 = (bf16[128,256]{1,0:T(8,128)(2,1)S(1)}, bf16[128,256]{1,0:T(8,128)(2,1)S(1)}, u32[]{:S(2)}, u32[]{:S(2)}) collective-permute-start(bf16[128,256]{1,0:T(8,128)(2,1)S(1)} %get-tuple-element.33.refs_5_.refs_8_), channel_id=1, source_target_pairs={{0,1},{1,0},{2,3},{3,2},{4,5},{5,4},{6,7},{7,6},{8,9},{9,8},{10,11... | collective-permute-start | bytes 196616 | tf_op jit(solution)/shard_map/ppermute | solution.py:488
  9.5 5.0 %collective-permute-start.6 = (bf16[80,256]{1,0:T(8,128)(2,1)S(1)}, bf16[80,256]{1,0:T(8,128)(2,1)S(1)}, u32[]{:S(2)}, u32[]{:S(2)}) collective-permute-start(bf16[80,256]{1,0:T(8,128)(2,1)S(1)} %get-tuple-element.36.refs_4_), channel_id=1, source_target_pairs={{0,5},{5,0},{4,9},{9,4},{8,13},{13,8},{1,3},{12,14},{2,7},{7,2},{6... | collective-permute-start | bytes 122888 | tf_op jit(solution)/shard_map/ppermute | solution.py:53
  11.1 4.0 %collective-permute-start.5 = (bf16[80,256]{1,0:T(8,128)(2,1)S(1)}, bf16[80,256]{1,0:T(8,128)(2,1)S(1)}, u32[]{:S(2)}, u32[]{:S(2)}) collective-permute-start(bf16[80,256]{1,0:T(8,128)(2,1)S(1)} %get-tuple-element.37), channel_id=1, source_target_pairs={{1,5},{4,0},{5,9},{8,4},{9,13},{12,8},{13,12},{0,1},{3,7},{6,2},{7... | collective-permute-start | bytes 122888 | tf_op jit(solution)/shard_map/ppermute | solution.py:53

commit v4 on v3

--- a/solution.py
+++ b/solution.py
@@ -11,6 +11,7 @@
 MOMENTS = 32
 SEND_ROWS = 8
 ID_ROWS = 16
+BLOCK = 16
 BF16 = jnp.bfloat16
 F32 = jnp.float32
 VMEM = pl.BlockSpec(memory_space=pltpu.VMEM)
@@ -61,7 +62,7 @@
         out_specs=jax.tree.map(lambda _: VMEM, out_shape),
         scratch_shapes=scratch,
         compiler_params=PARAMS,
-        cost_estimate=pl.CostEstimate(flops=flops, bytes_accessed=flops // 400, transcendentals=0),
+        cost_estimate=None if flops is None else pl.CostEstimate(flops=flops, bytes_accessed=flops // 400, transcendentals=0),
     )(*args)
 
 
@@ -70,30 +71,39 @@
     return jnp.sum(jnp.where(lane == n, small_ref[2:3, :], 0.0))
 
 
-def edge_kernel(frames_ref, split_ref, *edge_refs):
+def front_kernel(rows, pixels_ref, cross_ref, same_ref, both_ref, *edge_refs):
     chan = lax.axis_index("chan")
     odd = lax.axis_index("space") % 2 == 1
-    _, rows, half, columns = frames_ref.shape
+    half, columns = CHANNELS // 2, pixels_ref.shape[1]
+    size = 2 * rows * BLOCK
     source = lax.broadcasted_iota(jnp.int32, (columns, columns), 0)
     target = lax.broadcasted_iota(jnp.int32, (1, columns), 1)
     wanted = jnp.where(target < columns // 2, 2 * target, 2 * target - columns + 1)
-    split_ref[...] = jnp.where(source == wanted, 1.0, 0.0).astype(BF16)
-    for h, edge_ref in enumerate(edge_refs):
-        to_low = odd if h == 0 else jnp.logical_not(odd)
-        line = jnp.where(to_low, 0, rows - 1)
-        image = jnp.concatenate([frames_ref[1 - chan, line], frames_ref[chan, line]], axis=0)
-        edge_ref[...] = jnp.dot(image, split_ref[...], preferred_element_type=F32).astype(BF16)
-
-
-def interior_kernel(frames_ref, split_ref, cross_ref, same_ref, both_ref):
-    chan = lax.axis_index("chan")
-    _, rows, half, columns = frames_ref.shape
+    split = jnp.where(source == wanted, 1.0, 0.0).astype(BF16)
+    placed = lax.broadcasted_iota(jnp.int32, (size, size), 1)
+    line = lax.broadcasted_iota(jnp.int32, (size, 1), 0)
+    second = line // (rows * BLOCK)
+    frame = jnp.where(second == 0, 1 - chan, chan)
+    row = line // BLOCK % rows
+    origin = line % BLOCK * (2 * rows) + frame * rows + row
+    turn = jnp.where(placed == origin, 1.0, 0.0).astype(BF16)
     inside = rows * half
-    for out_ref, frame, n in ((cross_ref, 1 - chan, 0), (same_ref, chan, 1)):
-        image = frames_ref[frame].reshape(inside, columns)
-        value = jnp.dot(image, split_ref[...], preferred_element_type=F32).astype(BF16)
-        out_ref[...] = value
-        both_ref[n * inside : (n + 1) * inside, :] = value
+    for n in range(half // BLOCK):
+        image = pixels_ref[n * size : (n + 1) * size, :]
+        image = jnp.dot(turn, image, preferred_element_type=F32).astype(BF16)
+        image = jnp.dot(image, split, preferred_element_type=F32).astype(BF16)
+        for f, out_ref in enumerate((cross_ref, same_ref)):
+            for r in range(rows):
+                first = (f * rows + r) * BLOCK
+                block = image[first : first + BLOCK, :]
+                first = r * half + n * BLOCK
+                out_ref[first : first + BLOCK, :] = block
+                both_ref[f * inside + first : f * inside + first + BLOCK, :] = block
+    for f, out_ref in enumerate((cross_ref, same_ref)):
+        low, high = out_ref[:half, :], out_ref[(rows - 1) * half :, :]
+        for h, edge_ref in enumerate(edge_refs):
+            to_low = odd if h == 0 else jnp.logical_not(odd)
+            edge_ref[f * half : (f + 1) * half, :] = jnp.where(to_low, low, high)
 
 
 def halo_kernel(halos, capacity, small_ref, *refs):
@@ -341,7 +351,7 @@
 
 
 def norm_kernel(
-    count, capacity, message_ref, keys_ref, gathered_ref, small_ref, out_matrix_ref, conv_ref, extra_ref, latent_ref
+    count, message_ref, keys_ref, gathered_ref, small_ref, out_matrix_ref, conv_ref, extra_ref, mine_ref, theirs_ref
 ):
     rows, _, columns = conv_ref.shape
     half = columns // 2
@@ -373,7 +383,7 @@
         var = totals[first + 1 : first + 2, :] / counts - mean * mean
         scale = lax.rsqrt(var + 1e-06) * small_ref[0:1, :]
         offset = small_ref[1:2, :] - mean * scale
-        return [jnp.broadcast_to(value, (CHANNELS, CHANNELS)).T for value in (scale, offset)]
+        return [jnp.broadcast_to(0.5 * value, (CHANNELS, CHANNELS)).T for value in (scale, offset)]
 
     def project(source_ref, scale, offset):
         images = []
@@ -383,47 +393,90 @@
                 for j in range(2):
                     value = source_ref[2 * r + i, :, j * half : (j + 1) * half].astype(F32)
                     value = value * scale + offset
-                    pieces.append((value / (1.0 + jnp.exp(-value))).astype(BF16))
+                    pieces.append((value + value * jnp.tanh(value)).astype(BF16))
             images.append(jnp.concatenate(pieces, axis=0))
         image = jnp.concatenate(images, axis=1)
         return jnp.dot(out_matrix_ref[...], image, preferred_element_type=F32)
 
-    slots, places, chans = latent_ref.shape[1], latent_ref.shape[0] // 2, 2
-    part = MOMENTS // chans
-
-    def place(latent, first_key, wanted, slot):
-        for c in range(chans):
-            blocks = [
-                latent[c * part : (c + 1) * part, r * half : (r + 1) * half] for r in range(latent.shape[1] // half)
-            ]
-            for t in range(places):
-                for j in range(wanted):
-                    value = jnp.zeros((part, half), F32)
-                    for n, block in enumerate(blocks):
-                        key = keys_ref[first_key + n : first_key + n + 1, :]
-                        value = jnp.where(key == float(t * capacity + j + 1), block, value)
-                    yield t * chans + c, slot + j, value
-
+    chan = lax.axis_index("chan")
     kept = rows // 2
-    for p, j, value in place(project(conv_ref, *factors(0)), 0, capacity, 0):
-        latent_ref[p, j] = value.astype(BF16)
-    for p in range(latent_ref.shape[0]):
-        for j in range(capacity, slots):
-            latent_ref[p, j] = jnp.zeros((part, half), BF16)
+    part = MOMENTS // 2
+
+    def store(latent, first):
+        for n in range(latent.shape[1] // half):
+            blocks = [latent[c * part : (c + 1) * part, n * half : (n + 1) * half].astype(BF16) for c in range(2)]
+            mine_ref[first + n] = jnp.where(chan == 0, blocks[0], blocks[1])
+            theirs_ref[first + n] = jnp.where(chan == 0, blocks[1], blocks[0])
+
+    store(project(conv_ref, *factors(0)), 0)
+    theirs_ref[kept + kept // 2] = jnp.concatenate([keys_ref[...]] * 2, axis=0).astype(BF16)
 
     @pl.when(lax.axis_index("tm") == 0)
     def _():
-        latent = project(extra_ref, *factors(3))
-
-        @pl.when(lax.axis_index("chan") == 0)
+        store(project(extra_ref, *factors(3)), kept)
+
+    @pl.when(lax.axis_index("tm") > 0)
+    def _():
+        for n in range(kept // 2):
+            mine_ref[kept + n] = jnp.zeros((part, half), BF16)
+            theirs_ref[kept + n] = jnp.zeros((part, half), BF16)
+
+
+def crossed(slabs):
+    return slabs in (2, 4)
+
+
+def place_kernel(slabs, capacity, kept, keys_ref, mine_ref, other_ref, *send_refs):
+    slab = lax.axis_index("tm")
+    second = lax.axis_index("chan") == 1
+    count = kept + kept // 2
+    other_keys = other_ref[count].astype(F32)
+    rows = []
+    for n in range(count):
+        mine = (keys_ref[n : n + 1, :], mine_ref[n].astype(F32))
+        other = (other_keys[n : n + 1, :], other_ref[n].astype(F32))
+        if n < kept:
+            picked = [[jnp.where(second, x, y) for x, y in pair] for pair in (zip(mine, other), zip(other, mine))]
+            rows.append(((picked[0],), picked[1]))
+        else:
+            rows.append(((mine, other), None))
+    now = [row for group, _ in rows for row in group]
+    following = [row for _, row in rows if row is not None]
+    for d in range(slabs):
+        owner = (slab ^ d if crossed(slabs) else jnp.int32(d)).astype(F32)
+        for j in range(capacity):
+            wanted = owner * float(capacity) + float(j + 1)
+            for first, group in ((0, now), (capacity, following)):
+                value = jnp.zeros(mine_ref.shape[1:], F32)
+                for key, block in group:
+                    value = jnp.where(key == wanted, block, value)
+                if crossed(slabs):
+                    send_refs[d][first + j] = value.astype(BF16)
+                else:
+                    send_refs[0][d, first + j] = value.astype(BF16)
+
+
+def merge_kernel(slabs, capacity, *refs):
+    sources, owned_ref = refs[:-1], refs[-1]
+    slab = lax.axis_index("tm")
+
+    def source(d):
+        if crossed(slabs):
+            return slab ^ d, sources[d]
+        return d, sources[0].at[d]
+
+    for d in range(slabs):
+        block, ref = source(d)
+        for j in range(capacity):
+            owned_ref[block * capacity + j] = ref[j]
+    for d in range(slabs):
+        block, ref = source(d)
+
+        @pl.when(block + 1 < slabs)
         def _():
-            for p, j, value in place(latent, kept, slots - capacity, capacity):
-                latent_ref[p, j] = value.astype(BF16)
-
-        @pl.when(lax.axis_index("chan") == 1)
-        def _():
-            for p, j, value in place(latent, kept, capacity, 0):
-                latent_ref[p, j] = (latent_ref[p, j].astype(F32) + value).astype(BF16)
+            for j in range(capacity):
+                n = (block + 1) * capacity + j
+                owned_ref[n] = (owned_ref[n].astype(F32) + ref[capacity + j].astype(F32)).astype(BF16)
 
 
 def shards(activations, frame_clip, conv_weight, norm_gain, norm_bias, out_weight, owner):
@@ -439,21 +492,16 @@
     assert send_rows == SEND_ROWS
     payload = jax.ShapeDtypeStruct((rows * half, columns), BF16)
     pair = jax.ShapeDtypeStruct((2 * half, columns), BF16)
-    planes = activations.transpose(1, 2, 0, 3)
-    split, *edges = whole_call(
-        edge_kernel, (jax.ShapeDtypeStruct((columns, columns), BF16),) + (pair,) * halos, (planes,)
+    cross, same, both, *edges = whole_call(
+        lambda *refs: front_kernel(rows, *refs),
+        (payload, payload, jax.ShapeDtypeStruct((2 * rows * half, columns), BF16)) + (pair,) * halos,
+        (activations.reshape(half * frames * rows, columns),),
+        flops=300000000,
     )
     own_halos = [space_swap(edge, sizes, start) for start, edge in enumerate(edges)]
-    cross, same, both = whole_call(
-        interior_kernel,
-        (payload, payload, jax.ShapeDtypeStruct((2 * rows * half, columns), BF16)),
-        (planes, split),
-        flops=300_000_000,
-    )
     late_own = slab_swap(same, sizes, False)
     late_other = slab_swap(cross, sizes, True)
     turn = [(0, 1), (1, 0)]
-    other = lax.ppermute(both, "chan", turn)
     local_weight, late_weight, sum_weight, small, out_matrix = whole_call(
         weights_kernel,
         (
@@ -477,8 +525,9 @@
             pltpu.SemaphoreType.DMA((5,)),
         ],
         [pl.BlockSpec(memory_space=pl.ANY)] * 5 + [VMEM] * 2,
-        1_200_000_000,
-    )
+        1200000000,
+    )
+    other = lax.ppermute(both, "chan", turn)
     message_halo = jax.ShapeDtypeStruct((halos * half + ID_ROWS, columns), BF16)
     *own_halos, cross_halo, same_halo = whole_call(
         lambda *refs: halo_kernel(halos, capacity, *refs),
@@ -498,7 +547,7 @@
         ),
         (local_weight, sum_weight, *here),
         [pltpu.VMEM((rows // 2 + 2, CHANNELS, columns), BF16)],
-        flops=1_800_000_000,
+        flops=1800000000,
     )
     conv, message, keys = whole_call(
         lambda *refs: late_kernel(rows, halos, slabs, *refs),
@@ -511,21 +560,44 @@
             small, late_weight, part, extra_sums, cross_halo, *here, late_own, late_other, late_own_halo, late_other_halo,
         ),
         [pltpu.VMEM((rows + 2, CHANNELS, columns), BF16)],
-        flops=1_500_000_000,
+        flops=1500000000,
     )
     gathered = lax.all_to_all(message, PART, split_axis=0, concat_axis=0, tiled=True)
-    slots = capacity + kept // 2
-    latent = whole_call(
-        lambda *refs: norm_kernel(rows * columns, capacity, *refs),
-        jax.ShapeDtypeStruct((slabs * chans, slots, MOMENTS // chans, columns // 2), BF16),
+    part = MOMENTS // chans
+    width = columns // 2
+    count = kept + kept // 2
+    mine, theirs = whole_call(
+        lambda *refs: norm_kernel(rows * columns, *refs),
+        (
+            jax.ShapeDtypeStruct((count, part, width), BF16),
+            jax.ShapeDtypeStruct((count + 1, part, width), BF16),
+        ),
         (message, keys, gathered, small, out_matrix, conv, extra),
     )
-    arrived = lax.all_to_all(latent, ("tm", "chan"), split_axis=0, concat_axis=0, tiled=True)
-    arrived = arrived.reshape((slabs, chans) + arrived.shape[1:])
-    later = arrived[:, 1, :capacity]
-    begin = jnp.pad(arrived[:1, 0, capacity:], ((0, 0), (0, 2 * capacity - slots), (0, 0), (0, 0)))
-    sooner = jnp.concatenate([begin, arrived[:-1, 0, :capacity]])
-    return (later + sooner).reshape(1, slabs * capacity, MOMENTS // chans, columns // 2)
+    from_other = lax.ppermute(theirs, "chan", turn)
+    blocks = (2 * capacity, part, width)
+    if crossed(slabs):
+        shapes = (jax.ShapeDtypeStruct(blocks, BF16),) * slabs
+    else:
+        shapes = (jax.ShapeDtypeStruct((slabs,) + blocks, BF16),)
+    sends = whole_call(
+        lambda *refs: place_kernel(slabs, capacity, kept, *refs), shapes, (keys, mine, from_other)
+    )
+    if crossed(slabs):
+        received = [sends[0]]
+        for d in range(1, slabs):
+            received.append(lax.ppermute(sends[d], "tm", [(t, t ^ d) for t in range(slabs)]))
+    else:
+        received = [lax.all_to_all(sends[0], "tm", split_axis=0, concat_axis=0, tiled=True)]
+    turns = list((0, 3, 1, 2)) if crossed(slabs) else [0]
+    owned = pl.pallas_call(
+        lambda *refs: merge_kernel(slabs, capacity, *[refs[turns.index(d)] for d in range(len(turns))], refs[-1]),
+        out_shape=jax.ShapeDtypeStruct((slabs * capacity, part, width), BF16),
+        in_specs=[VMEM] * len(received),
+        out_specs=pl.BlockSpec((slabs * capacity, part, width), lambda: (0, 0, 0)),
+        compiler_params=PARAMS,
+    )(*[received[d] for d in turns])
+    return owned[None]
 
 
 def solution(mesh):

time: 39.6 us -> 36.3 us (0.917)
  blocking collectives: 21 us -> 10.3 us
  waiting for transfers between devices: 1.78 us -> 5.65 us
  starting transfers between devices: 7.45 us -> 11.1 us
  Pallas kernels: 6.47 us -> 7.2 us
  other arithmetic: 0.65 us -> 0 us
    all_to_all x1 -> x0, blocking collectives: 10.7 us -> none  [shards(): lax.all_to_all(latent, ('tm', 'chan'), split_axis=0, concat_axis=0, tiled...]
    ppermute x0 -> x4, waiting for transfers between devices: none -> 3.87 us  [the longest x3 2.68 us: shards(): lax.ppermute(sends[d], 'tm', [(t, t ^ d) for t in range(slabs)])]
    ppermute x0 -> x4, starting transfers between devices: none -> 3.62 us  [the longest x3 3.55 us: shards(): lax.ppermute(sends[d], 'tm', [(t, t ^ d) for t in range(slabs)])]
    pallas_call x0 -> x1, Pallas kernels: none -> 0.66 us  [shards(): pl.pallas_call(lambda *refs: merge_kernel(slabs, capacity, *[refs[turns.i...]
    add x1 -> x0, other arithmetic: 0.64 us -> none  [shards(): later + sooner]
    unnamed x13 -> x14, local copies, waits for them, and re-layouts: 1.88 us -> 1.79 us
  transfers between devices with their start and end apart: 7 -> 11, of which waited for: 2 -> 6; matrix products, arithmetic and copies ran while one was open for 0% -> 0% of each run, Pallas kernels for 9% -> 10%
where the time goes in v4:
time: 36.3 us; the launch traced here: 36.1 us
  starting transfers between devices  11.1 us (31%)
  blocking collectives  10.3 us (28%)
  Pallas kernels  7.2 us (20%)
  waiting for transfers between devices  5.65 us (16%)
  local copies, waits for them, and re-layouts  1.79 us (5%)
    all_to_all x1, blocking collectives, shards(): lax.all_to_all(message, PART, split_axis=0, concat_axis=0, tiled=True)  10.3 us
    pallas_call x7, Pallas kernels, whole_call(): pl.pallas_call(kernel, out_shape=out_shape, in_specs=specs or [VMEM] * le...  6.53 us
    ppermute x4, starting transfers between devices, slab_swap(): return lax.ppermute(value, PART, flat_pairs(sizes, pairs))  4.32 us
    ppermute x3, starting transfers between devices, shards(): lax.ppermute(sends[d], 'tm', [(t, t ^ d) for t in range(slabs)])  3.55 us
    ppermute x3, waiting for transfers between devices, shards(): lax.ppermute(sends[d], 'tm', [(t, t ^ d) for t in range(slabs)])  2.68 us
    ppermute x1, starting transfers between devices, space_swap(): return lax.ppermute(value, PART, flat_pairs(sizes, pairs))  2.56 us
    unnamed x14, local copies, waits for them, and re-layouts  1.79 us
    ppermute x4, waiting for transfers between devices, slab_swap(): return lax.ppermute(value, PART, flat_pairs(sizes, pairs))  1.77 us
  transfers between devices with their start and end apart: 11, of which 6 were waited for; matrix products, arithmetic and copies ran while one was open for 0% of the time, Pallas kernels for 10%

profile of v4, /device:TPU:0, one launch (start us, length us, event | category | flops | bytes accessed | tf_op | source)
XLA Modules:
  0.0 36.1 jit_solution(5896432612887362820)
XLA Ops:
  0.0 1.1 %copy-done.1 = bf16[64,2,8,256]{3,2,1,0:T(8,128)(2,1)S(1)} copy-done((bf16[64,2,8,256]{3,2,1,0:T(8,128)(2,1)S(1)}, bf16[64,2,8,256]{3,2,1,0:T(8,128)(2,1)}, u32[]{:S(2)}) %copy-start.1) | copy-done | bytes 524312
  1.1 0.5 %shard_map.73 = (bf16[512,256]{1,0:T(8,128)(2,1)S(1)}, bf16[512,256]{1,0:T(8,128)(2,1)S(1)}, bf16[1024,256]{1,0:T(8,128)(2,1)S(1)}, bf16[128,256]{1,0:T(8,128)(2,1)S(1)}) custom-call(bf16[1024,256]{1,0:T(8,128)(2,1)S(1)} %bitcast.7), custom_call_target="tpu_custom_call" | custom-call | flops 300000000 | bytes 750000 | tf_op jit(solution)/shard_map/pallas_call | solution.py:58
  1.7 0.5 %collective-permute-start = (bf16[1024,256]{1,0:T(8,128)(2,1)S(1)}, bf16[1024,256]{1,0:T(8,128)(2,1)S(1)}, u32[]{:S(2)}, u32[]{:S(2)}) collective-permute-start(bf16[1024,256]{1,0:T(8,128)(2,1)S(1)} %get-tuple-element.29._), channel_id=1, source_target_pairs={{0,1},{1,0},{2,3},{3,2},{4,5},{5,4},{6,7},{7,6},{8,9},{9,8},{10,11... | collective-permute-start | bytes 1572872 | tf_op jit(solution)/shard_map/ppermute | solution.py:530
  2.2 2.6 %collective-permute-start.1 = (bf16[128,256]{1,0:T(8,128)(2,1)S(1)}, bf16[128,256]{1,0:T(8,128)(2,1)S(1)}, u32[]{:S(2)}, u32[]{:S(2)}) collective-permute-start(bf16[128,256]{1,0:T(8,128)(2,1)S(1)} %get-tuple-element.36), channel_id=1, source_target_pairs={{0,2},{2,0},{1,3},{3,1},{4,6},{6,4},{5,7},{7,5},{8,10},{10,8},{9,1... | collective-permute-start | bytes 196616 | tf_op jit(solution)/shard_map/ppermute | solution.py:37
  4.8 0.2 collective-permute-start.3
  4.9 2.5 %collective-permute-start.4 = (bf16[512,256]{1,0:T(8,128)(2,1)S(1)}, bf16[512,256]{1,0:T(8,128)(2,1)S(1)}, u32[]{:S(2)}, u32[]{:S(2)}) collective-permute-start(bf16[512,256]{1,0:T(8,128)(2,1)S(1)} %get-tuple-element.34.refs_2_.refs_5_), channel_id=1, source_target_pairs={{0,5},{5,0},{4,9},{9,4},{8,13},{13,8},{1,3},{12,14},{2,7},{7,2},{6... | collective-permute-start | bytes 786440 | tf_op jit(solution)/shard_map/ppermute | solution.py:54
  7.4 0.6 %copy-done.3 = s32[2]{0:T(128)S(1)} copy-done((s32[2]{0:T(128)S(1)}, s32[2]{0:T(128)}, u32[]{:S(2)}) %copy-start.3) | copy-done | bytes 32
  8.1 1.1 %shard_map.74 = (bf16[384,768]{1,0:T(8,128)(2,1)S(1)}, bf16[2,384,384]{2,1,0:T(8,128)(2,1)S(1)}, bf16[384,384]{1,0:T(8,128)(2,1)S(1)}, f32[8,128]{1,0:T(8,128)S(1)}, bf16[32,512]{1,0:T(8,128)(2,1)S(1)}) custom-call(s32[1,2]{1,0:T(1,128)S(1)} %bitcast.9, s32[1,8]{1,0:T(1,128)S(1)} %bitcast.10, f32[1,128]{1,0:T(1,128)S(1)} %bitcast.11, f32[1,128]{1,0:T(1,128)S(1)} %bitcast.12, ...), custom_call_target="tpu_custom_call" | custom-call | flops 1200000000 | bytes 3000000 | tf_op jit(solution)/shard_map/pallas_call | solution.py:58
  9.2 0.2 shard_map.75
  9.4 1.7 %collective-permute-start.6 = (bf16[80,256]{1,0:T(8,128)(2,1)S(1)}, bf16[80,256]{1,0:T(8,128)(2,1)S(1)}, u32[]{:S(2)}, u32[]{:S(2)}) collective-permute-start(bf16[80,256]{1,0:T(8,128)(2,1)S(1)} %get-tuple-element.40.refs_4_), channel_id=1, source_target_pairs={{0,5},{5,0},{4,9},{9,4},{8,13},{13,8},{1,3},{12,14},{2,7},{7,2},{6... | collective-permute-start | bytes 122888 | tf_op jit(solution)/shard_map/ppermute | solution.py:54
  11.1 2.2 %shard_map.76 = (f32[8,128,256]{2,1,0:T(8,128)S(1)}, bf16[4,128,256]{2,1,0:T(8,128)(2,1)S(1)}, f32[8,128]{1,0:T(8,128)S(1)}) custom-call(bf16[384,768]{1,0:T(8,128)(2,1)S(1)} %get-tuple-element.32.refs_0_, bf16[384,384]{1,0:T(8,128)(2,1)S(1)} %get-tuple-element.33.refs_1_, bf16[512,256]{1,0:T(8,128)(2,1)S(1)} %get-tuple-element.34.refs_2_.refs_5_, ...), custom_call_target="tpu_custom_call" | custom-call | flops 1800000000 | bytes 4500000 | tf_op jit(solution)/shard_map/pallas_call | solution.py:58
  13.3 1.1 %collective-permute-done.6.refs_13_ = bf16[80,256]{1,0:T(8,128)(2,1)S(1)} collective-permute-done((bf16[80,256]{1,0:T(8,128)(2,1)S(1)}, bf16[80,256]{1,0:T(8,128)(2,1)S(1)}, u32[]{:S(2)}, u32[]{:S(2)}) %collective-permute-start.6) | collective-permute-done | bytes 40992 | tf_op jit(solution)/shard_map/ppermute | solution.py:54
  14.4 0.7 %collective-permute-done.5.refs_12_ = bf16[80,256]{1,0:T(8,128)(2,1)S(1)} collective-permute-done((bf16[80,256]{1,0:T(8,128)(2,1)S(1)}, bf16[80,256]{1,0:T(8,128)(2,1)S(1)}, u32[]{:S(2)}, u32[]{:S(2)}) %collective-permute-start.5) | collective-permute-done | bytes 40992 | tf_op jit(solution)/shard_map/ppermute | solution.py:54
  15.1 1.3 %shard_map.77 = (bf16[8,128,256]{2,1,0:T(8,128)(2,1)S(1)}, f32[16,8,128]{2,1,0:T(8,128)S(1)}, f32[8,128]{1,0:T(8,128)S(1)}) custom-call(f32[8,128]{1,0:T(8,128)S(1)} %get-tuple-element.30.refs_0_.refs_3_, bf16[2,384,384]{2,1,0:T(8,128)(2,1)S(1)} %get-tuple-element.31.refs_1_, f32[8,128,256]{2,1,0:T(8,128)S(1)} %get-tuple-element.38.refs_2_, ...), custom_call_target="tpu_custom_call" | custom-call | flops 1500000000 | bytes 3750000 | tf_op jit(solution)/shard_map/pallas_call | solution.py:58
  16.4 10.3 %all_to_all.5.refs_2_ = f32[16,8,128]{2,1,0:T(8,128)S(1)} all-to-all(f32[16,8,128]{2,1,0:T(8,128)S(1)} %get-tuple-element.43.refs_0_), channel_id=1, replica_groups=mesh['groups'=2,'tm'=4,'space'=2,'chan'=2] {'tm','space','chan'}, dimensions={0} | all-to-all | bytes 131072 | tf_op jit(solution)/shard_map/all_to_all | solution.py:565
  26.7 1.0 %shard_map.78 = (bf16[6,16,128]{2,1,0:T(8,128)(2,1)S(1)}, bf16[7,16,128]{2,1,0:T(8,128)(2,1)S(1)}) custom-call(f32[16,8,128]{2,1,0:T(8,128)S(1)} %get-tuple-element.43.refs_0_, f32[8,128]{1,0:T(8,128)S(1)} %get-tuple-element.42.refs_1_.refs_0_, f32[16,8,128]{2,1,0:T(8,128)S(1)} %all_to_all.5.refs_2_, f32[8,128]{1,0:T(8,128)S(1)} %get-tuple-element.30.refs_0_.refs_3_, ...), custom_call_target="tpu_custom_call" | custom-call | tf_op jit(solution)/shard_map/pallas_call | solution.py:58
  27.8 1.2 %collective-permute-done.7.refs_2_ = bf16[7,16,128]{2,1,0:T(8,128)(2,1)S(1)} collective-permute-done((bf16[7,16,128]{2,1,0:T(8,128)(2,1)S(1)}, bf16[7,16,128]{2,1,0:T(8,128)(2,1)S(1)}, u32[]{:S(2)}, u32[]{:S(2)}) %collective-permute-start.7) | collective-permute-done | bytes 28704 | tf_op jit(solution)/shard_map/ppermute | solution.py:577
  29.0 0.2 shard_map.79
  29.3 2.1 %collective-permute-start.8 = (bf16[8,16,128]{2,1,0:T(8,128)(2,1)S(1)}, bf16[8,16,128]{2,1,0:T(8,128)(2,1)S(1)}, u32[]{:S(2)}, u32[]{:S(2)}) collective-permute-start(bf16[8,16,128]{2,1,0:T(8,128)(2,1)S(1)} %get-tuple-element.50), channel_id=1, source_target_pairs={{0,12},{4,8},{8,4},{12,0},{1,13},{5,9},{9,5},{13,1},{2,14},{6,10},... | collective-permute-start | bytes 98312 | tf_op jit(solution)/shard_map/ppermute | solution.py:589
  31.4 1.3 %collective-permute-start.9 = (bf16[8,16,128]{2,1,0:T(8,128)(2,1)S(1)}, bf16[8,16,128]{2,1,0:T(8,128)(2,1)S(1)}, u32[]{:S(2)}, u32[]{:S(2)}) collective-permute-start(bf16[8,16,128]{2,1,0:T(8,128)(2,1)S(1)} %get-tuple-element.51), channel_id=1, source_target_pairs={{0,4},{4,0},{8,12},{12,8},{1,5},{5,1},{9,13},{13,9},{2,6},{6,2},{1... | collective-permute-start | bytes 98312 | tf_op jit(solution)/shard_map/ppermute | solution.py:589
  32.7 1.9 %collective-permute-done.10.refs_3_ = bf16[8,16,128]{2,1,0:T(8,128)(2,1)S(1)} collective-permute-done((bf16[8,16,128]{2,1,0:T(8,128)(2,1)S(1)}, bf16[8,16,128]{2,1,0:T(8,128)(2,1)S(1)}, u32[]{:S(2)}, u32[]{:S(2)}) %collective-permute-start.10) | collective-permute-done | bytes 32800 | tf_op jit(solution)/shard_map/ppermute | solution.py:589
  34.7 0.4 %collective-permute-done.8.refs_1_ = bf16[8,16,128]{2,1,0:T(8,128)(2,1)S(1)} collective-permute-done((bf16[8,16,128]{2,1,0:T(8,128)(2,1)S(1)}, bf16[8,16,128]{2,1,0:T(8,128)(2,1)S(1)}, u32[]{:S(2)}, u32[]{:S(2)}) %collective-permute-start.8) | collective-permute-done | bytes 32800 | tf_op jit(solution)/shard_map/ppermute | solution.py:589
  35.1 0.3 collective-permute-done.9.refs_2_
  35.4 0.7 %shard_map.80 = bf16[16,16,128]{2,1,0:T(8,128)(2,1)} custom-call(bf16[8,16,128]{2,1,0:T(8,128)(2,1)S(1)} %get-tuple-element.49.refs_0_, bf16[8,16,128]{2,1,0:T(8,128)(2,1)S(1)} %collective-permute-done.8.refs_1_, bf16[8,16,128]{2,1,0:T(8,128)(2,1)S(1)} %collective-permute-done.9.refs_2_, bf16[8,16,128]{2,1,0:T(8,128)(2,1)S(1)} %collective-permute-done.10.refs_3_), custom_call_target="tpu_custom_call" | custom-call | tf_op jit(solution)/shard_map/pallas_call | solution.py:593
  (21 shorter events, 0.3 us)
Async XLA Ops:
  0.0 7.4 %copy-start = (bf16[3,3,3,128,128]{4,3,2,1,0:T(8,128)(2,1)S(1)}, bf16[3,3,3,128,128]{4,3,2,1,0:T(8,128)(2,1)}, u32[]{:S(2)}) copy-start(bf16[3,3,3,128,128]{4,3,2,1,0:T(8,128)(2,1)} %weight_ref.1) | copy-start | bytes 2654212
  0.0 1.1 %copy-start.1 = (bf16[64,2,8,256]{3,2,1,0:T(8,128)(2,1)S(1)}, bf16[64,2,8,256]{3,2,1,0:T(8,128)(2,1)}, u32[]{:S(2)}) copy-start(bf16[64,2,8,256]{3,2,1,0:T(8,128)(2,1)} %param.7) | copy-start | bytes 1572868
  1.1 6.3 %copy-start.2 = (bf16[2,2,128,32]{2,3,1,0:T(8,128)(2,1)S(1)}, bf16[2,2,128,32]{2,3,1,0:T(8,128)(2,1)}, u32[]{:S(2)}) copy-start(bf16[2,2,128,32]{2,3,1,0:T(8,128)(2,1)} %param.12) | copy-start | bytes 98308
  1.7 9.4 %collective-permute-start = (bf16[1024,256]{1,0:T(8,128)(2,1)S(1)}, bf16[1024,256]{1,0:T(8,128)(2,1)S(1)}, u32[]{:S(2)}, u32[]{:S(2)}) collective-permute-start(bf16[1024,256]{1,0:T(8,128)(2,1)S(1)} %get-tuple-element.29._), channel_id=1, source_target_pairs={{0,1},{1,0},{2,3},{3,2},{4,5},{5,4},{6,7},{7,6},{8,9},{9,8},{10,11... | collective-permute-start | bytes 1572872 | tf_op jit(solution)/shard_map/ppermute | solution.py:530
  2.2 7.0 %collective-permute-start.1 = (bf16[128,256]{1,0:T(8,128)(2,1)S(1)}, bf16[128,256]{1,0:T(8,128)(2,1)S(1)}, u32[]{:S(2)}, u32[]{:S(2)}) collective-permute-start(bf16[128,256]{1,0:T(8,128)(2,1)S(1)} %get-tuple-element.36), channel_id=1, source_target_pairs={{0,2},{2,0},{1,3},{3,1},{4,6},{6,4},{5,7},{7,5},{8,10},{10,8},{9,1... | collective-permute-start | bytes 196616 | tf_op jit(solution)/shard_map/ppermute | solution.py:37
  4.8 2.7 %copy-start.6 = (f32[128]{0:T(128)S(1)}, f32[128]{0:T(128)}, u32[]{:S(2)}) copy-start(f32[128]{0:T(128)} %param.11) | copy-start | bytes 1540
  4.8 10.3 %collective-permute-start.3 = (bf16[512,256]{1,0:T(8,128)(2,1)S(1)}, bf16[512,256]{1,0:T(8,128)(2,1)S(1)}, u32[]{:S(2)}, u32[]{:S(2)}) collective-permute-start(bf16[512,256]{1,0:T(8,128)(2,1)S(1)} %get-tuple-element.35.refs_3_.refs_6_), channel_id=1, source_target_pairs={{1,5},{4,0},{5,9},{8,4},{9,13},{12,8},{13,12},{0,1},{3,7},{6,2},{7... | collective-permute-start | bytes 786440 | tf_op jit(solution)/shard_map/ppermute | solution.py:54
  4.9 10.2 %collective-permute-start.4 = (bf16[512,256]{1,0:T(8,128)(2,1)S(1)}, bf16[512,256]{1,0:T(8,128)(2,1)S(1)}, u32[]{:S(2)}, u32[]{:S(2)}) collective-permute-start(bf16[512,256]{1,0:T(8,128)(2,1)S(1)} %get-tuple-element.34.refs_2_.refs_5_), channel_id=1, source_target_pairs={{0,5},{5,0},{4,9},{9,4},{8,13},{13,8},{1,3},{12,14},{2,7},{7,2},{6... | collective-permute-start | bytes 786440 | tf_op jit(solution)/shard_map/ppermute | solution.py:54
  7.4 0.7 %copy-start.3 = (s32[2]{0:T(128)S(1)}, s32[2]{0:T(128)}, u32[]{:S(2)}) copy-start(s32[2]{0:T(128)} %param.8) | copy-start | bytes 28
  7.4 0.7 %copy-start.4 = (s32[1,8,1]{1,2,0:T(1,128)S(1)}, s32[1,8,1]{1,2,0:T(1,128)}, u32[]{:S(2)}) copy-start(s32[1,8,1]{1,2,0:T(1,128)} %param.13) | copy-start | bytes 100
  7.4 0.7 %copy-start.5 = (f32[128]{0:T(128)S(1)}, f32[128]{0:T(128)}, u32[]{:S(2)}) copy-start(f32[128]{0:T(128)} %param.10) | copy-start | bytes 1540
  9.4 1.7 %collective-permute-start.2 = (bf16[128,256]{1,0:T(8,128)(2,1)S(1)}, bf16[128,256]{1,0:T(8,128)(2,1)S(1)}, u32[]{:S(2)}, u32[]{:S(2)}) collective-permute-start(bf16[128,256]{1,0:T(8,128)(2,1)S(1)} %get-tuple-element.37.refs_5_.refs_8_), channel_id=1, source_target_pairs={{0,1},{1,0},{2,3},{3,2},{4,5},{5,4},{6,7},{7,6},{8,9},{9,8},{10,11... | collective-permute-start | bytes 196616 | tf_op jit(solution)/shard_map/ppermute | solution.py:537
  9.4 5.0 %collective-permute-start.6 = (bf16[80,256]{1,0:T(8,128)(2,1)S(1)}, bf16[80,256]{1,0:T(8,128)(2,1)S(1)}, u32[]{:S(2)}, u32[]{:S(2)}) collective-permute-start(bf16[80,256]{1,0:T(8,128)(2,1)S(1)} %get-tuple-element.40.refs_4_), channel_id=1, source_target_pairs={{0,5},{5,0},{4,9},{9,4},{8,13},{13,8},{1,3},{12,14},{2,7},{7,2},{6... | collective-permute-start | bytes 122888 | tf_op jit(solution)/shard_map/ppermute | solution.py:54
  11.1 4.0 %collective-permute-start.5 = (bf16[80,256]{1,0:T(8,128)(2,1)S(1)}, bf16[80,256]{1,0:T(8,128)(2,1)S(1)}, u32[]{:S(2)}, u32[]{:S(2)}) collective-permute-start(bf16[80,256]{1,0:T(8,128)(2,1)S(1)} %get-tuple-element.41), channel_id=1, source_target_pairs={{1,5},{4,0},{5,9},{8,4},{9,13},{12,8},{13,12},{0,1},{3,7},{6,2},{7... | collective-permute-start | bytes 122888 | tf_op jit(solution)/shard_map/ppermute | solution.py:54
  27.7 1.3 %collective-permute-start.7 = (bf16[7,16,128]{2,1,0:T(8,128)(2,1)S(1)}, bf16[7,16,128]{2,1,0:T(8,128)(2,1)S(1)}, u32[]{:S(2)}, u32[]{:S(2)}) collective-permute-start(bf16[7,16,128]{2,1,0:T(8,128)(2,1)S(1)} %get-tuple-element.48), channel_id=1, source_target_pairs={{0,1},{1,0},{2,3},{3,2},{4,5},{5,4},{6,7},{7,6},{8,9},{9,8},{10,11... | collective-permute-start | bytes 86024 | tf_op jit(solution)/shard_map/ppermute | solution.py:577
  29.2 5.5 %collective-permute-start.10 = (bf16[8,16,128]{2,1,0:T(8,128)(2,1)S(1)}, bf16[8,16,128]{2,1,0:T(8,128)(2,1)S(1)}, u32[]{:S(2)}, u32[]{:S(2)}) collective-permute-start(bf16[8,16,128]{2,1,0:T(8,128)(2,1)S(1)} %get-tuple-element.52), channel_id=1, source_target_pairs={{0,8},{4,12},{8,0},{12,4},{1,9},{5,13},{9,1},{13,5},{2,10},{6,14},... | collective-permute-start | bytes 98312 | tf_op jit(solution)/shard_map/ppermute | solution.py:589
  29.3 5.8 %collective-permute-start.8 = (bf16[8,16,128]{2,1,0:T(8,128)(2,1)S(1)}, bf16[8,16,128]{2,1,0:T(8,128)(2,1)S(1)}, u32[]{:S(2)}, u32[]{:S(2)}) collective-permute-start(bf16[8,16,128]{2,1,0:T(8,128)(2,1)S(1)} %get-tuple-element.50), channel_id=1, source_target_pairs={{0,12},{4,8},{8,4},{12,0},{1,13},{5,9},{9,5},{13,1},{2,14},{6,10},... | collective-permute-start | bytes 98312 | tf_op jit(solution)/shard_map/ppermute | solution.py:589
  31.4 4.0 %collective-permute-start.9 = (bf16[8,16,128]{2,1,0:T(8,128)(2,1)S(1)}, bf16[8,16,128]{2,1,0:T(8,128)(2,1)S(1)}, u32[]{:S(2)}, u32[]{:S(2)}) collective-permute-start(bf16[8,16,128]{2,1,0:T(8,128)(2,1)S(1)} %get-tuple-element.51), channel_id=1, source_target_pairs={{0,4},{4,0},{8,12},{12,8},{1,5},{5,1},{9,13},{13,9},{2,6},{6,2},{1... | collective-permute-start | bytes 98312 | tf_op jit(solution)/shard_map/ppermute | solution.py:589

commit v5 on v4

--- a/solution.py
+++ b/solution.py
@@ -247,6 +247,21 @@
     return even, odd
 
 
+def group_place():
+    return lax.broadcasted_iota(jnp.int32, (1, CHANNELS), 1) % (CHANNELS // GROUPS)
+
+
+def group_totals(lines):
+    lane = lax.broadcasted_iota(jnp.int32, lines.shape, 1)
+    step = 1
+    while step < CHANNELS // GROUPS:
+        ahead = pltpu.roll(lines, CHANNELS - step, 1)
+        behind = pltpu.roll(lines, step, 1)
+        lines = lines + jnp.where(lane // step % 2 == 0, ahead, behind)
+        step *= 2
+    return lines
+
+
 def lane_totals(first, second):
     rows = [jnp.sum(value.T, axis=0, keepdims=True) for value in (first, second)]
     return rows
@@ -288,7 +303,7 @@
         sums_ref[1:2, :] = two
 
 
-def late_kernel(rows, halos, slabs, small_ref, weight_ref, part_ref, sums_ref, own_edge_ref, *refs):
+def late_kernel(rows, halos, slabs, small_ref, weight_ref, part_ref, extra_ref, sums_ref, own_edge_ref, *refs):
     near, _ = local_sources(rows, *refs[:3], refs[3 : 3 + halos], refs[3 + halos : 3 + 2 * halos])
     refs = refs[3 + 2 * halos :]
     late_own_ref, late_other_ref, own_halo_ref, other_halo_ref = refs[:4]
@@ -331,12 +346,19 @@
     main_id = jnp.where(first, number, ids[1])
     extra_id = jnp.where(slab == 0, ids[0], -1.0)
     line = lax.broadcasted_iota(jnp.int32, (8, CHANNELS), 0)
-    message = jnp.where(line == 0, one, 0.0)
-    message = jnp.where(line == 1, two, message)
-    message = jnp.where(line == 2, sums_ref[0:1, :], message)
-    message = jnp.where(line == 3, sums_ref[1:2, :], message)
-    message = jnp.where(line == 4, main_id, message)
-    message = jnp.where(line == 5, extra_id, message)
+    sums = jnp.where(line == 0, one, 0.0)
+    sums = jnp.where(line == 1, two, sums)
+    sums = jnp.where(line == 2, sums_ref[0:1, :], sums)
+    sums = jnp.where(line == 3, sums_ref[1:2, :], sums)
+    sums = group_totals(sums)
+    place = group_place()
+    message = jnp.concatenate(
+        [
+            jnp.sum(jnp.where(line == jnp.broadcast_to(place, line.shape), sums, 0.0), axis=0, keepdims=True),
+            jnp.where(place < 2, main_id, extra_id),
+        ],
+        axis=0,
+    )
     for p in range(message_ref.shape[0]):
         message_ref[p] = message
     keys = jnp.zeros((8, CHANNELS), F32)
@@ -348,112 +370,98 @@
         extra_key = jnp.where(first, own_tail[n : n + 1, :], own_tail[quarter + n : quarter + n + 1, :])
         keys = jnp.where(line == kept + n, jnp.where(slab == 0, extra_key, 0.0), keys)
     keys_ref[...] = keys
+    conv_ref[rows + kept, :ID_ROWS, :CHANNELS] = jnp.concatenate([keys] * 2, axis=0).astype(BF16)
+
+    @pl.when(slab == 0)
+    def _():
+        conv_ref[rows : rows + kept] = extra_ref[...]
+
+
+def crossed(slabs):
+    return slabs in (2, 4)
 
 
 def norm_kernel(
-    count, message_ref, keys_ref, gathered_ref, small_ref, out_matrix_ref, conv_ref, extra_ref, mine_ref, theirs_ref
+    rows, slabs, spaces, capacity, message_ref, keys_ref, gathered_ref, small_ref, out_matrix_ref, conv_ref, other_ref,
+    *send_refs
 ):
-    rows, _, columns = conv_ref.shape
+    columns = conv_ref.shape[2]
     half = columns // 2
-    main = gathered_ref[:, 4, :]
-    extra = gathered_ref[:, 5, :]
+    kept = rows // 2
+    part = MOMENTS // 2
+    slab, space, chan = [lax.axis_index(name) for name in PART]
+    count = float(rows * columns)
+    sums, ids = gathered_ref[:, 0, :], gathered_ref[:, 1, :]
+    place = group_place()
+    beside = (slab * spaces + space) * 2 + 1 - chan
+    numbers = [message_ref[0, 1:2, 0:1], gathered_ref[beside, 1:2, 0:1], message_ref[0, 1:2, 2:3]]
     lines = []
-    for number in (message_ref[0, 4:5, :], message_ref[0, 5:6, :]):
-        on_main = main == number
-        on_extra = extra == number
-        for n in range(2):
-            picked = jnp.where(on_main, gathered_ref[:, n, :], 0.0) + jnp.where(
-                on_extra, gathered_ref[:, 2 + n, :], 0.0
-            )
-            lines.append(jnp.sum(picked, axis=0, keepdims=True))
-        held = jnp.where(on_main, float(count), 0.0) + jnp.where(on_extra, float(count // 2), 0.0)
-        lines.append(jnp.sum(held, axis=0, keepdims=True))
-    lines += [jnp.zeros((1, CHANNELS), F32)] * 2
-    size = CHANNELS // GROUPS
-    group_row = lax.broadcasted_iota(jnp.int32, (CHANNELS, CHANNELS), 0) // size
-    group_column = lax.broadcasted_iota(jnp.int32, (CHANNELS, CHANNELS), 1) // size
-    member = jnp.where(group_row == group_column, 1.0, 0.0)
-    totals = jnp.dot(
-        jnp.concatenate(lines, axis=0), member, preferred_element_type=F32, precision=lax.Precision.HIGHEST
-    )
+    for number in numbers:
+        mask = ids == number
+        picked = jnp.sum(jnp.where(mask, sums, 0.0), axis=0, keepdims=True)
+        pixels = jnp.where(place == 0, count, jnp.where(place == 2, 0.5 * count, 0.0))
+        held = jnp.sum(jnp.where(mask, pixels, 0.0), axis=0, keepdims=True)
+        lines += [jnp.where(place % 2 == n, picked, 0.0) for n in range(2)] + [held]
+    totals = group_totals(jnp.concatenate(lines + [jnp.zeros((7, CHANNELS), F32)], axis=0))
+    matrix = out_matrix_ref[pl.ds(pl.multiple_of(chan * part, part), part), :]
 
     def factors(first):
-        counts = totals[first + 2 : first + 3, :]
+        size = float(CHANNELS // GROUPS)
+        counts = totals[first + 2 : first + 3, :] * size
         mean = totals[first : first + 1, :] / counts
         var = totals[first + 1 : first + 2, :] / counts - mean * mean
         scale = lax.rsqrt(var + 1e-06) * small_ref[0:1, :]
         offset = small_ref[1:2, :] - mean * scale
         return [jnp.broadcast_to(0.5 * value, (CHANNELS, CHANNELS)).T for value in (scale, offset)]
 
-    def project(source_ref, scale, offset):
+    def project(source_ref, first, lines, scale, offset):
         images = []
-        for r in range(source_ref.shape[0] // 2):
+        for r in range(first, first + lines, 2):
             pieces = []
             for i in range(2):
                 for j in range(2):
-                    value = source_ref[2 * r + i, :, j * half : (j + 1) * half].astype(F32)
+                    value = source_ref[r + i, :, j * half : (j + 1) * half].astype(F32)
                     value = value * scale + offset
                     pieces.append((value + value * jnp.tanh(value)).astype(BF16))
             images.append(jnp.concatenate(pieces, axis=0))
         image = jnp.concatenate(images, axis=1)
-        return jnp.dot(out_matrix_ref[...], image, preferred_element_type=F32)
-
-    chan = lax.axis_index("chan")
-    kept = rows // 2
-    part = MOMENTS // 2
-
-    def store(latent, first):
-        for n in range(latent.shape[1] // half):
-            blocks = [latent[c * part : (c + 1) * part, n * half : (n + 1) * half].astype(BF16) for c in range(2)]
-            mine_ref[first + n] = jnp.where(chan == 0, blocks[0], blocks[1])
-            theirs_ref[first + n] = jnp.where(chan == 0, blocks[1], blocks[0])
-
-    store(project(conv_ref, *factors(0)), 0)
-    theirs_ref[kept + kept // 2] = jnp.concatenate([keys_ref[...]] * 2, axis=0).astype(BF16)
-
-    @pl.when(lax.axis_index("tm") == 0)
+        return jnp.dot(matrix, image, preferred_element_type=F32)
+
+    own_keys = keys_ref[...]
+    other_keys = other_ref[rows + kept, :ID_ROWS, :CHANNELS].astype(F32)
+
+    def blocks(latent, keys, first):
+        return [
+            (keys[first + n : first + n + 1, :], latent[:, n * half : (n + 1) * half])
+            for n in range(latent.shape[1] // half)
+        ]
+
+    def spread(groups, started):
+        for d in range(slabs):
+            owner = (slab ^ d if crossed(slabs) else jnp.int32(d)).astype(F32)
+            for j in range(capacity):
+                wanted = owner * float(capacity) + float(j + 1)
+                for first, group in groups:
+                    ref = send_refs[d].at[first + j] if crossed(slabs) else send_refs[0].at[d, first + j]
+                    value = ref[...].astype(F32) if started else jnp.zeros((part, half), F32)
+                    for key, block in group:
+                        value = jnp.where(key == wanted, block, value)
+                    ref[...] = value.astype(BF16)
+
+    mine = project(conv_ref, 0, rows, *factors(0))
+    others = project(other_ref, 0, rows, *factors(3))
+    second = chan == 1
+    now = blocks(jnp.where(second, mine, others), jnp.where(second, own_keys, other_keys[:8, :]), 0)
+    following = blocks(jnp.where(second, others, mine), jnp.where(second, other_keys[:8, :], own_keys), 0)
+    spread(((0, now), (capacity, following)), False)
+
+    @pl.when(slab == 0)
     def _():
-        store(project(extra_ref, *factors(3)), kept)
-
-    @pl.when(lax.axis_index("tm") > 0)
-    def _():
-        for n in range(kept // 2):
-            mine_ref[kept + n] = jnp.zeros((part, half), BF16)
-            theirs_ref[kept + n] = jnp.zeros((part, half), BF16)
-
-
-def crossed(slabs):
-    return slabs in (2, 4)
-
-
-def place_kernel(slabs, capacity, kept, keys_ref, mine_ref, other_ref, *send_refs):
-    slab = lax.axis_index("tm")
-    second = lax.axis_index("chan") == 1
-    count = kept + kept // 2
-    other_keys = other_ref[count].astype(F32)
-    rows = []
-    for n in range(count):
-        mine = (keys_ref[n : n + 1, :], mine_ref[n].astype(F32))
-        other = (other_keys[n : n + 1, :], other_ref[n].astype(F32))
-        if n < kept:
-            picked = [[jnp.where(second, x, y) for x, y in pair] for pair in (zip(mine, other), zip(other, mine))]
-            rows.append(((picked[0],), picked[1]))
-        else:
-            rows.append(((mine, other), None))
-    now = [row for group, _ in rows for row in group]
-    following = [row for _, row in rows if row is not None]
-    for d in range(slabs):
-        owner = (slab ^ d if crossed(slabs) else jnp.int32(d)).astype(F32)
-        for j in range(capacity):
-            wanted = owner * float(capacity) + float(j + 1)
-            for first, group in ((0, now), (capacity, following)):
-                value = jnp.zeros(mine_ref.shape[1:], F32)
-                for key, block in group:
-                    value = jnp.where(key == wanted, block, value)
-                if crossed(slabs):
-                    send_refs[d][first + j] = value.astype(BF16)
-                else:
-                    send_refs[0][d, first + j] = value.astype(BF16)
+        scale, offset = factors(6)
+        begin = []
+        for ref, keys in ((conv_ref, own_keys), (other_ref, other_keys)):
+            begin += blocks(project(ref, rows, kept, scale, offset), keys, kept)
+        spread(((0, begin),), True)
 
 
 def merge_kernel(slabs, capacity, *refs):
@@ -552,36 +560,29 @@
     conv, message, keys = whole_call(
         lambda *refs: late_kernel(rows, halos, slabs, *refs),
         (
-            jax.ShapeDtypeStruct((rows, CHANNELS, columns), BF16),
-            jax.ShapeDtypeStruct((parts, 8, CHANNELS), F32),
+            jax.ShapeDtypeStruct((rows + kept + 1, CHANNELS, columns), BF16),
+            jax.ShapeDtypeStruct((parts, 2, CHANNELS), F32),
             jax.ShapeDtypeStruct((8, CHANNELS), F32),
         ),
         (
-            small, late_weight, part, extra_sums, cross_halo, *here, late_own, late_other, late_own_halo, late_other_halo,
+            small, late_weight, part, extra, extra_sums, cross_halo, *here, late_own, late_other, late_own_halo, late_other_halo,
         ),
         [pltpu.VMEM((rows + 2, CHANNELS, columns), BF16)],
         flops=1500000000,
     )
+    conv_other = lax.ppermute(conv, "chan", turn)
     gathered = lax.all_to_all(message, PART, split_axis=0, concat_axis=0, tiled=True)
     part = MOMENTS // chans
     width = columns // 2
-    count = kept + kept // 2
-    mine, theirs = whole_call(
-        lambda *refs: norm_kernel(rows * columns, *refs),
-        (
-            jax.ShapeDtypeStruct((count, part, width), BF16),
-            jax.ShapeDtypeStruct((count + 1, part, width), BF16),
-        ),
-        (message, keys, gathered, small, out_matrix, conv, extra),
-    )
-    from_other = lax.ppermute(theirs, "chan", turn)
     blocks = (2 * capacity, part, width)
     if crossed(slabs):
         shapes = (jax.ShapeDtypeStruct(blocks, BF16),) * slabs
     else:
         shapes = (jax.ShapeDtypeStruct((slabs,) + blocks, BF16),)
     sends = whole_call(
-        lambda *refs: place_kernel(slabs, capacity, kept, *refs), shapes, (keys, mine, from_other)
+        lambda *refs: norm_kernel(rows, slabs, spaces, capacity, *refs),
+        shapes,
+        (message, keys, gathered, small, out_matrix, conv, conv_other),
     )
     if crossed(slabs):
         received = [sends[0]]

time: 36.3 us -> 35.3 us (0.972)
  waiting for transfers between devices: 5.65 us -> 4.55 us
  Pallas kernels: 7.2 us -> 7.63 us
    ppermute x1, waiting for transfers between devices: 1.19 us -> 0.01 us  [shards(): conv_other = lax.ppermute(conv, 'chan', turn)]
    pallas_call x7 -> x6, Pallas kernels: 6.53 us -> 6.96 us  [whole_call(): pl.pallas_call(kernel, out_shape=out_shape, in_specs=specs or [VMEM] * le...]
  transfers between devices with their start and end apart: 11 -> 11, of which waited for: 6 -> 5; matrix products, arithmetic and copies ran while one was open for 0% -> 0% of each run, Pallas kernels for 10% -> 10%
where the time goes in v5:
time: 35.3 us; the launch traced here: 35.1 us
  starting transfers between devices  11.1 us (31%)
  blocking collectives  10 us (28%)
  Pallas kernels  7.63 us (22%)
  waiting for transfers between devices  4.55 us (13%)
  local copies, waits for them, and re-layouts  1.79 us (5%)
    all_to_all x1, blocking collectives, shards(): lax.all_to_all(message, PART, split_axis=0, concat_axis=0, tiled=True)  10 us
    pallas_call x6, Pallas kernels, whole_call(): pl.pallas_call(kernel, out_shape=out_shape, in_specs=specs or [VMEM] * le...  6.96 us
    ppermute x4, starting transfers between devices, slab_swap(): return lax.ppermute(value, PART, flat_pairs(sizes, pairs))  4.32 us
    ppermute x3, starting transfers between devices, shards(): lax.ppermute(sends[d], 'tm', [(t, t ^ d) for t in range(slabs)])  3.55 us
    ppermute x3, waiting for transfers between devices, shards(): lax.ppermute(sends[d], 'tm', [(t, t ^ d) for t in range(slabs)])  2.76 us
    ppermute x1, starting transfers between devices, space_swap(): return lax.ppermute(value, PART, flat_pairs(sizes, pairs))  2.56 us
    unnamed x14, local copies, waits for them, and re-layouts  1.79 us
    ppermute x4, waiting for transfers between devices, slab_swap(): return lax.ppermute(value, PART, flat_pairs(sizes, pairs))  1.77 us
  transfers between devices with their start and end apart: 11, of which 5 were waited for; matrix products, arithmetic and copies ran while one was open for 0% of the time, Pallas kernels for 10%

profile of v5, /device:TPU:0, one launch (start us, length us, event | category | flops | bytes accessed | tf_op | source)
XLA Modules:
  0.0 35.1 jit_solution(4621624561933108872)
XLA Ops:
  0.0 1.1 %copy-done.1 = bf16[64,2,8,256]{3,2,1,0:T(8,128)(2,1)S(1)} copy-done((bf16[64,2,8,256]{3,2,1,0:T(8,128)(2,1)S(1)}, bf16[64,2,8,256]{3,2,1,0:T(8,128)(2,1)}, u32[]{:S(2)}) %copy-start.1) | copy-done | bytes 524312
  1.1 0.5 %shard_map.73 = (bf16[512,256]{1,0:T(8,128)(2,1)S(1)}, bf16[512,256]{1,0:T(8,128)(2,1)S(1)}, bf16[1024,256]{1,0:T(8,128)(2,1)S(1)}, bf16[128,256]{1,0:T(8,128)(2,1)S(1)}) custom-call(bf16[1024,256]{1,0:T(8,128)(2,1)S(1)} %bitcast.7), custom_call_target="tpu_custom_call" | custom-call | flops 300000000 | bytes 750000 | tf_op jit(solution)/shard_map/pallas_call | solution.py:58
  1.7 0.5 %collective-permute-start = (bf16[1024,256]{1,0:T(8,128)(2,1)S(1)}, bf16[1024,256]{1,0:T(8,128)(2,1)S(1)}, u32[]{:S(2)}, u32[]{:S(2)}) collective-permute-start(bf16[1024,256]{1,0:T(8,128)(2,1)S(1)} %get-tuple-element.27._), channel_id=1, source_target_pairs={{0,1},{1,0},{2,3},{3,2},{4,5},{5,4},{6,7},{7,6},{8,9},{9,8},{10,11... | collective-permute-start | bytes 1572872 | tf_op jit(solution)/shard_map/ppermute | solution.py:538
  2.2 2.6 %collective-permute-start.1 = (bf16[128,256]{1,0:T(8,128)(2,1)S(1)}, bf16[128,256]{1,0:T(8,128)(2,1)S(1)}, u32[]{:S(2)}, u32[]{:S(2)}) collective-permute-start(bf16[128,256]{1,0:T(8,128)(2,1)S(1)} %get-tuple-element.34), channel_id=1, source_target_pairs={{0,2},{2,0},{1,3},{3,1},{4,6},{6,4},{5,7},{7,5},{8,10},{10,8},{9,1... | collective-permute-start | bytes 196616 | tf_op jit(solution)/shard_map/ppermute | solution.py:37
  4.8 0.2 collective-permute-start.3
  4.9 2.5 %collective-permute-start.4 = (bf16[512,256]{1,0:T(8,128)(2,1)S(1)}, bf16[512,256]{1,0:T(8,128)(2,1)S(1)}, u32[]{:S(2)}, u32[]{:S(2)}) collective-permute-start(bf16[512,256]{1,0:T(8,128)(2,1)S(1)} %get-tuple-element.32.refs_2_.refs_6_), channel_id=1, source_target_pairs={{0,5},{5,0},{4,9},{9,4},{8,13},{13,8},{1,3},{12,14},{2,7},{7,2},{6... | collective-permute-start | bytes 786440 | tf_op jit(solution)/shard_map/ppermute | solution.py:54
  7.4 0.6 %copy-done.3 = s32[2]{0:T(128)S(1)} copy-done((s32[2]{0:T(128)S(1)}, s32[2]{0:T(128)}, u32[]{:S(2)}) %copy-start.3) | copy-done | bytes 32
  8.1 1.1 %shard_map.74 = (bf16[384,768]{1,0:T(8,128)(2,1)S(1)}, bf16[2,384,384]{2,1,0:T(8,128)(2,1)S(1)}, bf16[384,384]{1,0:T(8,128)(2,1)S(1)}, f32[8,128]{1,0:T(8,128)S(1)}, bf16[32,512]{1,0:T(8,128)(2,1)S(1)}) custom-call(s32[1,2]{1,0:T(1,128)S(1)} %bitcast.9, s32[1,8]{1,0:T(1,128)S(1)} %bitcast.10, f32[1,128]{1,0:T(1,128)S(1)} %bitcast.11, f32[1,128]{1,0:T(1,128)S(1)} %bitcast.12, ...), custom_call_target="tpu_custom_call" | custom-call | flops 1200000000 | bytes 3000000 | tf_op jit(solution)/shard_map/pallas_call | solution.py:58
  9.2 0.2 shard_map.75
  9.4 1.7 %collective-permute-start.6 = (bf16[80,256]{1,0:T(8,128)(2,1)S(1)}, bf16[80,256]{1,0:T(8,128)(2,1)S(1)}, u32[]{:S(2)}, u32[]{:S(2)}) collective-permute-start(bf16[80,256]{1,0:T(8,128)(2,1)S(1)} %get-tuple-element.39.refs_5_), channel_id=1, source_target_pairs={{0,5},{5,0},{4,9},{9,4},{8,13},{13,8},{1,3},{12,14},{2,7},{7,2},{6... | collective-permute-start | bytes 122888 | tf_op jit(solution)/shard_map/ppermute | solution.py:54
  11.1 2.2 %shard_map.76 = (f32[8,128,256]{2,1,0:T(8,128)S(1)}, bf16[4,128,256]{2,1,0:T(8,128)(2,1)S(1)}, f32[8,128]{1,0:T(8,128)S(1)}) custom-call(bf16[384,768]{1,0:T(8,128)(2,1)S(1)} %get-tuple-element.30.refs_0_, bf16[384,384]{1,0:T(8,128)(2,1)S(1)} %get-tuple-element.31.refs_1_, bf16[512,256]{1,0:T(8,128)(2,1)S(1)} %get-tuple-element.32.refs_2_.refs_6_, ...), custom_call_target="tpu_custom_call" | custom-call | flops 1800000000 | bytes 4500000 | tf_op jit(solution)/shard_map/pallas_call | solution.py:58
  13.3 1.1 %collective-permute-done.6.refs_14_ = bf16[80,256]{1,0:T(8,128)(2,1)S(1)} collective-permute-done((bf16[80,256]{1,0:T(8,128)(2,1)S(1)}, bf16[80,256]{1,0:T(8,128)(2,1)S(1)}, u32[]{:S(2)}, u32[]{:S(2)}) %collective-permute-start.6) | collective-permute-done | bytes 40992 | tf_op jit(solution)/shard_map/ppermute | solution.py:54
  14.4 0.7 %collective-permute-done.5.refs_13_ = bf16[80,256]{1,0:T(8,128)(2,1)S(1)} collective-permute-done((bf16[80,256]{1,0:T(8,128)(2,1)S(1)}, bf16[80,256]{1,0:T(8,128)(2,1)S(1)}, u32[]{:S(2)}, u32[]{:S(2)}) %collective-permute-start.5) | collective-permute-done | bytes 40992 | tf_op jit(solution)/shard_map/ppermute | solution.py:54
  15.1 1.5 %shard_map.77 = (bf16[13,128,256]{2,1,0:T(8,128)(2,1)S(1)}, f32[16,2,128]{2,1,0:T(2,128)S(1)}, f32[8,128]{1,0:T(8,128)S(1)}) custom-call(f32[8,128]{1,0:T(8,128)S(1)} %get-tuple-element.28.refs_0_.refs_3_, bf16[2,384,384]{2,1,0:T(8,128)(2,1)S(1)} %get-tuple-element.29.refs_1_, f32[8,128,256]{2,1,0:T(8,128)S(1)} %get-tuple-element.36.refs_2_, ...), custom_call_target="tpu_custom_call" | custom-call | flops 1500000000 | bytes 3750000 | tf_op jit(solution)/shard_map/pallas_call | solution.py:58
  16.6 0.1 collective-permute-start.7
  16.6 10.0 %all_to_all.5.refs_2_ = f32[16,2,128]{2,1,0:T(2,128)S(1)} all-to-all(f32[16,2,128]{2,1,0:T(2,128)S(1)} %get-tuple-element.41.refs_0_), channel_id=1, replica_groups=mesh['groups'=2,'tm'=4,'space'=2,'chan'=2] {'tm','space','chan'}, dimensions={0} | all-to-all | bytes 32768 | tf_op jit(solution)/shard_map/all_to_all | solution.py:574
  26.7 1.5 %shard_map.78 = (bf16[8,16,128]{2,1,0:T(8,128)(2,1)S(1)}, bf16[8,16,128]{2,1,0:T(8,128)(2,1)S(1)}, bf16[8,16,128]{2,1,0:T(8,128)(2,1)S(1)}, bf16[8,16,128]{2,1,0:T(8,128)(2,1)S(1)}) custom-call(f32[16,2,128]{2,1,0:T(2,128)S(1)} %get-tuple-element.41.refs_0_, f32[8,128]{1,0:T(8,128)S(1)} %get-tuple-element.42.refs_1_, f32[16,2,128]{2,1,0:T(2,128)S(1)} %all_to_all.5.refs_2_, ...), custom_call_target="tpu_custom_call" | custom-call | tf_op jit(solution)/shard_map/pallas_call | solution.py:58
  28.2 0.1 collective-permute-start.10
  28.2 2.3 %collective-permute-start.8 = (bf16[8,16,128]{2,1,0:T(8,128)(2,1)S(1)}, bf16[8,16,128]{2,1,0:T(8,128)(2,1)S(1)}, u32[]{:S(2)}, u32[]{:S(2)}) collective-permute-start(bf16[8,16,128]{2,1,0:T(8,128)(2,1)S(1)} %get-tuple-element.46), channel_id=1, source_target_pairs={{0,12},{4,8},{8,4},{12,0},{1,13},{5,9},{9,5},{13,1},{2,14},{6,10},... | collective-permute-start | bytes 98312 | tf_op jit(solution)/shard_map/ppermute | solution.py:590
  30.6 1.1 %collective-permute-start.9 = (bf16[8,16,128]{2,1,0:T(8,128)(2,1)S(1)}, bf16[8,16,128]{2,1,0:T(8,128)(2,1)S(1)}, u32[]{:S(2)}, u32[]{:S(2)}) collective-permute-start(bf16[8,16,128]{2,1,0:T(8,128)(2,1)S(1)} %get-tuple-element.47), channel_id=1, source_target_pairs={{0,4},{4,0},{8,12},{12,8},{1,5},{5,1},{9,13},{13,9},{2,6},{6,2},{1... | collective-permute-start | bytes 98312 | tf_op jit(solution)/shard_map/ppermute | solution.py:590
  31.7 1.7 %collective-permute-done.10.refs_3_ = bf16[8,16,128]{2,1,0:T(8,128)(2,1)S(1)} collective-permute-done((bf16[8,16,128]{2,1,0:T(8,128)(2,1)S(1)}, bf16[8,16,128]{2,1,0:T(8,128)(2,1)S(1)}, u32[]{:S(2)}, u32[]{:S(2)}) %collective-permute-start.10) | collective-permute-done | bytes 32800 | tf_op jit(solution)/shard_map/ppermute | solution.py:590
  33.4 0.7 %collective-permute-done.8.refs_1_ = bf16[8,16,128]{2,1,0:T(8,128)(2,1)S(1)} collective-permute-done((bf16[8,16,128]{2,1,0:T(8,128)(2,1)S(1)}, bf16[8,16,128]{2,1,0:T(8,128)(2,1)S(1)}, u32[]{:S(2)}, u32[]{:S(2)}) %collective-permute-start.8) | collective-permute-done | bytes 32800 | tf_op jit(solution)/shard_map/ppermute | solution.py:590
  34.1 0.4 %collective-permute-done.9.refs_2_ = bf16[8,16,128]{2,1,0:T(8,128)(2,1)S(1)} collective-permute-done((bf16[8,16,128]{2,1,0:T(8,128)(2,1)S(1)}, bf16[8,16,128]{2,1,0:T(8,128)(2,1)S(1)}, u32[]{:S(2)}, u32[]{:S(2)}) %collective-permute-start.9) | collective-permute-done | bytes 32800 | tf_op jit(solution)/shard_map/ppermute | solution.py:590
  34.5 0.7 %shard_map.79 = bf16[16,16,128]{2,1,0:T(8,128)(2,1)} custom-call(bf16[8,16,128]{2,1,0:T(8,128)(2,1)S(1)} %get-tuple-element.45.refs_0_, bf16[8,16,128]{2,1,0:T(8,128)(2,1)S(1)} %collective-permute-done.8.refs_1_, bf16[8,16,128]{2,1,0:T(8,128)(2,1)S(1)} %collective-permute-done.9.refs_2_, bf16[8,16,128]{2,1,0:T(8,128)(2,1)S(1)} %collective-permute-done.10.refs_3_), custom_call_target="tpu_custom_call" | custom-call | tf_op jit(solution)/shard_map/pallas_call | solution.py:594
  (20 shorter events, 0.1 us)
Async XLA Ops:
  0.0 7.4 %copy-start = (bf16[3,3,3,128,128]{4,3,2,1,0:T(8,128)(2,1)S(1)}, bf16[3,3,3,128,128]{4,3,2,1,0:T(8,128)(2,1)}, u32[]{:S(2)}) copy-start(bf16[3,3,3,128,128]{4,3,2,1,0:T(8,128)(2,1)} %weight_ref.1) | copy-start | bytes 2654212
  0.0 1.1 %copy-start.1 = (bf16[64,2,8,256]{3,2,1,0:T(8,128)(2,1)S(1)}, bf16[64,2,8,256]{3,2,1,0:T(8,128)(2,1)}, u32[]{:S(2)}) copy-start(bf16[64,2,8,256]{3,2,1,0:T(8,128)(2,1)} %param.7) | copy-start | bytes 1572868
  1.1 6.3 %copy-start.2 = (bf16[2,2,128,32]{2,3,1,0:T(8,128)(2,1)S(1)}, bf16[2,2,128,32]{2,3,1,0:T(8,128)(2,1)}, u32[]{:S(2)}) copy-start(bf16[2,2,128,32]{2,3,1,0:T(8,128)(2,1)} %param.12) | copy-start | bytes 98308
  1.7 9.4 %collective-permute-start = (bf16[1024,256]{1,0:T(8,128)(2,1)S(1)}, bf16[1024,256]{1,0:T(8,128)(2,1)S(1)}, u32[]{:S(2)}, u32[]{:S(2)}) collective-permute-start(bf16[1024,256]{1,0:T(8,128)(2,1)S(1)} %get-tuple-element.27._), channel_id=1, source_target_pairs={{0,1},{1,0},{2,3},{3,2},{4,5},{5,4},{6,7},{7,6},{8,9},{9,8},{10,11... | collective-permute-start | bytes 1572872 | tf_op jit(solution)/shard_map/ppermute | solution.py:538
  2.2 7.0 %collective-permute-start.1 = (bf16[128,256]{1,0:T(8,128)(2,1)S(1)}, bf16[128,256]{1,0:T(8,128)(2,1)S(1)}, u32[]{:S(2)}, u32[]{:S(2)}) collective-permute-start(bf16[128,256]{1,0:T(8,128)(2,1)S(1)} %get-tuple-element.34), channel_id=1, source_target_pairs={{0,2},{2,0},{1,3},{3,1},{4,6},{6,4},{5,7},{7,5},{8,10},{10,8},{9,1... | collective-permute-start | bytes 196616 | tf_op jit(solution)/shard_map/ppermute | solution.py:37
  4.8 2.7 %copy-start.6 = (f32[128]{0:T(128)S(1)}, f32[128]{0:T(128)}, u32[]{:S(2)}) copy-start(f32[128]{0:T(128)} %param.11) | copy-start | bytes 1540
  4.8 10.3 %collective-permute-start.3 = (bf16[512,256]{1,0:T(8,128)(2,1)S(1)}, bf16[512,256]{1,0:T(8,128)(2,1)S(1)}, u32[]{:S(2)}, u32[]{:S(2)}) collective-permute-start(bf16[512,256]{1,0:T(8,128)(2,1)S(1)} %get-tuple-element.33.refs_3_.refs_7_), channel_id=1, source_target_pairs={{1,5},{4,0},{5,9},{8,4},{9,13},{12,8},{13,12},{0,1},{3,7},{6,2},{7... | collective-permute-start | bytes 786440 | tf_op jit(solution)/shard_map/ppermute | solution.py:54
  4.9 10.2 %collective-permute-start.4 = (bf16[512,256]{1,0:T(8,128)(2,1)S(1)}, bf16[512,256]{1,0:T(8,128)(2,1)S(1)}, u32[]{:S(2)}, u32[]{:S(2)}) collective-permute-start(bf16[512,256]{1,0:T(8,128)(2,1)S(1)} %get-tuple-element.32.refs_2_.refs_6_), channel_id=1, source_target_pairs={{0,5},{5,0},{4,9},{9,4},{8,13},{13,8},{1,3},{12,14},{2,7},{7,2},{6... | collective-permute-start | bytes 786440 | tf_op jit(solution)/shard_map/ppermute | solution.py:54
  7.4 0.7 %copy-start.3 = (s32[2]{0:T(128)S(1)}, s32[2]{0:T(128)}, u32[]{:S(2)}) copy-start(s32[2]{0:T(128)} %param.8) | copy-start | bytes 28
  7.4 0.7 %copy-start.4 = (s32[1,8,1]{1,2,0:T(1,128)S(1)}, s32[1,8,1]{1,2,0:T(1,128)}, u32[]{:S(2)}) copy-start(s32[1,8,1]{1,2,0:T(1,128)} %param.13) | copy-start | bytes 100
  7.4 0.7 %copy-start.5 = (f32[128]{0:T(128)S(1)}, f32[128]{0:T(128)}, u32[]{:S(2)}) copy-start(f32[128]{0:T(128)} %param.10) | copy-start | bytes 1540
  9.4 1.7 %collective-permute-start.2 = (bf16[128,256]{1,0:T(8,128)(2,1)S(1)}, bf16[128,256]{1,0:T(8,128)(2,1)S(1)}, u32[]{:S(2)}, u32[]{:S(2)}) collective-permute-start(bf16[128,256]{1,0:T(8,128)(2,1)S(1)} %get-tuple-element.35.refs_5_.refs_9_), channel_id=1, source_target_pairs={{0,1},{1,0},{2,3},{3,2},{4,5},{5,4},{6,7},{7,6},{8,9},{9,8},{10,11... | collective-permute-start | bytes 196616 | tf_op jit(solution)/shard_map/ppermute | solution.py:545
  9.4 5.0 %collective-permute-start.6 = (bf16[80,256]{1,0:T(8,128)(2,1)S(1)}, bf16[80,256]{1,0:T(8,128)(2,1)S(1)}, u32[]{:S(2)}, u32[]{:S(2)}) collective-permute-start(bf16[80,256]{1,0:T(8,128)(2,1)S(1)} %get-tuple-element.39.refs_5_), channel_id=1, source_target_pairs={{0,5},{5,0},{4,9},{9,4},{8,13},{13,8},{1,3},{12,14},{2,7},{7,2},{6... | collective-permute-start | bytes 122888 | tf_op jit(solution)/shard_map/ppermute | solution.py:54
  11.1 4.0 %collective-permute-start.5 = (bf16[80,256]{1,0:T(8,128)(2,1)S(1)}, bf16[80,256]{1,0:T(8,128)(2,1)S(1)}, u32[]{:S(2)}, u32[]{:S(2)}) collective-permute-start(bf16[80,256]{1,0:T(8,128)(2,1)S(1)} %get-tuple-element.40), channel_id=1, source_target_pairs={{1,5},{4,0},{5,9},{8,4},{9,13},{12,8},{13,12},{0,1},{3,7},{6,2},{7... | collective-permute-start | bytes 122888 | tf_op jit(solution)/shard_map/ppermute | solution.py:54
  16.6 10.1 %collective-permute-start.7 = (bf16[13,128,256]{2,1,0:T(8,128)(2,1)S(1)}, bf16[13,128,256]{2,1,0:T(8,128)(2,1)S(1)}, u32[]{:S(2)}, u32[]{:S(2)}) collective-permute-start(bf16[13,128,256]{2,1,0:T(8,128)(2,1)S(1)} %get-tuple-element.44.refs_5_), channel_id=1, source_target_pairs={{0,1},{1,0},{2,3},{3,2},{4,5},{5,4},{6,7},{7,6},{8,9},{9,8},{10,11... | collective-permute-start | bytes 2555912 | tf_op jit(solution)/shard_map/ppermute | solution.py:573
  28.2 5.2 %collective-permute-start.10 = (bf16[8,16,128]{2,1,0:T(8,128)(2,1)S(1)}, bf16[8,16,128]{2,1,0:T(8,128)(2,1)S(1)}, u32[]{:S(2)}, u32[]{:S(2)}) collective-permute-start(bf16[8,16,128]{2,1,0:T(8,128)(2,1)S(1)} %get-tuple-element.48), channel_id=1, source_target_pairs={{0,8},{4,12},{8,0},{12,4},{1,9},{5,13},{9,1},{13,5},{2,10},{6,14},... | collective-permute-start | bytes 98312 | tf_op jit(solution)/shard_map/ppermute | solution.py:590
  28.2 5.8 %collective-permute-start.8 = (bf16[8,16,128]{2,1,0:T(8,128)(2,1)S(1)}, bf16[8,16,128]{2,1,0:T(8,128)(2,1)S(1)}, u32[]{:S(2)}, u32[]{:S(2)}) collective-permute-start(bf16[8,16,128]{2,1,0:T(8,128)(2,1)S(1)} %get-tuple-element.46), channel_id=1, source_target_pairs={{0,12},{4,8},{8,4},{12,0},{1,13},{5,9},{9,5},{13,1},{2,14},{6,10},... | collective-permute-start | bytes 98312 | tf_op jit(solution)/shard_map/ppermute | solution.py:590
  30.6 3.9 %collective-permute-start.9 = (bf16[8,16,128]{2,1,0:T(8,128)(2,1)S(1)}, bf16[8,16,128]{2,1,0:T(8,128)(2,1)S(1)}, u32[]{:S(2)}, u32[]{:S(2)}) collective-permute-start(bf16[8,16,128]{2,1,0:T(8,128)(2,1)S(1)} %get-tuple-element.47), channel_id=1, source_target_pairs={{0,4},{4,0},{8,12},{12,8},{1,5},{5,1},{9,13},{13,9},{2,6},{6,2},{1... | collective-permute-start | bytes 98312 | tf_op jit(solution)/shard_map/ppermute | solution.py:590

commit v6 on v5

--- a/solution.py
+++ b/solution.py
@@ -54,16 +54,22 @@
     return lax.ppermute(value, PART, flat_pairs(sizes, pairs))
 
 
-def whole_call(kernel, out_shape, args, scratch=(), specs=None, flops=0):
+def whole_call(kernel, out_shape, args, scratch=(), specs=None, flops=0, vmem=40, first=()):
+    turns = list(first) + [n for n in range(len(args)) if n not in first]
+    specs = specs or [VMEM] * len(args)
+
+    def turned(*refs):
+        kernel(*[refs[turns.index(n)] for n in range(len(args))], *refs[len(args) :])
+
     return pl.pallas_call(
-        kernel,
+        turned,
         out_shape=out_shape,
-        in_specs=specs or [VMEM] * len(args),
+        in_specs=[specs[n] for n in turns],
         out_specs=jax.tree.map(lambda _: VMEM, out_shape),
         scratch_shapes=scratch,
-        compiler_params=PARAMS,
-        cost_estimate=None if flops is None else pl.CostEstimate(flops=flops, bytes_accessed=flops // 400, transcendentals=0),
-    )(*args)
+        compiler_params=pltpu.CompilerParams(vmem_limit_bytes=vmem * 1024 * 1024),
+        cost_estimate=pl.CostEstimate(flops=flops, bytes_accessed=flops // 400, transcendentals=0),
+    )(*[args[n] for n in turns])
 
 
 def number_at(small_ref, n):
@@ -504,7 +510,7 @@
         lambda *refs: front_kernel(rows, *refs),
         (payload, payload, jax.ShapeDtypeStruct((2 * rows * half, columns), BF16)) + (pair,) * halos,
         (activations.reshape(half * frames * rows, columns),),
-        flops=300000000,
+        flops=3000000000,
     )
     own_halos = [space_swap(edge, sizes, start) for start, edge in enumerate(edges)]
     late_own = slab_swap(same, sizes, False)

time: 35.3 us -> 35.3 us (level)
  no operation moved by 1% of the time
where the time goes in v6:
time: 35.3 us; the launch traced here: 35.1 us
  starting transfers between devices  11.1 us (31%)
  blocking collectives  10 us (28%)
  Pallas kernels  7.63 us (22%)
  waiting for transfers between devices  4.55 us (13%)
  local copies, waits for them, and re-layouts  1.71 us (5%)
    all_to_all x1, blocking collectives, shards(): lax.all_to_all(message, PART, split_axis=0, concat_axis=0, tiled=True)  10 us
    pallas_call x6, Pallas kernels, whole_call(): pl.pallas_call(turned, out_shape=out_shape, in_specs=[specs[n] for n in t...  6.97 us
    ppermute x4, starting transfers between devices, slab_swap(): return lax.ppermute(value, PART, flat_pairs(sizes, pairs))  4.32 us
    ppermute x3, starting transfers between devices, shards(): lax.ppermute(sends[d], 'tm', [(t, t ^ d) for t in range(slabs)])  3.55 us
    ppermute x3, waiting for transfers between devices, shards(): lax.ppermute(sends[d], 'tm', [(t, t ^ d) for t in range(slabs)])  2.76 us
    ppermute x1, starting transfers between devices, space_swap(): return lax.ppermute(value, PART, flat_pairs(sizes, pairs))  2.56 us
    ppermute x4, waiting for transfers between devices, slab_swap(): return lax.ppermute(value, PART, flat_pairs(sizes, pairs))  1.77 us
    unnamed x14, local copies, waits for them, and re-layouts  1.71 us
  transfers between devices with their start and end apart: 11, of which 5 were waited for; matrix products, arithmetic and copies ran while one was open for 0% of the time, Pallas kernels for 10%

profile of v6, /device:TPU:0, one launch (start us, length us, event | category | flops | bytes accessed | tf_op | source)
XLA Modules:
  0.0 35.1 jit_solution(4221508094993938621)
XLA Ops:
  0.0 1.0 %copy-done.1 = bf16[64,2,8,256]{3,2,1,0:T(8,128)(2,1)S(1)} copy-done((bf16[64,2,8,256]{3,2,1,0:T(8,128)(2,1)S(1)}, bf16[64,2,8,256]{3,2,1,0:T(8,128)(2,1)}, u32[]{:S(2)}) %copy-start.1) | copy-done | bytes 524312
  1.0 0.5 %shard_map.73 = (bf16[512,256]{1,0:T(8,128)(2,1)S(1)}, bf16[512,256]{1,0:T(8,128)(2,1)S(1)}, bf16[1024,256]{1,0:T(8,128)(2,1)S(1)}, bf16[128,256]{1,0:T(8,128)(2,1)S(1)}) custom-call(bf16[1024,256]{1,0:T(8,128)(2,1)S(1)} %bitcast.7), custom_call_target="tpu_custom_call" | custom-call | flops 3000000000 | bytes 7500000 | tf_op jit(solution)/shard_map/pallas_call | solution.py:64
  1.6 0.5 %collective-permute-start = (bf16[1024,256]{1,0:T(8,128)(2,1)S(1)}, bf16[1024,256]{1,0:T(8,128)(2,1)S(1)}, u32[]{:S(2)}, u32[]{:S(2)}) collective-permute-start(bf16[1024,256]{1,0:T(8,128)(2,1)S(1)} %get-tuple-element.27.refs_6_), channel_id=1, source_target_pairs={{0,1},{1,0},{2,3},{3,2},{4,5},{5,4},{6,7},{7,6},{8,9},{9,8},{10,11... | collective-permute-start | bytes 1572872 | tf_op jit(solution)/shard_map/ppermute | solution.py:544
  2.1 2.6 %collective-permute-start.1 = (bf16[128,256]{1,0:T(8,128)(2,1)S(1)}, bf16[128,256]{1,0:T(8,128)(2,1)S(1)}, u32[]{:S(2)}, u32[]{:S(2)}) collective-permute-start(bf16[128,256]{1,0:T(8,128)(2,1)S(1)} %get-tuple-element.34), channel_id=1, source_target_pairs={{0,2},{2,0},{1,3},{3,1},{4,6},{6,4},{5,7},{7,5},{8,10},{10,8},{9,1... | collective-permute-start | bytes 196616 | tf_op jit(solution)/shard_map/ppermute | solution.py:37
  4.7 0.2 collective-permute-start.3
  4.8 2.5 %collective-permute-start.4 = (bf16[512,256]{1,0:T(8,128)(2,1)S(1)}, bf16[512,256]{1,0:T(8,128)(2,1)S(1)}, u32[]{:S(2)}, u32[]{:S(2)}) collective-permute-start(bf16[512,256]{1,0:T(8,128)(2,1)S(1)} %get-tuple-element.32.refs_2_.refs_6_), channel_id=1, source_target_pairs={{0,5},{5,0},{4,9},{9,4},{8,13},{13,8},{1,3},{12,14},{2,7},{7,2},{6... | collective-permute-start | bytes 786440 | tf_op jit(solution)/shard_map/ppermute | solution.py:54
  7.4 0.6 %copy-done.3 = s32[2]{0:T(128)S(1)} copy-done((s32[2]{0:T(128)S(1)}, s32[2]{0:T(128)}, u32[]{:S(2)}) %copy-start.3) | copy-done | bytes 32
  8.0 1.1 %shard_map.74 = (bf16[384,768]{1,0:T(8,128)(2,1)S(1)}, bf16[2,384,384]{2,1,0:T(8,128)(2,1)S(1)}, bf16[384,384]{1,0:T(8,128)(2,1)S(1)}, f32[8,128]{1,0:T(8,128)S(1)}, bf16[32,512]{1,0:T(8,128)(2,1)S(1)}) custom-call(s32[1,2]{1,0:T(1,128)S(1)} %bitcast.9, s32[1,8]{1,0:T(1,128)S(1)} %bitcast.10, f32[1,128]{1,0:T(1,128)S(1)} %bitcast.11, f32[1,128]{1,0:T(1,128)S(1)} %bitcast.12, ...), custom_call_target="tpu_custom_call" | custom-call | flops 1200000000 | bytes 3000000 | tf_op jit(solution)/shard_map/pallas_call | solution.py:64
  9.1 0.2 shard_map.75
  9.3 1.7 %collective-permute-start.6 = (bf16[80,256]{1,0:T(8,128)(2,1)S(1)}, bf16[80,256]{1,0:T(8,128)(2,1)S(1)}, u32[]{:S(2)}, u32[]{:S(2)}) collective-permute-start(bf16[80,256]{1,0:T(8,128)(2,1)S(1)} %get-tuple-element.39.refs_5_), channel_id=1, source_target_pairs={{0,5},{5,0},{4,9},{9,4},{8,13},{13,8},{1,3},{12,14},{2,7},{7,2},{6... | collective-permute-start | bytes 122888 | tf_op jit(solution)/shard_map/ppermute | solution.py:54
  11.0 2.2 %shard_map.76 = (f32[8,128,256]{2,1,0:T(8,128)S(1)}, bf16[4,128,256]{2,1,0:T(8,128)(2,1)S(1)}, f32[8,128]{1,0:T(8,128)S(1)}) custom-call(bf16[384,768]{1,0:T(8,128)(2,1)S(1)} %get-tuple-element.30.refs_0_, bf16[384,384]{1,0:T(8,128)(2,1)S(1)} %get-tuple-element.31.refs_1_, bf16[512,256]{1,0:T(8,128)(2,1)S(1)} %get-tuple-element.32.refs_2_.refs_6_, ...), custom_call_target="tpu_custom_call" | custom-call | flops 1800000000 | bytes 4500000 | tf_op jit(solution)/shard_map/pallas_call | solution.py:64
  13.3 1.0 %collective-permute-done.6.refs_14_ = bf16[80,256]{1,0:T(8,128)(2,1)S(1)} collective-permute-done((bf16[80,256]{1,0:T(8,128)(2,1)S(1)}, bf16[80,256]{1,0:T(8,128)(2,1)S(1)}, u32[]{:S(2)}, u32[]{:S(2)}) %collective-permute-start.6) | collective-permute-done | bytes 40992 | tf_op jit(solution)/shard_map/ppermute | solution.py:54
  14.3 0.7 %collective-permute-done.5.refs_13_ = bf16[80,256]{1,0:T(8,128)(2,1)S(1)} collective-permute-done((bf16[80,256]{1,0:T(8,128)(2,1)S(1)}, bf16[80,256]{1,0:T(8,128)(2,1)S(1)}, u32[]{:S(2)}, u32[]{:S(2)}) %collective-permute-start.5) | collective-permute-done | bytes 40992 | tf_op jit(solution)/shard_map/ppermute | solution.py:54
  15.0 1.5 %shard_map.77 = (bf16[13,128,256]{2,1,0:T(8,128)(2,1)S(1)}, f32[16,2,128]{2,1,0:T(2,128)S(1)}, f32[8,128]{1,0:T(8,128)S(1)}) custom-call(f32[8,128]{1,0:T(8,128)S(1)} %get-tuple-element.28.refs_0_.refs_3_, bf16[2,384,384]{2,1,0:T(8,128)(2,1)S(1)} %get-tuple-element.29.refs_1_, f32[8,128,256]{2,1,0:T(8,128)S(1)} %get-tuple-element.36.refs_2_, ...), custom_call_target="tpu_custom_call" | custom-call | flops 1500000000 | bytes 3750000 | tf_op jit(solution)/shard_map/pallas_call | solution.py:64
  16.5 0.1 collective-permute-start.7
  16.6 10.0 %all_to_all.5.refs_2_ = f32[16,2,128]{2,1,0:T(2,128)S(1)} all-to-all(f32[16,2,128]{2,1,0:T(2,128)S(1)} %get-tuple-element.41.refs_0_), channel_id=1, replica_groups=mesh['groups'=2,'tm'=4,'space'=2,'chan'=2] {'tm','space','chan'}, dimensions={0} | all-to-all | bytes 32768 | tf_op jit(solution)/shard_map/all_to_all | solution.py:580
  26.6 1.5 %shard_map.78 = (bf16[8,16,128]{2,1,0:T(8,128)(2,1)S(1)}, bf16[8,16,128]{2,1,0:T(8,128)(2,1)S(1)}, bf16[8,16,128]{2,1,0:T(8,128)(2,1)S(1)}, bf16[8,16,128]{2,1,0:T(8,128)(2,1)S(1)}) custom-call(f32[16,2,128]{2,1,0:T(2,128)S(1)} %get-tuple-element.41.refs_0_, f32[8,128]{1,0:T(8,128)S(1)} %get-tuple-element.42.refs_1_, f32[16,2,128]{2,1,0:T(2,128)S(1)} %all_to_all.5.refs_2_, ...), custom_call_target="tpu_custom_call" | custom-call | tf_op jit(solution)/shard_map/pallas_call | solution.py:64
  28.1 0.1 collective-permute-start.10
  28.2 2.3 %collective-permute-start.8 = (bf16[8,16,128]{2,1,0:T(8,128)(2,1)S(1)}, bf16[8,16,128]{2,1,0:T(8,128)(2,1)S(1)}, u32[]{:S(2)}, u32[]{:S(2)}) collective-permute-start(bf16[8,16,128]{2,1,0:T(8,128)(2,1)S(1)} %get-tuple-element.46), channel_id=1, source_target_pairs={{0,12},{4,8},{8,4},{12,0},{1,13},{5,9},{9,5},{13,1},{2,14},{6,10},... | collective-permute-start | bytes 98312 | tf_op jit(solution)/shard_map/ppermute | solution.py:596
  30.5 1.1 %collective-permute-start.9 = (bf16[8,16,128]{2,1,0:T(8,128)(2,1)S(1)}, bf16[8,16,128]{2,1,0:T(8,128)(2,1)S(1)}, u32[]{:S(2)}, u32[]{:S(2)}) collective-permute-start(bf16[8,16,128]{2,1,0:T(8,128)(2,1)S(1)} %get-tuple-element.47), channel_id=1, source_target_pairs={{0,4},{4,0},{8,12},{12,8},{1,5},{5,1},{9,13},{13,9},{2,6},{6,2},{1... | collective-permute-start | bytes 98312 | tf_op jit(solution)/shard_map/ppermute | solution.py:596
  31.6 1.7 %collective-permute-done.10.refs_3_ = bf16[8,16,128]{2,1,0:T(8,128)(2,1)S(1)} collective-permute-done((bf16[8,16,128]{2,1,0:T(8,128)(2,1)S(1)}, bf16[8,16,128]{2,1,0:T(8,128)(2,1)S(1)}, u32[]{:S(2)}, u32[]{:S(2)}) %collective-permute-start.10) | collective-permute-done | bytes 32800 | tf_op jit(solution)/shard_map/ppermute | solution.py:596
  33.3 0.7 %collective-permute-done.8.refs_1_ = bf16[8,16,128]{2,1,0:T(8,128)(2,1)S(1)} collective-permute-done((bf16[8,16,128]{2,1,0:T(8,128)(2,1)S(1)}, bf16[8,16,128]{2,1,0:T(8,128)(2,1)S(1)}, u32[]{:S(2)}, u32[]{:S(2)}) %collective-permute-start.8) | collective-permute-done | bytes 32800 | tf_op jit(solution)/shard_map/ppermute | solution.py:596
  34.0 0.4 %collective-permute-done.9.refs_2_ = bf16[8,16,128]{2,1,0:T(8,128)(2,1)S(1)} collective-permute-done((bf16[8,16,128]{2,1,0:T(8,128)(2,1)S(1)}, bf16[8,16,128]{2,1,0:T(8,128)(2,1)S(1)}, u32[]{:S(2)}, u32[]{:S(2)}) %collective-permute-start.9) | collective-permute-done | bytes 32800 | tf_op jit(solution)/shard_map/ppermute | solution.py:596
  34.4 0.7 %shard_map.79 = bf16[16,16,128]{2,1,0:T(8,128)(2,1)} custom-call(bf16[8,16,128]{2,1,0:T(8,128)(2,1)S(1)} %get-tuple-element.45.refs_0_, bf16[8,16,128]{2,1,0:T(8,128)(2,1)S(1)} %collective-permute-done.8.refs_1_, bf16[8,16,128]{2,1,0:T(8,128)(2,1)S(1)} %collective-permute-done.9.refs_2_, bf16[8,16,128]{2,1,0:T(8,128)(2,1)S(1)} %collective-permute-done.10.refs_3_), custom_call_target="tpu_custom_call" | custom-call | tf_op jit(solution)/shard_map/pallas_call | solution.py:600
  (20 shorter events, 0.1 us)
Async XLA Ops:
  0.0 1.0 %copy-start.1 = (bf16[64,2,8,256]{3,2,1,0:T(8,128)(2,1)S(1)}, bf16[64,2,8,256]{3,2,1,0:T(8,128)(2,1)}, u32[]{:S(2)}) copy-start(bf16[64,2,8,256]{3,2,1,0:T(8,128)(2,1)} %param.7) | copy-start | bytes 1572868
  1.0 6.3 %copy-start = (bf16[3,3,3,128,128]{4,3,2,1,0:T(8,128)(2,1)S(1)}, bf16[3,3,3,128,128]{4,3,2,1,0:T(8,128)(2,1)}, u32[]{:S(2)}) copy-start(bf16[3,3,3,128,128]{4,3,2,1,0:T(8,128)(2,1)} %refs_5_.1) | copy-start | bytes 2654212
  1.0 6.3 %copy-start.2 = (bf16[2,2,128,32]{2,3,1,0:T(8,128)(2,1)S(1)}, bf16[2,2,128,32]{2,3,1,0:T(8,128)(2,1)}, u32[]{:S(2)}) copy-start(bf16[2,2,128,32]{2,3,1,0:T(8,128)(2,1)} %param.12) | copy-start | bytes 98308
  1.0 6.3 %copy-start.6 = (f32[128]{0:T(128)S(1)}, f32[128]{0:T(128)}, u32[]{:S(2)}) copy-start(f32[128]{0:T(128)} %param.11) | copy-start | bytes 1540
  1.6 9.4 %collective-permute-start = (bf16[1024,256]{1,0:T(8,128)(2,1)S(1)}, bf16[1024,256]{1,0:T(8,128)(2,1)S(1)}, u32[]{:S(2)}, u32[]{:S(2)}) collective-permute-start(bf16[1024,256]{1,0:T(8,128)(2,1)S(1)} %get-tuple-element.27.refs_6_), channel_id=1, source_target_pairs={{0,1},{1,0},{2,3},{3,2},{4,5},{5,4},{6,7},{7,6},{8,9},{9,8},{10,11... | collective-permute-start | bytes 1572872 | tf_op jit(solution)/shard_map/ppermute | solution.py:544
  2.1 7.0 %collective-permute-start.1 = (bf16[128,256]{1,0:T(8,128)(2,1)S(1)}, bf16[128,256]{1,0:T(8,128)(2,1)S(1)}, u32[]{:S(2)}, u32[]{:S(2)}) collective-permute-start(bf16[128,256]{1,0:T(8,128)(2,1)S(1)} %get-tuple-element.34), channel_id=1, source_target_pairs={{0,2},{2,0},{1,3},{3,1},{4,6},{6,4},{5,7},{7,5},{8,10},{10,8},{9,1... | collective-permute-start | bytes 196616 | tf_op jit(solution)/shard_map/ppermute | solution.py:37
  4.7 10.3 %collective-permute-start.3 = (bf16[512,256]{1,0:T(8,128)(2,1)S(1)}, bf16[512,256]{1,0:T(8,128)(2,1)S(1)}, u32[]{:S(2)}, u32[]{:S(2)}) collective-permute-start(bf16[512,256]{1,0:T(8,128)(2,1)S(1)} %get-tuple-element.33.refs_3_.refs_7_), channel_id=1, source_target_pairs={{1,5},{4,0},{5,9},{8,4},{9,13},{12,8},{13,12},{0,1},{3,7},{6,2},{7... | collective-permute-start | bytes 786440 | tf_op jit(solution)/shard_map/ppermute | solution.py:54
  4.8 10.2 %collective-permute-start.4 = (bf16[512,256]{1,0:T(8,128)(2,1)S(1)}, bf16[512,256]{1,0:T(8,128)(2,1)S(1)}, u32[]{:S(2)}, u32[]{:S(2)}) collective-permute-start(bf16[512,256]{1,0:T(8,128)(2,1)S(1)} %get-tuple-element.32.refs_2_.refs_6_), channel_id=1, source_target_pairs={{0,5},{5,0},{4,9},{9,4},{8,13},{13,8},{1,3},{12,14},{2,7},{7,2},{6... | collective-permute-start | bytes 786440 | tf_op jit(solution)/shard_map/ppermute | solution.py:54
  7.3 0.7 %copy-start.3 = (s32[2]{0:T(128)S(1)}, s32[2]{0:T(128)}, u32[]{:S(2)}) copy-start(s32[2]{0:T(128)} %param.8) | copy-start | bytes 28
  7.3 0.7 %copy-start.4 = (s32[1,8,1]{1,2,0:T(1,128)S(1)}, s32[1,8,1]{1,2,0:T(1,128)}, u32[]{:S(2)}) copy-start(s32[1,8,1]{1,2,0:T(1,128)} %param.13) | copy-start | bytes 100
  7.3 0.7 %copy-start.5 = (f32[128]{0:T(128)S(1)}, f32[128]{0:T(128)}, u32[]{:S(2)}) copy-start(f32[128]{0:T(128)} %param.10) | copy-start | bytes 1540
  9.3 1.7 %collective-permute-start.2 = (bf16[128,256]{1,0:T(8,128)(2,1)S(1)}, bf16[128,256]{1,0:T(8,128)(2,1)S(1)}, u32[]{:S(2)}, u32[]{:S(2)}) collective-permute-start(bf16[128,256]{1,0:T(8,128)(2,1)S(1)} %get-tuple-element.35.refs_5_.refs_9_), channel_id=1, source_target_pairs={{0,1},{1,0},{2,3},{3,2},{4,5},{5,4},{6,7},{7,6},{8,9},{9,8},{10,11... | collective-permute-start | bytes 196616 | tf_op jit(solution)/shard_map/ppermute | solution.py:551
  9.3 5.0 %collective-permute-start.6 = (bf16[80,256]{1,0:T(8,128)(2,1)S(1)}, bf16[80,256]{1,0:T(8,128)(2,1)S(1)}, u32[]{:S(2)}, u32[]{:S(2)}) collective-permute-start(bf16[80,256]{1,0:T(8,128)(2,1)S(1)} %get-tuple-element.39.refs_5_), channel_id=1, source_target_pairs={{0,5},{5,0},{4,9},{9,4},{8,13},{13,8},{1,3},{12,14},{2,7},{7,2},{6... | collective-permute-start | bytes 122888 | tf_op jit(solution)/shard_map/ppermute | solution.py:54
  11.0 4.0 %collective-permute-start.5 = (bf16[80,256]{1,0:T(8,128)(2,1)S(1)}, bf16[80,256]{1,0:T(8,128)(2,1)S(1)}, u32[]{:S(2)}, u32[]{:S(2)}) collective-permute-start(bf16[80,256]{1,0:T(8,128)(2,1)S(1)} %get-tuple-element.40), channel_id=1, source_target_pairs={{1,5},{4,0},{5,9},{8,4},{9,13},{12,8},{13,12},{0,1},{3,7},{6,2},{7... | collective-permute-start | bytes 122888 | tf_op jit(solution)/shard_map/ppermute | solution.py:54
  16.5 10.1 %collective-permute-start.7 = (bf16[13,128,256]{2,1,0:T(8,128)(2,1)S(1)}, bf16[13,128,256]{2,1,0:T(8,128)(2,1)S(1)}, u32[]{:S(2)}, u32[]{:S(2)}) collective-permute-start(bf16[13,128,256]{2,1,0:T(8,128)(2,1)S(1)} %get-tuple-element.44.refs_5_), channel_id=1, source_target_pairs={{0,1},{1,0},{2,3},{3,2},{4,5},{5,4},{6,7},{7,6},{8,9},{9,8},{10,11... | collective-permute-start | bytes 2555912 | tf_op jit(solution)/shard_map/ppermute | solution.py:579
  28.1 5.2 %collective-permute-start.10 = (bf16[8,16,128]{2,1,0:T(8,128)(2,1)S(1)}, bf16[8,16,128]{2,1,0:T(8,128)(2,1)S(1)}, u32[]{:S(2)}, u32[]{:S(2)}) collective-permute-start(bf16[8,16,128]{2,1,0:T(8,128)(2,1)S(1)} %get-tuple-element.48), channel_id=1, source_target_pairs={{0,8},{4,12},{8,0},{12,4},{1,9},{5,13},{9,1},{13,5},{2,10},{6,14},... | collective-permute-start | bytes 98312 | tf_op jit(solution)/shard_map/ppermute | solution.py:596
  28.2 5.8 %collective-permute-start.8 = (bf16[8,16,128]{2,1,0:T(8,128)(2,1)S(1)}, bf16[8,16,128]{2,1,0:T(8,128)(2,1)S(1)}, u32[]{:S(2)}, u32[]{:S(2)}) collective-permute-start(bf16[8,16,128]{2,1,0:T(8,128)(2,1)S(1)} %get-tuple-element.46), channel_id=1, source_target_pairs={{0,12},{4,8},{8,4},{12,0},{1,13},{5,9},{9,5},{13,1},{2,14},{6,10},... | collective-permute-start | bytes 98312 | tf_op jit(solution)/shard_map/ppermute | solution.py:596
  30.5 3.9 %collective-permute-start.9 = (bf16[8,16,128]{2,1,0:T(8,128)(2,1)S(1)}, bf16[8,16,128]{2,1,0:T(8,128)(2,1)S(1)}, u32[]{:S(2)}, u32[]{:S(2)}) collective-permute-start(bf16[8,16,128]{2,1,0:T(8,128)(2,1)S(1)} %get-tuple-element.47), channel_id=1, source_target_pairs={{0,4},{4,0},{8,12},{12,8},{1,5},{5,1},{9,13},{13,9},{2,6},{6,2},{1... | collective-permute-start | bytes 98312 | tf_op jit(solution)/shard_map/ppermute | solution.py:596

commit v7 on v6

--- a/solution.py
+++ b/solution.py
@@ -363,10 +363,9 @@
             jnp.sum(jnp.where(line == jnp.broadcast_to(place, line.shape), sums, 0.0), axis=0, keepdims=True),
             jnp.where(place < 2, main_id, extra_id),
         ],
-        axis=0,
-    )
-    for p in range(message_ref.shape[0]):
-        message_ref[p] = message
+        axis=1,
+    )
+    message_ref[...] = jnp.broadcast_to(message, message_ref.shape)
     keys = jnp.zeros((8, CHANNELS), F32)
     for n in range(kept):
         main_key = jnp.where(first, late_tail[n : n + 1, :], own_tail[kept + n : kept + n + 1, :])
@@ -397,10 +396,15 @@
     part = MOMENTS // 2
     slab, space, chan = [lax.axis_index(name) for name in PART]
     count = float(rows * columns)
-    sums, ids = gathered_ref[:, 0, :], gathered_ref[:, 1, :]
+    sums, ids = gathered_ref[:, :CHANNELS], gathered_ref[:, CHANNELS:]
     place = group_place()
     beside = (slab * spaces + space) * 2 + 1 - chan
-    numbers = [message_ref[0, 1:2, 0:1], gathered_ref[beside, 1:2, 0:1], message_ref[0, 1:2, 2:3]]
+    line = lax.broadcasted_iota(jnp.int32, (gathered_ref.shape[0], 1), 0)
+    numbers = [
+        message_ref[0:1, CHANNELS : CHANNELS + 1],
+        jnp.sum(jnp.where(line == beside, gathered_ref[:, CHANNELS : CHANNELS + 1], 0.0), axis=0, keepdims=True),
+        message_ref[0:1, CHANNELS + 2 : CHANNELS + 3],
+    ]
     lines = []
     for number in numbers:
         mask = ids == number
@@ -544,9 +548,9 @@
     other = lax.ppermute(both, "chan", turn)
     message_halo = jax.ShapeDtypeStruct((halos * half + ID_ROWS, columns), BF16)
     *own_halos, cross_halo, same_halo = whole_call(
-        lambda *refs: halo_kernel(halos, capacity, *refs),
+        lambda *refs: halo_kernel(halos, capacity, *refs[: 1 + halos], *refs[2 + halos :]),
         (pair,) * halos + (message_halo, message_halo),
-        (small, *own_halos),
+        (small, *own_halos, other),
     )
     other_halos = [lax.ppermute(halo, "chan", turn) for halo in own_halos]
     late_own_halo = slab_swap(same_halo, sizes, False)
@@ -567,7 +571,7 @@
         lambda *refs: late_kernel(rows, halos, slabs, *refs),
         (
             jax.ShapeDtypeStruct((rows + kept + 1, CHANNELS, columns), BF16),
-            jax.ShapeDtypeStruct((parts, 2, CHANNELS), F32),
+            jax.ShapeDtypeStruct((parts, 2 * CHANNELS), F32),
             jax.ShapeDtypeStruct((8, CHANNELS), F32),
         ),
         (

time: 35.3 us -> 35.2 us (level)
    unnamed x14 -> x15, local copies, waits for them, and re-layouts: 1.71 us -> 1.71 us
  transfers between devices with their start and end apart: 11 -> 11, of which waited for: 5 -> 7; matrix products, arithmetic and copies ran while one was open for 0% -> 0% of each run, Pallas kernels for 10% -> 10%
where the time goes in v7:
time: 35.2 us; the launch traced here: 35 us
  starting transfers between devices  11.1 us (32%)
  blocking collectives  9.94 us (28%)
  Pallas kernels  7.6 us (22%)
  waiting for transfers between devices  4.54 us (13%)
  local copies, waits for them, and re-layouts  1.73 us (5%)
    all_to_all x1, blocking collectives, shards(): lax.all_to_all(message, PART, split_axis=0, concat_axis=0, tiled=True)  9.94 us
    pallas_call x6, Pallas kernels, whole_call(): pl.pallas_call(turned, out_shape=out_shape, in_specs=[specs[n] for n in t...  6.94 us
    ppermute x4, starting transfers between devices, slab_swap(): return lax.ppermute(value, PART, flat_pairs(sizes, pairs))  4.32 us
    ppermute x3, starting transfers between devices, shards(): lax.ppermute(sends[d], 'tm', [(t, t ^ d) for t in range(slabs)])  3.55 us
    ppermute x3, waiting for transfers between devices, shards(): lax.ppermute(sends[d], 'tm', [(t, t ^ d) for t in range(slabs)])  2.77 us
    ppermute x1, starting transfers between devices, space_swap(): return lax.ppermute(value, PART, flat_pairs(sizes, pairs))  2.56 us
    ppermute x4, waiting for transfers between devices, slab_swap(): return lax.ppermute(value, PART, flat_pairs(sizes, pairs))  1.76 us
    unnamed x15, local copies, waits for them, and re-layouts  1.71 us
  transfers between devices with their start and end apart: 11, of which 7 were waited for; matrix products, arithmetic and copies ran while one was open for 0% of the time, Pallas kernels for 10%

profile of v7, /device:TPU:0, one launch (start us, length us, event | category | flops | bytes accessed | tf_op | source)
XLA Modules:
  0.0 35.0 jit_solution(16947954468677426336)
XLA Ops:
  0.0 1.0 %copy-done.1 = bf16[64,2,8,256]{3,2,1,0:T(8,128)(2,1)S(1)} copy-done((bf16[64,2,8,256]{3,2,1,0:T(8,128)(2,1)S(1)}, bf16[64,2,8,256]{3,2,1,0:T(8,128)(2,1)}, u32[]{:S(2)}) %copy-start.1) | copy-done | bytes 524312
  1.0 0.5 %shard_map.73 = (bf16[512,256]{1,0:T(8,128)(2,1)S(1)}, bf16[512,256]{1,0:T(8,128)(2,1)S(1)}, bf16[1024,256]{1,0:T(8,128)(2,1)S(1)}, bf16[128,256]{1,0:T(8,128)(2,1)S(1)}) custom-call(bf16[1024,256]{1,0:T(8,128)(2,1)S(1)} %bitcast.13), custom_call_target="tpu_custom_call" | custom-call | flops 3000000000 | bytes 7500000 | tf_op jit(solution)/shard_map/pallas_call | solution.py:64
  1.6 0.5 %collective-permute-start = (bf16[1024,256]{1,0:T(8,128)(2,1)S(1)}, bf16[1024,256]{1,0:T(8,128)(2,1)S(1)}, u32[]{:S(2)}, u32[]{:S(2)}) collective-permute-start(bf16[1024,256]{1,0:T(8,128)(2,1)S(1)} %get-tuple-element.27.refs_6_), channel_id=1, source_target_pairs={{0,1},{1,0},{2,3},{3,2},{4,5},{5,4},{6,7},{7,6},{8,9},{9,8},{10,11... | collective-permute-start | bytes 1572872 | tf_op jit(solution)/shard_map/ppermute | solution.py:548
  2.1 2.6 %collective-permute-start.1 = (bf16[128,256]{1,0:T(8,128)(2,1)S(1)}, bf16[128,256]{1,0:T(8,128)(2,1)S(1)}, u32[]{:S(2)}, u32[]{:S(2)}) collective-permute-start(bf16[128,256]{1,0:T(8,128)(2,1)S(1)} %get-tuple-element.34), channel_id=1, source_target_pairs={{0,2},{2,0},{1,3},{3,1},{4,6},{6,4},{5,7},{7,5},{8,10},{10,8},{9,1... | collective-permute-start | bytes 196616 | tf_op jit(solution)/shard_map/ppermute | solution.py:37
  4.7 0.2 collective-permute-start.3
  4.8 2.5 %collective-permute-start.4 = (bf16[512,256]{1,0:T(8,128)(2,1)S(1)}, bf16[512,256]{1,0:T(8,128)(2,1)S(1)}, u32[]{:S(2)}, u32[]{:S(2)}) collective-permute-start(bf16[512,256]{1,0:T(8,128)(2,1)S(1)} %get-tuple-element.32.refs_2_.refs_6_), channel_id=1, source_target_pairs={{0,5},{5,0},{4,9},{9,4},{8,13},{13,8},{1,3},{12,14},{2,7},{7,2},{6... | collective-permute-start | bytes 786440 | tf_op jit(solution)/shard_map/ppermute | solution.py:54
  7.4 0.6 %copy-done.3 = s32[2]{0:T(128)S(1)} copy-done((s32[2]{0:T(128)S(1)}, s32[2]{0:T(128)}, u32[]{:S(2)}) %copy-start.3) | copy-done | bytes 32
  8.0 1.1 %shard_map.74 = (bf16[384,768]{1,0:T(8,128)(2,1)S(1)}, bf16[2,384,384]{2,1,0:T(8,128)(2,1)S(1)}, bf16[384,384]{1,0:T(8,128)(2,1)S(1)}, f32[8,128]{1,0:T(8,128)S(1)}, bf16[32,512]{1,0:T(8,128)(2,1)S(1)}) custom-call(s32[1,2]{1,0:T(1,128)S(1)} %bitcast.15, s32[1,8]{1,0:T(1,128)S(1)} %bitcast.16, f32[1,128]{1,0:T(1,128)S(1)} %bitcast.17, ...), custom_call_target="tpu_custom_call" | custom-call | flops 1200000000 | bytes 3000000 | tf_op jit(solution)/shard_map/pallas_call | solution.py:64
  9.1 0.2 shard_map.75
  9.3 1.7 %collective-permute-start.6 = (bf16[80,256]{1,0:T(8,128)(2,1)S(1)}, bf16[80,256]{1,0:T(8,128)(2,1)S(1)}, u32[]{:S(2)}, u32[]{:S(2)}) collective-permute-start(bf16[80,256]{1,0:T(8,128)(2,1)S(1)} %get-tuple-element.39.refs_5_), channel_id=1, source_target_pairs={{0,5},{5,0},{4,9},{9,4},{8,13},{13,8},{1,3},{12,14},{2,7},{7,2},{6... | collective-permute-start | bytes 122888 | tf_op jit(solution)/shard_map/ppermute | solution.py:54
  11.0 2.2 %shard_map.76 = (f32[8,128,256]{2,1,0:T(8,128)S(1)}, bf16[4,128,256]{2,1,0:T(8,128)(2,1)S(1)}, f32[8,128]{1,0:T(8,128)S(1)}) custom-call(bf16[384,768]{1,0:T(8,128)(2,1)S(1)} %get-tuple-element.30.refs_0_, bf16[384,384]{1,0:T(8,128)(2,1)S(1)} %get-tuple-element.31.refs_1_, bf16[512,256]{1,0:T(8,128)(2,1)S(1)} %get-tuple-element.32.refs_2_.refs_6_, ...), custom_call_target="tpu_custom_call" | custom-call | flops 1800000000 | bytes 4500000 | tf_op jit(solution)/shard_map/pallas_call | solution.py:64
  13.3 0.3 collective-permute-done.3.refs_11_
  13.5 0.3 collective-permute-done.4.refs_12_
  13.9 0.4 %collective-permute-done.6.refs_14_ = bf16[80,256]{1,0:T(8,128)(2,1)S(1)} collective-permute-done((bf16[80,256]{1,0:T(8,128)(2,1)S(1)}, bf16[80,256]{1,0:T(8,128)(2,1)S(1)}, u32[]{:S(2)}, u32[]{:S(2)}) %collective-permute-start.6) | collective-permute-done | bytes 40992 | tf_op jit(solution)/shard_map/ppermute | solution.py:54
  14.3 0.7 %collective-permute-done.5.refs_13_ = bf16[80,256]{1,0:T(8,128)(2,1)S(1)} collective-permute-done((bf16[80,256]{1,0:T(8,128)(2,1)S(1)}, bf16[80,256]{1,0:T(8,128)(2,1)S(1)}, u32[]{:S(2)}, u32[]{:S(2)}) %collective-permute-start.5) | collective-permute-done | bytes 40992 | tf_op jit(solution)/shard_map/ppermute | solution.py:54
  15.0 1.5 %shard_map.77 = (bf16[13,128,256]{2,1,0:T(8,128)(2,1)S(1)}, f32[16,256]{1,0:T(8,128)S(1)}, f32[8,128]{1,0:T(8,128)S(1)}) custom-call(f32[8,128]{1,0:T(8,128)S(1)} %get-tuple-element.28.refs_0_.refs_3_, bf16[2,384,384]{2,1,0:T(8,128)(2,1)S(1)} %get-tuple-element.29.refs_1_, f32[8,128,256]{2,1,0:T(8,128)S(1)} %get-tuple-element.36.refs_2_, ...), custom_call_target="tpu_custom_call" | custom-call | flops 1500000000 | bytes 3750000 | tf_op jit(solution)/shard_map/pallas_call | solution.py:64
  16.6 9.9 %all_to_all.11 = f32[16,1,256]{2,1,0:T(1,128)S(1)} all-to-all(f32[16,1,256]{2,1,0:T(1,128)S(1)} %copy.8), channel_id=1, replica_groups=mesh['groups'=2,'tm'=4,'space'=2,'chan'=2] {'tm','space','chan'}, dimensions={0} | all-to-all | bytes 32768 | tf_op jit(solution)/shard_map/all_to_all | solution.py:584
  26.5 1.5 %shard_map.78 = (bf16[8,16,128]{2,1,0:T(8,128)(2,1)S(1)}, bf16[8,16,128]{2,1,0:T(8,128)(2,1)S(1)}, bf16[8,16,128]{2,1,0:T(8,128)(2,1)S(1)}, bf16[8,16,128]{2,1,0:T(8,128)(2,1)S(1)}) custom-call(f32[16,256]{1,0:T(8,128)S(1)} %get-tuple-element.41.refs_0_, f32[8,128]{1,0:T(8,128)S(1)} %get-tuple-element.42.refs_1_, f32[16,256]{1,0:T(8,128)S(1)} %bitcast.12, ...), custom_call_target="tpu_custom_call" | custom-call | tf_op jit(solution)/shard_map/pallas_call | solution.py:64
  28.1 2.3 %collective-permute-start.8 = (bf16[8,16,128]{2,1,0:T(8,128)(2,1)S(1)}, bf16[8,16,128]{2,1,0:T(8,128)(2,1)S(1)}, u32[]{:S(2)}, u32[]{:S(2)}) collective-permute-start(bf16[8,16,128]{2,1,0:T(8,128)(2,1)S(1)} %get-tuple-element.46), channel_id=1, source_target_pairs={{0,12},{4,8},{8,4},{12,0},{1,13},{5,9},{9,5},{13,1},{2,14},{6,10},... | collective-permute-start | bytes 98312 | tf_op jit(solution)/shard_map/ppermute | solution.py:600
  30.4 1.1 %collective-permute-start.9 = (bf16[8,16,128]{2,1,0:T(8,128)(2,1)S(1)}, bf16[8,16,128]{2,1,0:T(8,128)(2,1)S(1)}, u32[]{:S(2)}, u32[]{:S(2)}) collective-permute-start(bf16[8,16,128]{2,1,0:T(8,128)(2,1)S(1)} %get-tuple-element.47), channel_id=1, source_target_pairs={{0,4},{4,0},{8,12},{12,8},{1,5},{5,1},{9,13},{13,9},{2,6},{6,2},{1... | collective-permute-start | bytes 98312 | tf_op jit(solution)/shard_map/ppermute | solution.py:600
  31.6 1.7 %collective-permute-done.10.refs_3_ = bf16[8,16,128]{2,1,0:T(8,128)(2,1)S(1)} collective-permute-done((bf16[8,16,128]{2,1,0:T(8,128)(2,1)S(1)}, bf16[8,16,128]{2,1,0:T(8,128)(2,1)S(1)}, u32[]{:S(2)}, u32[]{:S(2)}) %collective-permute-start.10) | collective-permute-done | bytes 32800 | tf_op jit(solution)/shard_map/ppermute | solution.py:600
  33.2 0.7 %collective-permute-done.8.refs_1_ = bf16[8,16,128]{2,1,0:T(8,128)(2,1)S(1)} collective-permute-done((bf16[8,16,128]{2,1,0:T(8,128)(2,1)S(1)}, bf16[8,16,128]{2,1,0:T(8,128)(2,1)S(1)}, u32[]{:S(2)}, u32[]{:S(2)}) %collective-permute-start.8) | collective-permute-done | bytes 32800 | tf_op jit(solution)/shard_map/ppermute | solution.py:600
  33.9 0.4 %collective-permute-done.9.refs_2_ = bf16[8,16,128]{2,1,0:T(8,128)(2,1)S(1)} collective-permute-done((bf16[8,16,128]{2,1,0:T(8,128)(2,1)S(1)}, bf16[8,16,128]{2,1,0:T(8,128)(2,1)S(1)}, u32[]{:S(2)}, u32[]{:S(2)}) %collective-permute-start.9) | collective-permute-done | bytes 32800 | tf_op jit(solution)/shard_map/ppermute | solution.py:600
  34.3 0.7 %shard_map.79 = bf16[16,16,128]{2,1,0:T(8,128)(2,1)} custom-call(bf16[8,16,128]{2,1,0:T(8,128)(2,1)S(1)} %get-tuple-element.45.refs_0_, bf16[8,16,128]{2,1,0:T(8,128)(2,1)S(1)} %collective-permute-done.8.refs_1_, bf16[8,16,128]{2,1,0:T(8,128)(2,1)S(1)} %collective-permute-done.9.refs_2_, bf16[8,16,128]{2,1,0:T(8,128)(2,1)S(1)} %collective-permute-done.10.refs_3_), custom_call_target="tpu_custom_call" | custom-call | tf_op jit(solution)/shard_map/pallas_call | solution.py:604
  (22 shorter events, 0.3 us)
Async XLA Ops:
  0.0 1.0 %copy-start.1 = (bf16[64,2,8,256]{3,2,1,0:T(8,128)(2,1)S(1)}, bf16[64,2,8,256]{3,2,1,0:T(8,128)(2,1)}, u32[]{:S(2)}) copy-start(bf16[64,2,8,256]{3,2,1,0:T(8,128)(2,1)} %param.7) | copy-start | bytes 1572868
  1.0 6.3 %copy-start = (bf16[3,3,3,128,128]{4,3,2,1,0:T(8,128)(2,1)S(1)}, bf16[3,3,3,128,128]{4,3,2,1,0:T(8,128)(2,1)}, u32[]{:S(2)}) copy-start(bf16[3,3,3,128,128]{4,3,2,1,0:T(8,128)(2,1)} %refs_5_.1) | copy-start | bytes 2654212
  1.0 6.3 %copy-start.2 = (bf16[2,2,128,32]{2,3,1,0:T(8,128)(2,1)S(1)}, bf16[2,2,128,32]{2,3,1,0:T(8,128)(2,1)}, u32[]{:S(2)}) copy-start(bf16[2,2,128,32]{2,3,1,0:T(8,128)(2,1)} %param.12) | copy-start | bytes 98308
  1.0 6.3 %copy-start.6 = (f32[128]{0:T(128)S(1)}, f32[128]{0:T(128)}, u32[]{:S(2)}) copy-start(f32[128]{0:T(128)} %param.11) | copy-start | bytes 1540
  1.6 7.5 %collective-permute-start = (bf16[1024,256]{1,0:T(8,128)(2,1)S(1)}, bf16[1024,256]{1,0:T(8,128)(2,1)S(1)}, u32[]{:S(2)}, u32[]{:S(2)}) collective-permute-start(bf16[1024,256]{1,0:T(8,128)(2,1)S(1)} %get-tuple-element.27.refs_6_), channel_id=1, source_target_pairs={{0,1},{1,0},{2,3},{3,2},{4,5},{5,4},{6,7},{7,6},{8,9},{9,8},{10,11... | collective-permute-start | bytes 1572872 | tf_op jit(solution)/shard_map/ppermute | solution.py:548
  2.1 7.0 %collective-permute-start.1 = (bf16[128,256]{1,0:T(8,128)(2,1)S(1)}, bf16[128,256]{1,0:T(8,128)(2,1)S(1)}, u32[]{:S(2)}, u32[]{:S(2)}) collective-permute-start(bf16[128,256]{1,0:T(8,128)(2,1)S(1)} %get-tuple-element.34), channel_id=1, source_target_pairs={{0,2},{2,0},{1,3},{3,1},{4,6},{6,4},{5,7},{7,5},{8,10},{10,8},{9,1... | collective-permute-start | bytes 196616 | tf_op jit(solution)/shard_map/ppermute | solution.py:37
  4.7 8.9 %collective-permute-start.3 = (bf16[512,256]{1,0:T(8,128)(2,1)S(1)}, bf16[512,256]{1,0:T(8,128)(2,1)S(1)}, u32[]{:S(2)}, u32[]{:S(2)}) collective-permute-start(bf16[512,256]{1,0:T(8,128)(2,1)S(1)} %get-tuple-element.33.refs_3_.refs_7_), channel_id=1, source_target_pairs={{1,5},{4,0},{5,9},{8,4},{9,13},{12,8},{13,12},{0,1},{3,7},{6,2},{7... | collective-permute-start | bytes 786440 | tf_op jit(solution)/shard_map/ppermute | solution.py:54
  4.8 9.0 %collective-permute-start.4 = (bf16[512,256]{1,0:T(8,128)(2,1)S(1)}, bf16[512,256]{1,0:T(8,128)(2,1)S(1)}, u32[]{:S(2)}, u32[]{:S(2)}) collective-permute-start(bf16[512,256]{1,0:T(8,128)(2,1)S(1)} %get-tuple-element.32.refs_2_.refs_6_), channel_id=1, source_target_pairs={{0,5},{5,0},{4,9},{9,4},{8,13},{13,8},{1,3},{12,14},{2,7},{7,2},{6... | collective-permute-start | bytes 786440 | tf_op jit(solution)/shard_map/ppermute | solution.py:54
  7.3 0.7 %copy-start.3 = (s32[2]{0:T(128)S(1)}, s32[2]{0:T(128)}, u32[]{:S(2)}) copy-start(s32[2]{0:T(128)} %param.8) | copy-start | bytes 28
  7.3 0.7 %copy-start.4 = (s32[1,8,1]{1,2,0:T(1,128)S(1)}, s32[1,8,1]{1,2,0:T(1,128)}, u32[]{:S(2)}) copy-start(s32[1,8,1]{1,2,0:T(1,128)} %param.13) | copy-start | bytes 100
  7.3 0.7 %copy-start.5 = (f32[128]{0:T(128)S(1)}, f32[128]{0:T(128)}, u32[]{:S(2)}) copy-start(f32[128]{0:T(128)} %param.10) | copy-start | bytes 1540
  9.3 1.7 %collective-permute-start.2 = (bf16[128,256]{1,0:T(8,128)(2,1)S(1)}, bf16[128,256]{1,0:T(8,128)(2,1)S(1)}, u32[]{:S(2)}, u32[]{:S(2)}) collective-permute-start(bf16[128,256]{1,0:T(8,128)(2,1)S(1)} %get-tuple-element.35.refs_5_.refs_9_), channel_id=1, source_target_pairs={{0,1},{1,0},{2,3},{3,2},{4,5},{5,4},{6,7},{7,6},{8,9},{9,8},{10,11... | collective-permute-start | bytes 196616 | tf_op jit(solution)/shard_map/ppermute | solution.py:555
  9.3 5.0 %collective-permute-start.6 = (bf16[80,256]{1,0:T(8,128)(2,1)S(1)}, bf16[80,256]{1,0:T(8,128)(2,1)S(1)}, u32[]{:S(2)}, u32[]{:S(2)}) collective-permute-start(bf16[80,256]{1,0:T(8,128)(2,1)S(1)} %get-tuple-element.39.refs_5_), channel_id=1, source_target_pairs={{0,5},{5,0},{4,9},{9,4},{8,13},{13,8},{1,3},{12,14},{2,7},{7,2},{6... | collective-permute-start | bytes 122888 | tf_op jit(solution)/shard_map/ppermute | solution.py:54
  11.0 4.0 %collective-permute-start.5 = (bf16[80,256]{1,0:T(8,128)(2,1)S(1)}, bf16[80,256]{1,0:T(8,128)(2,1)S(1)}, u32[]{:S(2)}, u32[]{:S(2)}) collective-permute-start(bf16[80,256]{1,0:T(8,128)(2,1)S(1)} %get-tuple-element.40), channel_id=1, source_target_pairs={{1,5},{4,0},{5,9},{8,4},{9,13},{12,8},{13,12},{0,1},{3,7},{6,2},{7... | collective-permute-start | bytes 122888 | tf_op jit(solution)/shard_map/ppermute | solution.py:54
  16.5 10.0 %collective-permute-start.7 = (bf16[13,128,256]{2,1,0:T(8,128)(2,1)S(1)}, bf16[13,128,256]{2,1,0:T(8,128)(2,1)S(1)}, u32[]{:S(2)}, u32[]{:S(2)}) collective-permute-start(bf16[13,128,256]{2,1,0:T(8,128)(2,1)S(1)} %get-tuple-element.44.refs_5_), channel_id=1, source_target_pairs={{0,1},{1,0},{2,3},{3,2},{4,5},{5,4},{6,7},{7,6},{8,9},{9,8},{10,11... | collective-permute-start | bytes 2555912 | tf_op jit(solution)/shard_map/ppermute | solution.py:583
  28.0 5.2 %collective-permute-start.10 = (bf16[8,16,128]{2,1,0:T(8,128)(2,1)S(1)}, bf16[8,16,128]{2,1,0:T(8,128)(2,1)S(1)}, u32[]{:S(2)}, u32[]{:S(2)}) collective-permute-start(bf16[8,16,128]{2,1,0:T(8,128)(2,1)S(1)} %get-tuple-element.48), channel_id=1, source_target_pairs={{0,8},{4,12},{8,0},{12,4},{1,9},{5,13},{9,1},{13,5},{2,10},{6,14},... | collective-permute-start | bytes 98312 | tf_op jit(solution)/shard_map/ppermute | solution.py:600
  28.1 5.8 %collective-permute-start.8 = (bf16[8,16,128]{2,1,0:T(8,128)(2,1)S(1)}, bf16[8,16,128]{2,1,0:T(8,128)(2,1)S(1)}, u32[]{:S(2)}, u32[]{:S(2)}) collective-permute-start(bf16[8,16,128]{2,1,0:T(8,128)(2,1)S(1)} %get-tuple-element.46), channel_id=1, source_target_pairs={{0,12},{4,8},{8,4},{12,0},{1,13},{5,9},{9,5},{13,1},{2,14},{6,10},... | collective-permute-start | bytes 98312 | tf_op jit(solution)/shard_map/ppermute | solution.py:600
  30.4 3.9 %collective-permute-start.9 = (bf16[8,16,128]{2,1,0:T(8,128)(2,1)S(1)}, bf16[8,16,128]{2,1,0:T(8,128)(2,1)S(1)}, u32[]{:S(2)}, u32[]{:S(2)}) collective-permute-start(bf16[8,16,128]{2,1,0:T(8,128)(2,1)S(1)} %get-tuple-element.47), channel_id=1, source_target_pairs={{0,4},{4,0},{8,12},{12,8},{1,5},{5,1},{9,13},{13,9},{2,6},{6,2},{1... | collective-permute-start | bytes 98312 | tf_op jit(solution)/shard_map/ppermute | solution.py:600

commit v8 on v7

--- a/solution.py
+++ b/solution.py
@@ -132,7 +132,8 @@
         for h in range(halos):
             out_ref[h * half : (h + 1) * half, :] = halo_refs[h][n * half : (n + 1) * half, :]
         number = jnp.where(frame == 0, ids[0], ids[1])
-        out_ref[halos * half :, :] = jnp.where(place == count, number + 1.0, tail).astype(BF16)
+        if n == 1:
+            out_ref[halos * half :, :] = jnp.where(place == count, number + 1.0, tail).astype(BF16)
 
 
 def weights_kernel(
@@ -549,7 +550,7 @@
     message_halo = jax.ShapeDtypeStruct((halos * half + ID_ROWS, columns), BF16)
     *own_halos, cross_halo, same_halo = whole_call(
         lambda *refs: halo_kernel(halos, capacity, *refs[: 1 + halos], *refs[2 + halos :]),
-        (pair,) * halos + (message_halo, message_halo),
+        (pair,) * halos + (jax.ShapeDtypeStruct((halos * half, columns), BF16), message_halo),
         (small, *own_halos, other),
     )
     other_halos = [lax.ppermute(halo, "chan", turn) for halo in own_halos]
@@ -575,7 +576,7 @@
             jax.ShapeDtypeStruct((8, CHANNELS), F32),
         ),
         (
-            small, late_weight, part, extra, extra_sums, cross_halo, *here, late_own, late_other, late_own_halo, late_other_halo,
+            small, late_weight, part, extra, extra_sums, same_halo, *here, late_own, late_other, late_own_halo, late_other_halo,
         ),
         [pltpu.VMEM((rows + 2, CHANNELS, columns), BF16)],
         flops=1500000000,

time: 35.2 us -> 35.1 us (level)
  waiting for transfers between devices: 4.54 us -> 3.82 us
    ppermute x4, waiting for transfers between devices: 1.76 us -> 1.05 us  [slab_swap(): return lax.ppermute(value, PART, flat_pairs(sizes, pairs))]
  transfers between devices with their start and end apart: 11 -> 11, of which waited for: 7 -> 5; matrix products, arithmetic and copies ran while one was open for 0% -> 0% of each run, Pallas kernels for 10% -> 10%
where the time goes in v8:
time: 35.1 us; the launch traced here: 34.9 us
  starting transfers between devices  11.4 us (32%)
  blocking collectives  10.2 us (29%)
  Pallas kernels  7.58 us (22%)
  waiting for transfers between devices  3.82 us (11%)
  local copies, waits for them, and re-layouts  1.73 us (5%)
    all_to_all x1, blocking collectives, shards(): lax.all_to_all(message, PART, split_axis=0, concat_axis=0, tiled=True)  10.2 us
    pallas_call x6, Pallas kernels, whole_call(): pl.pallas_call(turned, out_shape=out_shape, in_specs=[specs[n] for n in t...  6.92 us
    ppermute x4, starting transfers between devices, slab_swap(): return lax.ppermute(value, PART, flat_pairs(sizes, pairs))  4.67 us
    ppermute x3, starting transfers between devices, shards(): lax.ppermute(sends[d], 'tm', [(t, t ^ d) for t in range(slabs)])  3.55 us
    ppermute x3, waiting for transfers between devices, shards(): lax.ppermute(sends[d], 'tm', [(t, t ^ d) for t in range(slabs)])  2.76 us
    ppermute x1, starting transfers between devices, space_swap(): return lax.ppermute(value, PART, flat_pairs(sizes, pairs))  2.56 us
    unnamed x15, local copies, waits for them, and re-layouts  1.71 us
    ppermute x4, waiting for transfers between devices, slab_swap(): return lax.ppermute(value, PART, flat_pairs(sizes, pairs))  1.05 us
  transfers between devices with their start and end apart: 11, of which 5 were waited for; matrix products, arithmetic and copies ran while one was open for 0% of the time, Pallas kernels for 10%

profile of v8, /device:TPU:0, one launch (start us, length us, event | category | flops | bytes accessed | tf_op | source)
XLA Modules:
  0.0 34.9 jit_solution(10925040007965803084)
XLA Ops:
  0.0 1.0 %copy-done.1 = bf16[64,2,8,256]{3,2,1,0:T(8,128)(2,1)S(1)} copy-done((bf16[64,2,8,256]{3,2,1,0:T(8,128)(2,1)S(1)}, bf16[64,2,8,256]{3,2,1,0:T(8,128)(2,1)}, u32[]{:S(2)}) %copy-start.1) | copy-done | bytes 524312
  1.0 0.5 %shard_map.73 = (bf16[512,256]{1,0:T(8,128)(2,1)S(1)}, bf16[512,256]{1,0:T(8,128)(2,1)S(1)}, bf16[1024,256]{1,0:T(8,128)(2,1)S(1)}, bf16[128,256]{1,0:T(8,128)(2,1)S(1)}) custom-call(bf16[1024,256]{1,0:T(8,128)(2,1)S(1)} %bitcast.13), custom_call_target="tpu_custom_call" | custom-call | flops 3000000000 | bytes 7500000 | tf_op jit(solution)/shard_map/pallas_call | solution.py:64
  1.6 0.5 %collective-permute-start = (bf16[1024,256]{1,0:T(8,128)(2,1)S(1)}, bf16[1024,256]{1,0:T(8,128)(2,1)S(1)}, u32[]{:S(2)}, u32[]{:S(2)}) collective-permute-start(bf16[1024,256]{1,0:T(8,128)(2,1)S(1)} %get-tuple-element.27.refs_6_), channel_id=1, source_target_pairs={{0,1},{1,0},{2,3},{3,2},{4,5},{5,4},{6,7},{7,6},{8,9},{9,8},{10,11... | collective-permute-start | bytes 1572872 | tf_op jit(solution)/shard_map/ppermute | solution.py:549
  2.1 2.6 %collective-permute-start.1 = (bf16[128,256]{1,0:T(8,128)(2,1)S(1)}, bf16[128,256]{1,0:T(8,128)(2,1)S(1)}, u32[]{:S(2)}, u32[]{:S(2)}) collective-permute-start(bf16[128,256]{1,0:T(8,128)(2,1)S(1)} %get-tuple-element.34), channel_id=1, source_target_pairs={{0,2},{2,0},{1,3},{3,1},{4,6},{6,4},{5,7},{7,5},{8,10},{10,8},{9,1... | collective-permute-start | bytes 196616 | tf_op jit(solution)/shard_map/ppermute | solution.py:37
  4.7 0.2 collective-permute-start.3
  4.8 2.5 %collective-permute-start.4 = (bf16[512,256]{1,0:T(8,128)(2,1)S(1)}, bf16[512,256]{1,0:T(8,128)(2,1)S(1)}, u32[]{:S(2)}, u32[]{:S(2)}) collective-permute-start(bf16[512,256]{1,0:T(8,128)(2,1)S(1)} %get-tuple-element.32.refs_2_.refs_6_), channel_id=1, source_target_pairs={{0,5},{5,0},{4,9},{9,4},{8,13},{13,8},{1,3},{12,14},{2,7},{7,2},{6... | collective-permute-start | bytes 786440 | tf_op jit(solution)/shard_map/ppermute | solution.py:54
  7.4 0.6 %copy-done.3 = s32[2]{0:T(128)S(1)} copy-done((s32[2]{0:T(128)S(1)}, s32[2]{0:T(128)}, u32[]{:S(2)}) %copy-start.3) | copy-done | bytes 32
  8.0 1.1 %shard_map.74 = (bf16[384,768]{1,0:T(8,128)(2,1)S(1)}, bf16[2,384,384]{2,1,0:T(8,128)(2,1)S(1)}, bf16[384,384]{1,0:T(8,128)(2,1)S(1)}, f32[8,128]{1,0:T(8,128)S(1)}, bf16[32,512]{1,0:T(8,128)(2,1)S(1)}) custom-call(s32[1,2]{1,0:T(1,128)S(1)} %bitcast.15, s32[1,8]{1,0:T(1,128)S(1)} %bitcast.16, f32[1,128]{1,0:T(1,128)S(1)} %bitcast.17, ...), custom_call_target="tpu_custom_call" | custom-call | flops 1200000000 | bytes 3000000 | tf_op jit(solution)/shard_map/pallas_call | solution.py:64
  9.1 0.2 shard_map.75
  9.3 0.5 %collective-permute-start.5 = (bf16[80,256]{1,0:T(8,128)(2,1)S(1)}, bf16[80,256]{1,0:T(8,128)(2,1)S(1)}, u32[]{:S(2)}, u32[]{:S(2)}) collective-permute-start(bf16[80,256]{1,0:T(8,128)(2,1)S(1)} %get-tuple-element.39.refs_5_), channel_id=1, source_target_pairs={{1,5},{4,0},{5,9},{8,4},{9,13},{12,8},{13,12},{0,1},{3,7},{6,2},{7... | collective-permute-start | bytes 122888 | tf_op jit(solution)/shard_map/ppermute | solution.py:54
  9.8 1.5 %collective-permute-start.6 = (bf16[64,256]{1,0:T(8,128)(2,1)S(1)}, bf16[64,256]{1,0:T(8,128)(2,1)S(1)}, u32[]{:S(2)}, u32[]{:S(2)}) collective-permute-start(bf16[64,256]{1,0:T(8,128)(2,1)S(1)} %get-tuple-element.40), channel_id=1, source_target_pairs={{0,5},{5,0},{4,9},{9,4},{8,13},{13,8},{1,3},{12,14},{2,7},{7,2},{6... | collective-permute-start | bytes 98312 | tf_op jit(solution)/shard_map/ppermute | solution.py:54
  11.4 2.2 %shard_map.76 = (f32[8,128,256]{2,1,0:T(8,128)S(1)}, bf16[4,128,256]{2,1,0:T(8,128)(2,1)S(1)}, f32[8,128]{1,0:T(8,128)S(1)}) custom-call(bf16[384,768]{1,0:T(8,128)(2,1)S(1)} %get-tuple-element.30.refs_0_, bf16[384,384]{1,0:T(8,128)(2,1)S(1)} %get-tuple-element.31.refs_1_, bf16[512,256]{1,0:T(8,128)(2,1)S(1)} %get-tuple-element.32.refs_2_.refs_6_, ...), custom_call_target="tpu_custom_call" | custom-call | flops 1800000000 | bytes 4500000 | tf_op jit(solution)/shard_map/pallas_call | solution.py:64
  13.6 0.6 %collective-permute-done.4.refs_12_ = bf16[512,256]{1,0:T(8,128)(2,1)S(1)} collective-permute-done((bf16[512,256]{1,0:T(8,128)(2,1)S(1)}, bf16[512,256]{1,0:T(8,128)(2,1)S(1)}, u32[]{:S(2)}, u32[]{:S(2)}) %collective-permute-start.4) | collective-permute-done | bytes 262176 | tf_op jit(solution)/shard_map/ppermute | solution.py:54
  14.2 0.5 %collective-permute-done.6.refs_14_ = bf16[64,256]{1,0:T(8,128)(2,1)S(1)} collective-permute-done((bf16[64,256]{1,0:T(8,128)(2,1)S(1)}, bf16[64,256]{1,0:T(8,128)(2,1)S(1)}, u32[]{:S(2)}, u32[]{:S(2)}) %collective-permute-start.6) | collective-permute-done | bytes 32800 | tf_op jit(solution)/shard_map/ppermute | solution.py:54
  14.7 1.4 %shard_map.77 = (bf16[13,128,256]{2,1,0:T(8,128)(2,1)S(1)}, f32[16,256]{1,0:T(8,128)S(1)}, f32[8,128]{1,0:T(8,128)S(1)}) custom-call(f32[8,128]{1,0:T(8,128)S(1)} %get-tuple-element.28.refs_0_.refs_3_, bf16[2,384,384]{2,1,0:T(8,128)(2,1)S(1)} %get-tuple-element.29.refs_1_, f32[8,128,256]{2,1,0:T(8,128)S(1)} %get-tuple-element.36.refs_2_, ...), custom_call_target="tpu_custom_call" | custom-call | flops 1500000000 | bytes 3750000 | tf_op jit(solution)/shard_map/pallas_call | solution.py:64
  16.2 10.2 %all_to_all.11 = f32[16,1,256]{2,1,0:T(1,128)S(1)} all-to-all(f32[16,1,256]{2,1,0:T(1,128)S(1)} %copy.8), channel_id=1, replica_groups=mesh['groups'=2,'tm'=4,'space'=2,'chan'=2] {'tm','space','chan'}, dimensions={0} | all-to-all | bytes 32768 | tf_op jit(solution)/shard_map/all_to_all | solution.py:585
  26.4 1.5 %shard_map.78 = (bf16[8,16,128]{2,1,0:T(8,128)(2,1)S(1)}, bf16[8,16,128]{2,1,0:T(8,128)(2,1)S(1)}, bf16[8,16,128]{2,1,0:T(8,128)(2,1)S(1)}, bf16[8,16,128]{2,1,0:T(8,128)(2,1)S(1)}) custom-call(f32[16,256]{1,0:T(8,128)S(1)} %get-tuple-element.41.refs_0_, f32[8,128]{1,0:T(8,128)S(1)} %get-tuple-element.42.refs_1_, f32[16,256]{1,0:T(8,128)S(1)} %bitcast.12, ...), custom_call_target="tpu_custom_call" | custom-call | tf_op jit(solution)/shard_map/pallas_call | solution.py:64
  27.9 0.1 collective-permute-start.10
  28.0 2.3 %collective-permute-start.8 = (bf16[8,16,128]{2,1,0:T(8,128)(2,1)S(1)}, bf16[8,16,128]{2,1,0:T(8,128)(2,1)S(1)}, u32[]{:S(2)}, u32[]{:S(2)}) collective-permute-start(bf16[8,16,128]{2,1,0:T(8,128)(2,1)S(1)} %get-tuple-element.46), channel_id=1, source_target_pairs={{0,12},{4,8},{8,4},{12,0},{1,13},{5,9},{9,5},{13,1},{2,14},{6,10},... | collective-permute-start | bytes 98312 | tf_op jit(solution)/shard_map/ppermute | solution.py:601
  30.3 1.1 %collective-permute-start.9 = (bf16[8,16,128]{2,1,0:T(8,128)(2,1)S(1)}, bf16[8,16,128]{2,1,0:T(8,128)(2,1)S(1)}, u32[]{:S(2)}, u32[]{:S(2)}) collective-permute-start(bf16[8,16,128]{2,1,0:T(8,128)(2,1)S(1)} %get-tuple-element.47), channel_id=1, source_target_pairs={{0,4},{4,0},{8,12},{12,8},{1,5},{5,1},{9,13},{13,9},{2,6},{6,2},{1... | collective-permute-start | bytes 98312 | tf_op jit(solution)/shard_map/ppermute | solution.py:601
  31.5 1.7 %collective-permute-done.10.refs_3_ = bf16[8,16,128]{2,1,0:T(8,128)(2,1)S(1)} collective-permute-done((bf16[8,16,128]{2,1,0:T(8,128)(2,1)S(1)}, bf16[8,16,128]{2,1,0:T(8,128)(2,1)S(1)}, u32[]{:S(2)}, u32[]{:S(2)}) %collective-permute-start.10) | collective-permute-done | bytes 32800 | tf_op jit(solution)/shard_map/ppermute | solution.py:601
  33.1 0.7 %collective-permute-done.8.refs_1_ = bf16[8,16,128]{2,1,0:T(8,128)(2,1)S(1)} collective-permute-done((bf16[8,16,128]{2,1,0:T(8,128)(2,1)S(1)}, bf16[8,16,128]{2,1,0:T(8,128)(2,1)S(1)}, u32[]{:S(2)}, u32[]{:S(2)}) %collective-permute-start.8) | collective-permute-done | bytes 32800 | tf_op jit(solution)/shard_map/ppermute | solution.py:601
  33.8 0.4 %collective-permute-done.9.refs_2_ = bf16[8,16,128]{2,1,0:T(8,128)(2,1)S(1)} collective-permute-done((bf16[8,16,128]{2,1,0:T(8,128)(2,1)S(1)}, bf16[8,16,128]{2,1,0:T(8,128)(2,1)S(1)}, u32[]{:S(2)}, u32[]{:S(2)}) %collective-permute-start.9) | collective-permute-done | bytes 32800 | tf_op jit(solution)/shard_map/ppermute | solution.py:601
  34.2 0.7 %shard_map.79 = bf16[16,16,128]{2,1,0:T(8,128)(2,1)} custom-call(bf16[8,16,128]{2,1,0:T(8,128)(2,1)S(1)} %get-tuple-element.45.refs_0_, bf16[8,16,128]{2,1,0:T(8,128)(2,1)S(1)} %collective-permute-done.8.refs_1_, bf16[8,16,128]{2,1,0:T(8,128)(2,1)S(1)} %collective-permute-done.9.refs_2_, bf16[8,16,128]{2,1,0:T(8,128)(2,1)S(1)} %collective-permute-done.10.refs_3_), custom_call_target="tpu_custom_call" | custom-call | tf_op jit(solution)/shard_map/pallas_call | solution.py:605
  (22 shorter events, 0.2 us)
Async XLA Ops:
  0.0 1.0 %copy-start.1 = (bf16[64,2,8,256]{3,2,1,0:T(8,128)(2,1)S(1)}, bf16[64,2,8,256]{3,2,1,0:T(8,128)(2,1)}, u32[]{:S(2)}) copy-start(bf16[64,2,8,256]{3,2,1,0:T(8,128)(2,1)} %param.7) | copy-start | bytes 1572868
  1.0 6.3 %copy-start = (bf16[3,3,3,128,128]{4,3,2,1,0:T(8,128)(2,1)S(1)}, bf16[3,3,3,128,128]{4,3,2,1,0:T(8,128)(2,1)}, u32[]{:S(2)}) copy-start(bf16[3,3,3,128,128]{4,3,2,1,0:T(8,128)(2,1)} %refs_5_.1) | copy-start | bytes 2654212
  1.0 6.3 %copy-start.2 = (bf16[2,2,128,32]{2,3,1,0:T(8,128)(2,1)S(1)}, bf16[2,2,128,32]{2,3,1,0:T(8,128)(2,1)}, u32[]{:S(2)}) copy-start(bf16[2,2,128,32]{2,3,1,0:T(8,128)(2,1)} %param.12) | copy-start | bytes 98308
  1.0 6.3 %copy-start.6 = (f32[128]{0:T(128)S(1)}, f32[128]{0:T(128)}, u32[]{:S(2)}) copy-start(f32[128]{0:T(128)} %param.11) | copy-start | bytes 1540
  1.6 7.5 %collective-permute-start = (bf16[1024,256]{1,0:T(8,128)(2,1)S(1)}, bf16[1024,256]{1,0:T(8,128)(2,1)S(1)}, u32[]{:S(2)}, u32[]{:S(2)}) collective-permute-start(bf16[1024,256]{1,0:T(8,128)(2,1)S(1)} %get-tuple-element.27.refs_6_), channel_id=1, source_target_pairs={{0,1},{1,0},{2,3},{3,2},{4,5},{5,4},{6,7},{7,6},{8,9},{9,8},{10,11... | collective-permute-start | bytes 1572872 | tf_op jit(solution)/shard_map/ppermute | solution.py:549
  2.1 7.0 %collective-permute-start.1 = (bf16[128,256]{1,0:T(8,128)(2,1)S(1)}, bf16[128,256]{1,0:T(8,128)(2,1)S(1)}, u32[]{:S(2)}, u32[]{:S(2)}) collective-permute-start(bf16[128,256]{1,0:T(8,128)(2,1)S(1)} %get-tuple-element.34), channel_id=1, source_target_pairs={{0,2},{2,0},{1,3},{3,1},{4,6},{6,4},{5,7},{7,5},{8,10},{10,8},{9,1... | collective-permute-start | bytes 196616 | tf_op jit(solution)/shard_map/ppermute | solution.py:37
  4.7 8.9 %collective-permute-start.3 = (bf16[512,256]{1,0:T(8,128)(2,1)S(1)}, bf16[512,256]{1,0:T(8,128)(2,1)S(1)}, u32[]{:S(2)}, u32[]{:S(2)}) collective-permute-start(bf16[512,256]{1,0:T(8,128)(2,1)S(1)} %get-tuple-element.33.refs_3_.refs_7_), channel_id=1, source_target_pairs={{1,5},{4,0},{5,9},{8,4},{9,13},{12,8},{13,12},{0,1},{3,7},{6,2},{7... | collective-permute-start | bytes 786440 | tf_op jit(solution)/shard_map/ppermute | solution.py:54
  4.8 9.3 %collective-permute-start.4 = (bf16[512,256]{1,0:T(8,128)(2,1)S(1)}, bf16[512,256]{1,0:T(8,128)(2,1)S(1)}, u32[]{:S(2)}, u32[]{:S(2)}) collective-permute-start(bf16[512,256]{1,0:T(8,128)(2,1)S(1)} %get-tuple-element.32.refs_2_.refs_6_), channel_id=1, source_target_pairs={{0,5},{5,0},{4,9},{9,4},{8,13},{13,8},{1,3},{12,14},{2,7},{7,2},{6... | collective-permute-start | bytes 786440 | tf_op jit(solution)/shard_map/ppermute | solution.py:54
  7.3 0.7 %copy-start.3 = (s32[2]{0:T(128)S(1)}, s32[2]{0:T(128)}, u32[]{:S(2)}) copy-start(s32[2]{0:T(128)} %param.8) | copy-start | bytes 28
  7.3 0.7 %copy-start.4 = (s32[1,8,1]{1,2,0:T(1,128)S(1)}, s32[1,8,1]{1,2,0:T(1,128)}, u32[]{:S(2)}) copy-start(s32[1,8,1]{1,2,0:T(1,128)} %param.13) | copy-start | bytes 100
  7.3 0.7 %copy-start.5 = (f32[128]{0:T(128)S(1)}, f32[128]{0:T(128)}, u32[]{:S(2)}) copy-start(f32[128]{0:T(128)} %param.10) | copy-start | bytes 1540
  9.3 2.1 %collective-permute-start.2 = (bf16[128,256]{1,0:T(8,128)(2,1)S(1)}, bf16[128,256]{1,0:T(8,128)(2,1)S(1)}, u32[]{:S(2)}, u32[]{:S(2)}) collective-permute-start(bf16[128,256]{1,0:T(8,128)(2,1)S(1)} %get-tuple-element.35.refs_5_.refs_9_), channel_id=1, source_target_pairs={{0,1},{1,0},{2,3},{3,2},{4,5},{5,4},{6,7},{7,6},{8,9},{9,8},{10,11... | collective-permute-start | bytes 196616 | tf_op jit(solution)/shard_map/ppermute | solution.py:556
  9.3 5.3 %collective-permute-start.5 = (bf16[80,256]{1,0:T(8,128)(2,1)S(1)}, bf16[80,256]{1,0:T(8,128)(2,1)S(1)}, u32[]{:S(2)}, u32[]{:S(2)}) collective-permute-start(bf16[80,256]{1,0:T(8,128)(2,1)S(1)} %get-tuple-element.39.refs_5_), channel_id=1, source_target_pairs={{1,5},{4,0},{5,9},{8,4},{9,13},{12,8},{13,12},{0,1},{3,7},{6,2},{7... | collective-permute-start | bytes 122888 | tf_op jit(solution)/shard_map/ppermute | solution.py:54
  9.8 4.8 %collective-permute-start.6 = (bf16[64,256]{1,0:T(8,128)(2,1)S(1)}, bf16[64,256]{1,0:T(8,128)(2,1)S(1)}, u32[]{:S(2)}, u32[]{:S(2)}) collective-permute-start(bf16[64,256]{1,0:T(8,128)(2,1)S(1)} %get-tuple-element.40), channel_id=1, source_target_pairs={{0,5},{5,0},{4,9},{9,4},{8,13},{13,8},{1,3},{12,14},{2,7},{7,2},{6... | collective-permute-start | bytes 98312 | tf_op jit(solution)/shard_map/ppermute | solution.py:54
  16.1 10.3 %collective-permute-start.7 = (bf16[13,128,256]{2,1,0:T(8,128)(2,1)S(1)}, bf16[13,128,256]{2,1,0:T(8,128)(2,1)S(1)}, u32[]{:S(2)}, u32[]{:S(2)}) collective-permute-start(bf16[13,128,256]{2,1,0:T(8,128)(2,1)S(1)} %get-tuple-element.44.refs_5_), channel_id=1, source_target_pairs={{0,1},{1,0},{2,3},{3,2},{4,5},{5,4},{6,7},{7,6},{8,9},{9,8},{10,11... | collective-permute-start | bytes 2555912 | tf_op jit(solution)/shard_map/ppermute | solution.py:584
  27.9 5.2 %collective-permute-start.10 = (bf16[8,16,128]{2,1,0:T(8,128)(2,1)S(1)}, bf16[8,16,128]{2,1,0:T(8,128)(2,1)S(1)}, u32[]{:S(2)}, u32[]{:S(2)}) collective-permute-start(bf16[8,16,128]{2,1,0:T(8,128)(2,1)S(1)} %get-tuple-element.48), channel_id=1, source_target_pairs={{0,8},{4,12},{8,0},{12,4},{1,9},{5,13},{9,1},{13,5},{2,10},{6,14},... | collective-permute-start | bytes 98312 | tf_op jit(solution)/shard_map/ppermute | solution.py:601
  28.0 5.8 %collective-permute-start.8 = (bf16[8,16,128]{2,1,0:T(8,128)(2,1)S(1)}, bf16[8,16,128]{2,1,0:T(8,128)(2,1)S(1)}, u32[]{:S(2)}, u32[]{:S(2)}) collective-permute-start(bf16[8,16,128]{2,1,0:T(8,128)(2,1)S(1)} %get-tuple-element.46), channel_id=1, source_target_pairs={{0,12},{4,8},{8,4},{12,0},{1,13},{5,9},{9,5},{13,1},{2,14},{6,10},... | collective-permute-start | bytes 98312 | tf_op jit(solution)/shard_map/ppermute | solution.py:601
  30.3 3.9 %collective-permute-start.9 = (bf16[8,16,128]{2,1,0:T(8,128)(2,1)S(1)}, bf16[8,16,128]{2,1,0:T(8,128)(2,1)S(1)}, u32[]{:S(2)}, u32[]{:S(2)}) collective-permute-start(bf16[8,16,128]{2,1,0:T(8,128)(2,1)S(1)} %get-tuple-element.47), channel_id=1, source_target_pairs={{0,4},{4,0},{8,12},{12,8},{1,5},{5,1},{9,13},{13,9},{2,6},{6,2},{1... | collective-permute-start | bytes 98312 | tf_op jit(solution)/shard_map/ppermute | solution.py:601

commit v9 on v8

--- a/solution.py
+++ b/solution.py
@@ -544,7 +544,7 @@
             pltpu.SemaphoreType.DMA((5,)),
         ],
         [pl.BlockSpec(memory_space=pl.ANY)] * 5 + [VMEM] * 2,
-        1200000000,
+        4800000000,
     )
     other = lax.ppermute(both, "chan", turn)
     message_halo = jax.ShapeDtypeStruct((halos * half + ID_ROWS, columns), BF16)
@@ -566,7 +566,7 @@
         ),
         (local_weight, sum_weight, *here),
         [pltpu.VMEM((rows // 2 + 2, CHANNELS, columns), BF16)],
-        flops=1800000000,
+        flops=1000000,
     )
     conv, message, keys = whole_call(
         lambda *refs: late_kernel(rows, halos, slabs, *refs),

time: 35.1 us -> 35.1 us (level)
  no operation moved by 1% of the time
where the time goes in v9:
time: 35.1 us; the launch traced here: 34.9 us
  starting transfers between devices  11.4 us (32%)
  blocking collectives  10.2 us (29%)
  Pallas kernels  7.58 us (22%)
  waiting for transfers between devices  3.82 us (11%)
  local copies, waits for them, and re-layouts  1.73 us (5%)
    all_to_all x1, blocking collectives, shards(): lax.all_to_all(message, PART, split_axis=0, concat_axis=0, tiled=True)  10.2 us
    pallas_call x6, Pallas kernels, whole_call(): pl.pallas_call(turned, out_shape=out_shape, in_specs=[specs[n] for n in t...  6.92 us
    ppermute x4, starting transfers between devices, slab_swap(): return lax.ppermute(value, PART, flat_pairs(sizes, pairs))  4.67 us
    ppermute x3, starting transfers between devices, shards(): lax.ppermute(sends[d], 'tm', [(t, t ^ d) for t in range(slabs)])  3.55 us
    ppermute x3, waiting for transfers between devices, shards(): lax.ppermute(sends[d], 'tm', [(t, t ^ d) for t in range(slabs)])  2.76 us
    ppermute x1, starting transfers between devices, space_swap(): return lax.ppermute(value, PART, flat_pairs(sizes, pairs))  2.56 us
    unnamed x15, local copies, waits for them, and re-layouts  1.71 us
    ppermute x4, waiting for transfers between devices, slab_swap(): return lax.ppermute(value, PART, flat_pairs(sizes, pairs))  1.05 us
  transfers between devices with their start and end apart: 11, of which 5 were waited for; matrix products, arithmetic and copies ran while one was open for 0% of the time, Pallas kernels for 10%

profile of v9, /device:TPU:0, one launch (start us, length us, event | category | flops | bytes accessed | tf_op | source)
XLA Modules:
  0.0 34.9 jit_solution(10323139617605298532)
XLA Ops:
  0.0 1.0 %copy-done.1 = bf16[64,2,8,256]{3,2,1,0:T(8,128)(2,1)S(1)} copy-done((bf16[64,2,8,256]{3,2,1,0:T(8,128)(2,1)S(1)}, bf16[64,2,8,256]{3,2,1,0:T(8,128)(2,1)}, u32[]{:S(2)}) %copy-start.1) | copy-done | bytes 524312
  1.0 0.5 %shard_map.73 = (bf16[512,256]{1,0:T(8,128)(2,1)S(1)}, bf16[512,256]{1,0:T(8,128)(2,1)S(1)}, bf16[1024,256]{1,0:T(8,128)(2,1)S(1)}, bf16[128,256]{1,0:T(8,128)(2,1)S(1)}) custom-call(bf16[1024,256]{1,0:T(8,128)(2,1)S(1)} %bitcast.13), custom_call_target="tpu_custom_call" | custom-call | flops 3000000000 | bytes 7500000 | tf_op jit(solution)/shard_map/pallas_call | solution.py:64
  1.6 0.5 %collective-permute-start = (bf16[1024,256]{1,0:T(8,128)(2,1)S(1)}, bf16[1024,256]{1,0:T(8,128)(2,1)S(1)}, u32[]{:S(2)}, u32[]{:S(2)}) collective-permute-start(bf16[1024,256]{1,0:T(8,128)(2,1)S(1)} %get-tuple-element.27.refs_6_), channel_id=1, source_target_pairs={{0,1},{1,0},{2,3},{3,2},{4,5},{5,4},{6,7},{7,6},{8,9},{9,8},{10,11... | collective-permute-start | bytes 1572872 | tf_op jit(solution)/shard_map/ppermute | solution.py:549
  2.1 2.6 %collective-permute-start.1 = (bf16[128,256]{1,0:T(8,128)(2,1)S(1)}, bf16[128,256]{1,0:T(8,128)(2,1)S(1)}, u32[]{:S(2)}, u32[]{:S(2)}) collective-permute-start(bf16[128,256]{1,0:T(8,128)(2,1)S(1)} %get-tuple-element.34), channel_id=1, source_target_pairs={{0,2},{2,0},{1,3},{3,1},{4,6},{6,4},{5,7},{7,5},{8,10},{10,8},{9,1... | collective-permute-start | bytes 196616 | tf_op jit(solution)/shard_map/ppermute | solution.py:37
  4.7 0.2 collective-permute-start.3
  4.8 2.5 %collective-permute-start.4 = (bf16[512,256]{1,0:T(8,128)(2,1)S(1)}, bf16[512,256]{1,0:T(8,128)(2,1)S(1)}, u32[]{:S(2)}, u32[]{:S(2)}) collective-permute-start(bf16[512,256]{1,0:T(8,128)(2,1)S(1)} %get-tuple-element.32.refs_2_.refs_6_), channel_id=1, source_target_pairs={{0,5},{5,0},{4,9},{9,4},{8,13},{13,8},{1,3},{12,14},{2,7},{7,2},{6... | collective-permute-start | bytes 786440 | tf_op jit(solution)/shard_map/ppermute | solution.py:54
  7.4 0.6 %copy-done.3 = s32[2]{0:T(128)S(1)} copy-done((s32[2]{0:T(128)S(1)}, s32[2]{0:T(128)}, u32[]{:S(2)}) %copy-start.3) | copy-done | bytes 32
  8.0 1.1 %shard_map.74 = (bf16[384,768]{1,0:T(8,128)(2,1)S(1)}, bf16[2,384,384]{2,1,0:T(8,128)(2,1)S(1)}, bf16[384,384]{1,0:T(8,128)(2,1)S(1)}, f32[8,128]{1,0:T(8,128)S(1)}, bf16[32,512]{1,0:T(8,128)(2,1)S(1)}) custom-call(s32[1,2]{1,0:T(1,128)S(1)} %bitcast.15, s32[1,8]{1,0:T(1,128)S(1)} %bitcast.16, f32[1,128]{1,0:T(1,128)S(1)} %bitcast.17, ...), custom_call_target="tpu_custom_call" | custom-call | flops 4800000000 | bytes 12000000 | tf_op jit(solution)/shard_map/pallas_call | solution.py:64
  9.1 0.2 shard_map.75
  9.3 0.5 %collective-permute-start.5 = (bf16[80,256]{1,0:T(8,128)(2,1)S(1)}, bf16[80,256]{1,0:T(8,128)(2,1)S(1)}, u32[]{:S(2)}, u32[]{:S(2)}) collective-permute-start(bf16[80,256]{1,0:T(8,128)(2,1)S(1)} %get-tuple-element.39.refs_5_), channel_id=1, source_target_pairs={{1,5},{4,0},{5,9},{8,4},{9,13},{12,8},{13,12},{0,1},{3,7},{6,2},{7... | collective-permute-start | bytes 122888 | tf_op jit(solution)/shard_map/ppermute | solution.py:54
  9.8 1.5 %collective-permute-start.6 = (bf16[64,256]{1,0:T(8,128)(2,1)S(1)}, bf16[64,256]{1,0:T(8,128)(2,1)S(1)}, u32[]{:S(2)}, u32[]{:S(2)}) collective-permute-start(bf16[64,256]{1,0:T(8,128)(2,1)S(1)} %get-tuple-element.40), channel_id=1, source_target_pairs={{0,5},{5,0},{4,9},{9,4},{8,13},{13,8},{1,3},{12,14},{2,7},{7,2},{6... | collective-permute-start | bytes 98312 | tf_op jit(solution)/shard_map/ppermute | solution.py:54
  11.4 2.2 %shard_map.76 = (f32[8,128,256]{2,1,0:T(8,128)S(1)}, bf16[4,128,256]{2,1,0:T(8,128)(2,1)S(1)}, f32[8,128]{1,0:T(8,128)S(1)}) custom-call(bf16[384,768]{1,0:T(8,128)(2,1)S(1)} %get-tuple-element.30.refs_0_, bf16[384,384]{1,0:T(8,128)(2,1)S(1)} %get-tuple-element.31.refs_1_, bf16[512,256]{1,0:T(8,128)(2,1)S(1)} %get-tuple-element.32.refs_2_.refs_6_, ...), custom_call_target="tpu_custom_call" | custom-call | flops 1000000 | bytes 2500 | tf_op jit(solution)/shard_map/pallas_call | solution.py:64
  13.6 0.6 %collective-permute-done.4.refs_12_ = bf16[512,256]{1,0:T(8,128)(2,1)S(1)} collective-permute-done((bf16[512,256]{1,0:T(8,128)(2,1)S(1)}, bf16[512,256]{1,0:T(8,128)(2,1)S(1)}, u32[]{:S(2)}, u32[]{:S(2)}) %collective-permute-start.4) | collective-permute-done | bytes 262176 | tf_op jit(solution)/shard_map/ppermute | solution.py:54
  14.2 0.5 %collective-permute-done.6.refs_14_ = bf16[64,256]{1,0:T(8,128)(2,1)S(1)} collective-permute-done((bf16[64,256]{1,0:T(8,128)(2,1)S(1)}, bf16[64,256]{1,0:T(8,128)(2,1)S(1)}, u32[]{:S(2)}, u32[]{:S(2)}) %collective-permute-start.6) | collective-permute-done | bytes 32800 | tf_op jit(solution)/shard_map/ppermute | solution.py:54
  14.7 1.4 %shard_map.77 = (bf16[13,128,256]{2,1,0:T(8,128)(2,1)S(1)}, f32[16,256]{1,0:T(8,128)S(1)}, f32[8,128]{1,0:T(8,128)S(1)}) custom-call(f32[8,128]{1,0:T(8,128)S(1)} %get-tuple-element.28.refs_0_.refs_3_, bf16[2,384,384]{2,1,0:T(8,128)(2,1)S(1)} %get-tuple-element.29.refs_1_, f32[8,128,256]{2,1,0:T(8,128)S(1)} %get-tuple-element.36.refs_2_, ...), custom_call_target="tpu_custom_call" | custom-call | flops 1500000000 | bytes 3750000 | tf_op jit(solution)/shard_map/pallas_call | solution.py:64
  16.2 10.2 %all_to_all.11 = f32[16,1,256]{2,1,0:T(1,128)S(1)} all-to-all(f32[16,1,256]{2,1,0:T(1,128)S(1)} %copy.8), channel_id=1, replica_groups=mesh['groups'=2,'tm'=4,'space'=2,'chan'=2] {'tm','space','chan'}, dimensions={0} | all-to-all | bytes 32768 | tf_op jit(solution)/shard_map/all_to_all | solution.py:585
  26.4 1.5 %shard_map.78 = (bf16[8,16,128]{2,1,0:T(8,128)(2,1)S(1)}, bf16[8,16,128]{2,1,0:T(8,128)(2,1)S(1)}, bf16[8,16,128]{2,1,0:T(8,128)(2,1)S(1)}, bf16[8,16,128]{2,1,0:T(8,128)(2,1)S(1)}) custom-call(f32[16,256]{1,0:T(8,128)S(1)} %get-tuple-element.41.refs_0_, f32[8,128]{1,0:T(8,128)S(1)} %get-tuple-element.42.refs_1_, f32[16,256]{1,0:T(8,128)S(1)} %bitcast.12, ...), custom_call_target="tpu_custom_call" | custom-call | tf_op jit(solution)/shard_map/pallas_call | solution.py:64
  27.9 0.1 collective-permute-start.10
  28.0 2.3 %collective-permute-start.8 = (bf16[8,16,128]{2,1,0:T(8,128)(2,1)S(1)}, bf16[8,16,128]{2,1,0:T(8,128)(2,1)S(1)}, u32[]{:S(2)}, u32[]{:S(2)}) collective-permute-start(bf16[8,16,128]{2,1,0:T(8,128)(2,1)S(1)} %get-tuple-element.46), channel_id=1, source_target_pairs={{0,12},{4,8},{8,4},{12,0},{1,13},{5,9},{9,5},{13,1},{2,14},{6,10},... | collective-permute-start | bytes 98312 | tf_op jit(solution)/shard_map/ppermute | solution.py:601
  30.3 1.1 %collective-permute-start.9 = (bf16[8,16,128]{2,1,0:T(8,128)(2,1)S(1)}, bf16[8,16,128]{2,1,0:T(8,128)(2,1)S(1)}, u32[]{:S(2)}, u32[]{:S(2)}) collective-permute-start(bf16[8,16,128]{2,1,0:T(8,128)(2,1)S(1)} %get-tuple-element.47), channel_id=1, source_target_pairs={{0,4},{4,0},{8,12},{12,8},{1,5},{5,1},{9,13},{13,9},{2,6},{6,2},{1... | collective-permute-start | bytes 98312 | tf_op jit(solution)/shard_map/ppermute | solution.py:601
  31.5 1.7 %collective-permute-done.10.refs_3_ = bf16[8,16,128]{2,1,0:T(8,128)(2,1)S(1)} collective-permute-done((bf16[8,16,128]{2,1,0:T(8,128)(2,1)S(1)}, bf16[8,16,128]{2,1,0:T(8,128)(2,1)S(1)}, u32[]{:S(2)}, u32[]{:S(2)}) %collective-permute-start.10) | collective-permute-done | bytes 32800 | tf_op jit(solution)/shard_map/ppermute | solution.py:601
  33.1 0.7 %collective-permute-done.8.refs_1_ = bf16[8,16,128]{2,1,0:T(8,128)(2,1)S(1)} collective-permute-done((bf16[8,16,128]{2,1,0:T(8,128)(2,1)S(1)}, bf16[8,16,128]{2,1,0:T(8,128)(2,1)S(1)}, u32[]{:S(2)}, u32[]{:S(2)}) %collective-permute-start.8) | collective-permute-done | bytes 32800 | tf_op jit(solution)/shard_map/ppermute | solution.py:601
  33.8 0.4 %collective-permute-done.9.refs_2_ = bf16[8,16,128]{2,1,0:T(8,128)(2,1)S(1)} collective-permute-done((bf16[8,16,128]{2,1,0:T(8,128)(2,1)S(1)}, bf16[8,16,128]{2,1,0:T(8,128)(2,1)S(1)}, u32[]{:S(2)}, u32[]{:S(2)}) %collective-permute-start.9) | collective-permute-done | bytes 32800 | tf_op jit(solution)/shard_map/ppermute | solution.py:601
  34.2 0.7 %shard_map.79 = bf16[16,16,128]{2,1,0:T(8,128)(2,1)} custom-call(bf16[8,16,128]{2,1,0:T(8,128)(2,1)S(1)} %get-tuple-element.45.refs_0_, bf16[8,16,128]{2,1,0:T(8,128)(2,1)S(1)} %collective-permute-done.8.refs_1_, bf16[8,16,128]{2,1,0:T(8,128)(2,1)S(1)} %collective-permute-done.9.refs_2_, bf16[8,16,128]{2,1,0:T(8,128)(2,1)S(1)} %collective-permute-done.10.refs_3_), custom_call_target="tpu_custom_call" | custom-call | tf_op jit(solution)/shard_map/pallas_call | solution.py:605
  (22 shorter events, 0.2 us)
Async XLA Ops:
  0.0 1.0 %copy-start.1 = (bf16[64,2,8,256]{3,2,1,0:T(8,128)(2,1)S(1)}, bf16[64,2,8,256]{3,2,1,0:T(8,128)(2,1)}, u32[]{:S(2)}) copy-start(bf16[64,2,8,256]{3,2,1,0:T(8,128)(2,1)} %param.7) | copy-start | bytes 1572868
  1.0 6.3 %copy-start = (bf16[3,3,3,128,128]{4,3,2,1,0:T(8,128)(2,1)S(1)}, bf16[3,3,3,128,128]{4,3,2,1,0:T(8,128)(2,1)}, u32[]{:S(2)}) copy-start(bf16[3,3,3,128,128]{4,3,2,1,0:T(8,128)(2,1)} %refs_5_.1) | copy-start | bytes 2654212
  1.0 6.3 %copy-start.2 = (bf16[2,2,128,32]{2,3,1,0:T(8,128)(2,1)S(1)}, bf16[2,2,128,32]{2,3,1,0:T(8,128)(2,1)}, u32[]{:S(2)}) copy-start(bf16[2,2,128,32]{2,3,1,0:T(8,128)(2,1)} %param.12) | copy-start | bytes 98308
  1.0 6.3 %copy-start.6 = (f32[128]{0:T(128)S(1)}, f32[128]{0:T(128)}, u32[]{:S(2)}) copy-start(f32[128]{0:T(128)} %param.11) | copy-start | bytes 1540
  1.6 7.5 %collective-permute-start = (bf16[1024,256]{1,0:T(8,128)(2,1)S(1)}, bf16[1024,256]{1,0:T(8,128)(2,1)S(1)}, u32[]{:S(2)}, u32[]{:S(2)}) collective-permute-start(bf16[1024,256]{1,0:T(8,128)(2,1)S(1)} %get-tuple-element.27.refs_6_), channel_id=1, source_target_pairs={{0,1},{1,0},{2,3},{3,2},{4,5},{5,4},{6,7},{7,6},{8,9},{9,8},{10,11... | collective-permute-start | bytes 1572872 | tf_op jit(solution)/shard_map/ppermute | solution.py:549
  2.1 7.0 %collective-permute-start.1 = (bf16[128,256]{1,0:T(8,128)(2,1)S(1)}, bf16[128,256]{1,0:T(8,128)(2,1)S(1)}, u32[]{:S(2)}, u32[]{:S(2)}) collective-permute-start(bf16[128,256]{1,0:T(8,128)(2,1)S(1)} %get-tuple-element.34), channel_id=1, source_target_pairs={{0,2},{2,0},{1,3},{3,1},{4,6},{6,4},{5,7},{7,5},{8,10},{10,8},{9,1... | collective-permute-start | bytes 196616 | tf_op jit(solution)/shard_map/ppermute | solution.py:37
  4.7 8.9 %collective-permute-start.3 = (bf16[512,256]{1,0:T(8,128)(2,1)S(1)}, bf16[512,256]{1,0:T(8,128)(2,1)S(1)}, u32[]{:S(2)}, u32[]{:S(2)}) collective-permute-start(bf16[512,256]{1,0:T(8,128)(2,1)S(1)} %get-tuple-element.33.refs_3_.refs_7_), channel_id=1, source_target_pairs={{1,5},{4,0},{5,9},{8,4},{9,13},{12,8},{13,12},{0,1},{3,7},{6,2},{7... | collective-permute-start | bytes 786440 | tf_op jit(solution)/shard_map/ppermute | solution.py:54
  4.8 9.3 %collective-permute-start.4 = (bf16[512,256]{1,0:T(8,128)(2,1)S(1)}, bf16[512,256]{1,0:T(8,128)(2,1)S(1)}, u32[]{:S(2)}, u32[]{:S(2)}) collective-permute-start(bf16[512,256]{1,0:T(8,128)(2,1)S(1)} %get-tuple-element.32.refs_2_.refs_6_), channel_id=1, source_target_pairs={{0,5},{5,0},{4,9},{9,4},{8,13},{13,8},{1,3},{12,14},{2,7},{7,2},{6... | collective-permute-start | bytes 786440 | tf_op jit(solution)/shard_map/ppermute | solution.py:54
  7.3 0.7 %copy-start.3 = (s32[2]{0:T(128)S(1)}, s32[2]{0:T(128)}, u32[]{:S(2)}) copy-start(s32[2]{0:T(128)} %param.8) | copy-start | bytes 28
  7.3 0.7 %copy-start.4 = (s32[1,8,1]{1,2,0:T(1,128)S(1)}, s32[1,8,1]{1,2,0:T(1,128)}, u32[]{:S(2)}) copy-start(s32[1,8,1]{1,2,0:T(1,128)} %param.13) | copy-start | bytes 100
  7.3 0.7 %copy-start.5 = (f32[128]{0:T(128)S(1)}, f32[128]{0:T(128)}, u32[]{:S(2)}) copy-start(f32[128]{0:T(128)} %param.10) | copy-start | bytes 1540
  9.3 2.1 %collective-permute-start.2 = (bf16[128,256]{1,0:T(8,128)(2,1)S(1)}, bf16[128,256]{1,0:T(8,128)(2,1)S(1)}, u32[]{:S(2)}, u32[]{:S(2)}) collective-permute-start(bf16[128,256]{1,0:T(8,128)(2,1)S(1)} %get-tuple-element.35.refs_5_.refs_9_), channel_id=1, source_target_pairs={{0,1},{1,0},{2,3},{3,2},{4,5},{5,4},{6,7},{7,6},{8,9},{9,8},{10,11... | collective-permute-start | bytes 196616 | tf_op jit(solution)/shard_map/ppermute | solution.py:556
  9.3 5.3 %collective-permute-start.5 = (bf16[80,256]{1,0:T(8,128)(2,1)S(1)}, bf16[80,256]{1,0:T(8,128)(2,1)S(1)}, u32[]{:S(2)}, u32[]{:S(2)}) collective-permute-start(bf16[80,256]{1,0:T(8,128)(2,1)S(1)} %get-tuple-element.39.refs_5_), channel_id=1, source_target_pairs={{1,5},{4,0},{5,9},{8,4},{9,13},{12,8},{13,12},{0,1},{3,7},{6,2},{7... | collective-permute-start | bytes 122888 | tf_op jit(solution)/shard_map/ppermute | solution.py:54
  9.8 4.8 %collective-permute-start.6 = (bf16[64,256]{1,0:T(8,128)(2,1)S(1)}, bf16[64,256]{1,0:T(8,128)(2,1)S(1)}, u32[]{:S(2)}, u32[]{:S(2)}) collective-permute-start(bf16[64,256]{1,0:T(8,128)(2,1)S(1)} %get-tuple-element.40), channel_id=1, source_target_pairs={{0,5},{5,0},{4,9},{9,4},{8,13},{13,8},{1,3},{12,14},{2,7},{7,2},{6... | collective-permute-start | bytes 98312 | tf_op jit(solution)/shard_map/ppermute | solution.py:54
  16.1 10.3 %collective-permute-start.7 = (bf16[13,128,256]{2,1,0:T(8,128)(2,1)S(1)}, bf16[13,128,256]{2,1,0:T(8,128)(2,1)S(1)}, u32[]{:S(2)}, u32[]{:S(2)}) collective-permute-start(bf16[13,128,256]{2,1,0:T(8,128)(2,1)S(1)} %get-tuple-element.44.refs_5_), channel_id=1, source_target_pairs={{0,1},{1,0},{2,3},{3,2},{4,5},{5,4},{6,7},{7,6},{8,9},{9,8},{10,11... | collective-permute-start | bytes 2555912 | tf_op jit(solution)/shard_map/ppermute | solution.py:584
  27.9 5.2 %collective-permute-start.10 = (bf16[8,16,128]{2,1,0:T(8,128)(2,1)S(1)}, bf16[8,16,128]{2,1,0:T(8,128)(2,1)S(1)}, u32[]{:S(2)}, u32[]{:S(2)}) collective-permute-start(bf16[8,16,128]{2,1,0:T(8,128)(2,1)S(1)} %get-tuple-element.48), channel_id=1, source_target_pairs={{0,8},{4,12},{8,0},{12,4},{1,9},{5,13},{9,1},{13,5},{2,10},{6,14},... | collective-permute-start | bytes 98312 | tf_op jit(solution)/shard_map/ppermute | solution.py:601
  28.0 5.8 %collective-permute-start.8 = (bf16[8,16,128]{2,1,0:T(8,128)(2,1)S(1)}, bf16[8,16,128]{2,1,0:T(8,128)(2,1)S(1)}, u32[]{:S(2)}, u32[]{:S(2)}) collective-permute-start(bf16[8,16,128]{2,1,0:T(8,128)(2,1)S(1)} %get-tuple-element.46), channel_id=1, source_target_pairs={{0,12},{4,8},{8,4},{12,0},{1,13},{5,9},{9,5},{13,1},{2,14},{6,10},... | collective-permute-start | bytes 98312 | tf_op jit(solution)/shard_map/ppermute | solution.py:601
  30.3 3.9 %collective-permute-start.9 = (bf16[8,16,128]{2,1,0:T(8,128)(2,1)S(1)}, bf16[8,16,128]{2,1,0:T(8,128)(2,1)S(1)}, u32[]{:S(2)}, u32[]{:S(2)}) collective-permute-start(bf16[8,16,128]{2,1,0:T(8,128)(2,1)S(1)} %get-tuple-element.47), channel_id=1, source_target_pairs={{0,4},{4,0},{8,12},{12,8},{1,5},{5,1},{9,13},{13,9},{2,6},{6,2},{1... | collective-permute-start | bytes 98312 | tf_op jit(solution)/shard_map/ppermute | solution.py:601

commit v10 on v9

--- a/solution.py
+++ b/solution.py
@@ -491,11 +491,11 @@
     for d in range(slabs):
         block, ref = source(d)
 
-        @pl.when(block + 1 < slabs)
-        def _():
-            for j in range(capacity):
-                n = (block + 1) * capacity + j
-                owned_ref[n] = (owned_ref[n].astype(F32) + ref[capacity + j].astype(F32)).astype(BF16)
+        inside = block + 1 < slabs
+        first = jnp.minimum(block + 1, slabs - 1) * capacity
+        for j in range(capacity):
+            value = jnp.where(inside, ref[capacity + j].astype(F32), 0.0)
+            owned_ref[first + j] = (owned_ref[first + j].astype(F32) + value).astype(BF16)
 
 
 def shards(activations, frame_clip, conv_weight, norm_gain, norm_bias, out_weight, owner):

time: 35.1 us -> 35.1 us (level)
  no operation moved by 1% of the time
where the time goes in v10:
time: 35.1 us; the launch traced here: 34.9 us
  starting transfers between devices  11.4 us (32%)
  blocking collectives  10.2 us (29%)
  Pallas kernels  7.59 us (22%)
  waiting for transfers between devices  3.82 us (11%)
  local copies, waits for them, and re-layouts  1.73 us (5%)
    all_to_all x1, blocking collectives, shards(): lax.all_to_all(message, PART, split_axis=0, concat_axis=0, tiled=True)  10.2 us
    pallas_call x6, Pallas kernels, whole_call(): pl.pallas_call(turned, out_shape=out_shape, in_specs=[specs[n] for n in t...  6.92 us
    ppermute x4, starting transfers between devices, slab_swap(): return lax.ppermute(value, PART, flat_pairs(sizes, pairs))  4.67 us
    ppermute x3, starting transfers between devices, shards(): lax.ppermute(sends[d], 'tm', [(t, t ^ d) for t in range(slabs)])  3.55 us
    ppermute x3, waiting for transfers between devices, shards(): lax.ppermute(sends[d], 'tm', [(t, t ^ d) for t in range(slabs)])  2.76 us
    ppermute x1, starting transfers between devices, space_swap(): return lax.ppermute(value, PART, flat_pairs(sizes, pairs))  2.56 us
    unnamed x15, local copies, waits for them, and re-layouts  1.71 us
    ppermute x4, waiting for transfers between devices, slab_swap(): return lax.ppermute(value, PART, flat_pairs(sizes, pairs))  1.05 us
  transfers between devices with their start and end apart: 11, of which 5 were waited for; matrix products, arithmetic and copies ran while one was open for 0% of the time, Pallas kernels for 10%

profile of v10, /device:TPU:0, one launch (start us, length us, event | category | flops | bytes accessed | tf_op | source)
XLA Modules:
  0.0 34.9 jit_solution(8214582121405446324)
XLA Ops:
  0.0 1.0 %copy-done.1 = bf16[64,2,8,256]{3,2,1,0:T(8,128)(2,1)S(1)} copy-done((bf16[64,2,8,256]{3,2,1,0:T(8,128)(2,1)S(1)}, bf16[64,2,8,256]{3,2,1,0:T(8,128)(2,1)}, u32[]{:S(2)}) %copy-start.1) | copy-done | bytes 524312
  1.0 0.5 %shard_map.73 = (bf16[512,256]{1,0:T(8,128)(2,1)S(1)}, bf16[512,256]{1,0:T(8,128)(2,1)S(1)}, bf16[1024,256]{1,0:T(8,128)(2,1)S(1)}, bf16[128,256]{1,0:T(8,128)(2,1)S(1)}) custom-call(bf16[1024,256]{1,0:T(8,128)(2,1)S(1)} %bitcast.13), custom_call_target="tpu_custom_call" | custom-call | flops 3000000000 | bytes 7500000 | tf_op jit(solution)/shard_map/pallas_call | solution.py:64
  1.6 0.5 %collective-permute-start = (bf16[1024,256]{1,0:T(8,128)(2,1)S(1)}, bf16[1024,256]{1,0:T(8,128)(2,1)S(1)}, u32[]{:S(2)}, u32[]{:S(2)}) collective-permute-start(bf16[1024,256]{1,0:T(8,128)(2,1)S(1)} %get-tuple-element.27.refs_6_), channel_id=1, source_target_pairs={{0,1},{1,0},{2,3},{3,2},{4,5},{5,4},{6,7},{7,6},{8,9},{9,8},{10,11... | collective-permute-start | bytes 1572872 | tf_op jit(solution)/shard_map/ppermute | solution.py:549
  2.1 2.6 %collective-permute-start.1 = (bf16[128,256]{1,0:T(8,128)(2,1)S(1)}, bf16[128,256]{1,0:T(8,128)(2,1)S(1)}, u32[]{:S(2)}, u32[]{:S(2)}) collective-permute-start(bf16[128,256]{1,0:T(8,128)(2,1)S(1)} %get-tuple-element.34), channel_id=1, source_target_pairs={{0,2},{2,0},{1,3},{3,1},{4,6},{6,4},{5,7},{7,5},{8,10},{10,8},{9,1... | collective-permute-start | bytes 196616 | tf_op jit(solution)/shard_map/ppermute | solution.py:37
  4.7 0.2 collective-permute-start.3
  4.8 2.5 %collective-permute-start.4 = (bf16[512,256]{1,0:T(8,128)(2,1)S(1)}, bf16[512,256]{1,0:T(8,128)(2,1)S(1)}, u32[]{:S(2)}, u32[]{:S(2)}) collective-permute-start(bf16[512,256]{1,0:T(8,128)(2,1)S(1)} %get-tuple-element.32.refs_2_.refs_6_), channel_id=1, source_target_pairs={{0,5},{5,0},{4,9},{9,4},{8,13},{13,8},{1,3},{12,14},{2,7},{7,2},{6... | collective-permute-start | bytes 786440 | tf_op jit(solution)/shard_map/ppermute | solution.py:54
  7.4 0.6 %copy-done.3 = s32[2]{0:T(128)S(1)} copy-done((s32[2]{0:T(128)S(1)}, s32[2]{0:T(128)}, u32[]{:S(2)}) %copy-start.3) | copy-done | bytes 32
  8.0 1.1 %shard_map.74 = (bf16[384,768]{1,0:T(8,128)(2,1)S(1)}, bf16[2,384,384]{2,1,0:T(8,128)(2,1)S(1)}, bf16[384,384]{1,0:T(8,128)(2,1)S(1)}, f32[8,128]{1,0:T(8,128)S(1)}, bf16[32,512]{1,0:T(8,128)(2,1)S(1)}) custom-call(s32[1,2]{1,0:T(1,128)S(1)} %bitcast.15, s32[1,8]{1,0:T(1,128)S(1)} %bitcast.16, f32[1,128]{1,0:T(1,128)S(1)} %bitcast.17, ...), custom_call_target="tpu_custom_call" | custom-call | flops 4800000000 | bytes 12000000 | tf_op jit(solution)/shard_map/pallas_call | solution.py:64
  9.1 0.2 shard_map.75
  9.3 0.5 %collective-permute-start.5 = (bf16[80,256]{1,0:T(8,128)(2,1)S(1)}, bf16[80,256]{1,0:T(8,128)(2,1)S(1)}, u32[]{:S(2)}, u32[]{:S(2)}) collective-permute-start(bf16[80,256]{1,0:T(8,128)(2,1)S(1)} %get-tuple-element.39.refs_5_), channel_id=1, source_target_pairs={{1,5},{4,0},{5,9},{8,4},{9,13},{12,8},{13,12},{0,1},{3,7},{6,2},{7... | collective-permute-start | bytes 122888 | tf_op jit(solution)/shard_map/ppermute | solution.py:54
  9.8 1.5 %collective-permute-start.6 = (bf16[64,256]{1,0:T(8,128)(2,1)S(1)}, bf16[64,256]{1,0:T(8,128)(2,1)S(1)}, u32[]{:S(2)}, u32[]{:S(2)}) collective-permute-start(bf16[64,256]{1,0:T(8,128)(2,1)S(1)} %get-tuple-element.40), channel_id=1, source_target_pairs={{0,5},{5,0},{4,9},{9,4},{8,13},{13,8},{1,3},{12,14},{2,7},{7,2},{6... | collective-permute-start | bytes 98312 | tf_op jit(solution)/shard_map/ppermute | solution.py:54
  11.4 2.2 %shard_map.76 = (f32[8,128,256]{2,1,0:T(8,128)S(1)}, bf16[4,128,256]{2,1,0:T(8,128)(2,1)S(1)}, f32[8,128]{1,0:T(8,128)S(1)}) custom-call(bf16[384,768]{1,0:T(8,128)(2,1)S(1)} %get-tuple-element.30.refs_0_, bf16[384,384]{1,0:T(8,128)(2,1)S(1)} %get-tuple-element.31.refs_1_, bf16[512,256]{1,0:T(8,128)(2,1)S(1)} %get-tuple-element.32.refs_2_.refs_6_, ...), custom_call_target="tpu_custom_call" | custom-call | flops 1000000 | bytes 2500 | tf_op jit(solution)/shard_map/pallas_call | solution.py:64
  13.6 0.6 %collective-permute-done.4.refs_12_ = bf16[512,256]{1,0:T(8,128)(2,1)S(1)} collective-permute-done((bf16[512,256]{1,0:T(8,128)(2,1)S(1)}, bf16[512,256]{1,0:T(8,128)(2,1)S(1)}, u32[]{:S(2)}, u32[]{:S(2)}) %collective-permute-start.4) | collective-permute-done | bytes 262176 | tf_op jit(solution)/shard_map/ppermute | solution.py:54
  14.2 0.5 %collective-permute-done.6.refs_14_ = bf16[64,256]{1,0:T(8,128)(2,1)S(1)} collective-permute-done((bf16[64,256]{1,0:T(8,128)(2,1)S(1)}, bf16[64,256]{1,0:T(8,128)(2,1)S(1)}, u32[]{:S(2)}, u32[]{:S(2)}) %collective-permute-start.6) | collective-permute-done | bytes 32800 | tf_op jit(solution)/shard_map/ppermute | solution.py:54
  14.7 1.4 %shard_map.77 = (bf16[13,128,256]{2,1,0:T(8,128)(2,1)S(1)}, f32[16,256]{1,0:T(8,128)S(1)}, f32[8,128]{1,0:T(8,128)S(1)}) custom-call(f32[8,128]{1,0:T(8,128)S(1)} %get-tuple-element.28.refs_0_.refs_3_, bf16[2,384,384]{2,1,0:T(8,128)(2,1)S(1)} %get-tuple-element.29.refs_1_, f32[8,128,256]{2,1,0:T(8,128)S(1)} %get-tuple-element.36.refs_2_, ...), custom_call_target="tpu_custom_call" | custom-call | flops 1500000000 | bytes 3750000 | tf_op jit(solution)/shard_map/pallas_call | solution.py:64
  16.2 10.2 %all_to_all.11 = f32[16,1,256]{2,1,0:T(1,128)S(1)} all-to-all(f32[16,1,256]{2,1,0:T(1,128)S(1)} %copy.8), channel_id=1, replica_groups=mesh['groups'=2,'tm'=4,'space'=2,'chan'=2] {'tm','space','chan'}, dimensions={0} | all-to-all | bytes 32768 | tf_op jit(solution)/shard_map/all_to_all | solution.py:585
  26.4 1.5 %shard_map.78 = (bf16[8,16,128]{2,1,0:T(8,128)(2,1)S(1)}, bf16[8,16,128]{2,1,0:T(8,128)(2,1)S(1)}, bf16[8,16,128]{2,1,0:T(8,128)(2,1)S(1)}, bf16[8,16,128]{2,1,0:T(8,128)(2,1)S(1)}) custom-call(f32[16,256]{1,0:T(8,128)S(1)} %get-tuple-element.41.refs_0_, f32[8,128]{1,0:T(8,128)S(1)} %get-tuple-element.42.refs_1_, f32[16,256]{1,0:T(8,128)S(1)} %bitcast.12, ...), custom_call_target="tpu_custom_call" | custom-call | tf_op jit(solution)/shard_map/pallas_call | solution.py:64
  27.9 0.1 collective-permute-start.10
  28.0 2.3 %collective-permute-start.8 = (bf16[8,16,128]{2,1,0:T(8,128)(2,1)S(1)}, bf16[8,16,128]{2,1,0:T(8,128)(2,1)S(1)}, u32[]{:S(2)}, u32[]{:S(2)}) collective-permute-start(bf16[8,16,128]{2,1,0:T(8,128)(2,1)S(1)} %get-tuple-element.46), channel_id=1, source_target_pairs={{0,12},{4,8},{8,4},{12,0},{1,13},{5,9},{9,5},{13,1},{2,14},{6,10},... | collective-permute-start | bytes 98312 | tf_op jit(solution)/shard_map/ppermute | solution.py:601
  30.3 1.1 %collective-permute-start.9 = (bf16[8,16,128]{2,1,0:T(8,128)(2,1)S(1)}, bf16[8,16,128]{2,1,0:T(8,128)(2,1)S(1)}, u32[]{:S(2)}, u32[]{:S(2)}) collective-permute-start(bf16[8,16,128]{2,1,0:T(8,128)(2,1)S(1)} %get-tuple-element.47), channel_id=1, source_target_pairs={{0,4},{4,0},{8,12},{12,8},{1,5},{5,1},{9,13},{13,9},{2,6},{6,2},{1... | collective-permute-start | bytes 98312 | tf_op jit(solution)/shard_map/ppermute | solution.py:601
  31.5 1.7 %collective-permute-done.10.refs_3_ = bf16[8,16,128]{2,1,0:T(8,128)(2,1)S(1)} collective-permute-done((bf16[8,16,128]{2,1,0:T(8,128)(2,1)S(1)}, bf16[8,16,128]{2,1,0:T(8,128)(2,1)S(1)}, u32[]{:S(2)}, u32[]{:S(2)}) %collective-permute-start.10) | collective-permute-done | bytes 32800 | tf_op jit(solution)/shard_map/ppermute | solution.py:601
  33.1 0.7 %collective-permute-done.8.refs_1_ = bf16[8,16,128]{2,1,0:T(8,128)(2,1)S(1)} collective-permute-done((bf16[8,16,128]{2,1,0:T(8,128)(2,1)S(1)}, bf16[8,16,128]{2,1,0:T(8,128)(2,1)S(1)}, u32[]{:S(2)}, u32[]{:S(2)}) %collective-permute-start.8) | collective-permute-done | bytes 32800 | tf_op jit(solution)/shard_map/ppermute | solution.py:601
  33.8 0.4 %collective-permute-done.9.refs_2_ = bf16[8,16,128]{2,1,0:T(8,128)(2,1)S(1)} collective-permute-done((bf16[8,16,128]{2,1,0:T(8,128)(2,1)S(1)}, bf16[8,16,128]{2,1,0:T(8,128)(2,1)S(1)}, u32[]{:S(2)}, u32[]{:S(2)}) %collective-permute-start.9) | collective-permute-done | bytes 32800 | tf_op jit(solution)/shard_map/ppermute | solution.py:601
  34.2 0.7 %shard_map.79 = bf16[16,16,128]{2,1,0:T(8,128)(2,1)} custom-call(bf16[8,16,128]{2,1,0:T(8,128)(2,1)S(1)} %get-tuple-element.45.refs_0_, bf16[8,16,128]{2,1,0:T(8,128)(2,1)S(1)} %collective-permute-done.8.refs_1_, bf16[8,16,128]{2,1,0:T(8,128)(2,1)S(1)} %collective-permute-done.9.refs_2_, bf16[8,16,128]{2,1,0:T(8,128)(2,1)S(1)} %collective-permute-done.10.refs_3_), custom_call_target="tpu_custom_call" | custom-call | tf_op jit(solution)/shard_map/pallas_call | solution.py:605
  (22 shorter events, 0.2 us)
Async XLA Ops:
  0.0 1.0 %copy-start.1 = (bf16[64,2,8,256]{3,2,1,0:T(8,128)(2,1)S(1)}, bf16[64,2,8,256]{3,2,1,0:T(8,128)(2,1)}, u32[]{:S(2)}) copy-start(bf16[64,2,8,256]{3,2,1,0:T(8,128)(2,1)} %param.7) | copy-start | bytes 1572868
  1.0 6.3 %copy-start = (bf16[3,3,3,128,128]{4,3,2,1,0:T(8,128)(2,1)S(1)}, bf16[3,3,3,128,128]{4,3,2,1,0:T(8,128)(2,1)}, u32[]{:S(2)}) copy-start(bf16[3,3,3,128,128]{4,3,2,1,0:T(8,128)(2,1)} %refs_5_.1) | copy-start | bytes 2654212
  1.0 6.3 %copy-start.2 = (bf16[2,2,128,32]{2,3,1,0:T(8,128)(2,1)S(1)}, bf16[2,2,128,32]{2,3,1,0:T(8,128)(2,1)}, u32[]{:S(2)}) copy-start(bf16[2,2,128,32]{2,3,1,0:T(8,128)(2,1)} %param.12) | copy-start | bytes 98308
  1.0 6.3 %copy-start.6 = (f32[128]{0:T(128)S(1)}, f32[128]{0:T(128)}, u32[]{:S(2)}) copy-start(f32[128]{0:T(128)} %param.11) | copy-start | bytes 1540
  1.6 7.5 %collective-permute-start = (bf16[1024,256]{1,0:T(8,128)(2,1)S(1)}, bf16[1024,256]{1,0:T(8,128)(2,1)S(1)}, u32[]{:S(2)}, u32[]{:S(2)}) collective-permute-start(bf16[1024,256]{1,0:T(8,128)(2,1)S(1)} %get-tuple-element.27.refs_6_), channel_id=1, source_target_pairs={{0,1},{1,0},{2,3},{3,2},{4,5},{5,4},{6,7},{7,6},{8,9},{9,8},{10,11... | collective-permute-start | bytes 1572872 | tf_op jit(solution)/shard_map/ppermute | solution.py:549
  2.1 7.0 %collective-permute-start.1 = (bf16[128,256]{1,0:T(8,128)(2,1)S(1)}, bf16[128,256]{1,0:T(8,128)(2,1)S(1)}, u32[]{:S(2)}, u32[]{:S(2)}) collective-permute-start(bf16[128,256]{1,0:T(8,128)(2,1)S(1)} %get-tuple-element.34), channel_id=1, source_target_pairs={{0,2},{2,0},{1,3},{3,1},{4,6},{6,4},{5,7},{7,5},{8,10},{10,8},{9,1... | collective-permute-start | bytes 196616 | tf_op jit(solution)/shard_map/ppermute | solution.py:37
  4.7 8.9 %collective-permute-start.3 = (bf16[512,256]{1,0:T(8,128)(2,1)S(1)}, bf16[512,256]{1,0:T(8,128)(2,1)S(1)}, u32[]{:S(2)}, u32[]{:S(2)}) collective-permute-start(bf16[512,256]{1,0:T(8,128)(2,1)S(1)} %get-tuple-element.33.refs_3_.refs_7_), channel_id=1, source_target_pairs={{1,5},{4,0},{5,9},{8,4},{9,13},{12,8},{13,12},{0,1},{3,7},{6,2},{7... | collective-permute-start | bytes 786440 | tf_op jit(solution)/shard_map/ppermute | solution.py:54
  4.8 9.3 %collective-permute-start.4 = (bf16[512,256]{1,0:T(8,128)(2,1)S(1)}, bf16[512,256]{1,0:T(8,128)(2,1)S(1)}, u32[]{:S(2)}, u32[]{:S(2)}) collective-permute-start(bf16[512,256]{1,0:T(8,128)(2,1)S(1)} %get-tuple-element.32.refs_2_.refs_6_), channel_id=1, source_target_pairs={{0,5},{5,0},{4,9},{9,4},{8,13},{13,8},{1,3},{12,14},{2,7},{7,2},{6... | collective-permute-start | bytes 786440 | tf_op jit(solution)/shard_map/ppermute | solution.py:54
  7.3 0.7 %copy-start.3 = (s32[2]{0:T(128)S(1)}, s32[2]{0:T(128)}, u32[]{:S(2)}) copy-start(s32[2]{0:T(128)} %param.8) | copy-start | bytes 28
  7.3 0.7 %copy-start.4 = (s32[1,8,1]{1,2,0:T(1,128)S(1)}, s32[1,8,1]{1,2,0:T(1,128)}, u32[]{:S(2)}) copy-start(s32[1,8,1]{1,2,0:T(1,128)} %param.13) | copy-start | bytes 100
  7.3 0.7 %copy-start.5 = (f32[128]{0:T(128)S(1)}, f32[128]{0:T(128)}, u32[]{:S(2)}) copy-start(f32[128]{0:T(128)} %param.10) | copy-start | bytes 1540
  9.3 2.1 %collective-permute-start.2 = (bf16[128,256]{1,0:T(8,128)(2,1)S(1)}, bf16[128,256]{1,0:T(8,128)(2,1)S(1)}, u32[]{:S(2)}, u32[]{:S(2)}) collective-permute-start(bf16[128,256]{1,0:T(8,128)(2,1)S(1)} %get-tuple-element.35.refs_5_.refs_9_), channel_id=1, source_target_pairs={{0,1},{1,0},{2,3},{3,2},{4,5},{5,4},{6,7},{7,6},{8,9},{9,8},{10,11... | collective-permute-start | bytes 196616 | tf_op jit(solution)/shard_map/ppermute | solution.py:556
  9.3 5.3 %collective-permute-start.5 = (bf16[80,256]{1,0:T(8,128)(2,1)S(1)}, bf16[80,256]{1,0:T(8,128)(2,1)S(1)}, u32[]{:S(2)}, u32[]{:S(2)}) collective-permute-start(bf16[80,256]{1,0:T(8,128)(2,1)S(1)} %get-tuple-element.39.refs_5_), channel_id=1, source_target_pairs={{1,5},{4,0},{5,9},{8,4},{9,13},{12,8},{13,12},{0,1},{3,7},{6,2},{7... | collective-permute-start | bytes 122888 | tf_op jit(solution)/shard_map/ppermute | solution.py:54
  9.8 4.8 %collective-permute-start.6 = (bf16[64,256]{1,0:T(8,128)(2,1)S(1)}, bf16[64,256]{1,0:T(8,128)(2,1)S(1)}, u32[]{:S(2)}, u32[]{:S(2)}) collective-permute-start(bf16[64,256]{1,0:T(8,128)(2,1)S(1)} %get-tuple-element.40), channel_id=1, source_target_pairs={{0,5},{5,0},{4,9},{9,4},{8,13},{13,8},{1,3},{12,14},{2,7},{7,2},{6... | collective-permute-start | bytes 98312 | tf_op jit(solution)/shard_map/ppermute | solution.py:54
  16.1 10.3 %collective-permute-start.7 = (bf16[13,128,256]{2,1,0:T(8,128)(2,1)S(1)}, bf16[13,128,256]{2,1,0:T(8,128)(2,1)S(1)}, u32[]{:S(2)}, u32[]{:S(2)}) collective-permute-start(bf16[13,128,256]{2,1,0:T(8,128)(2,1)S(1)} %get-tuple-element.44.refs_5_), channel_id=1, source_target_pairs={{0,1},{1,0},{2,3},{3,2},{4,5},{5,4},{6,7},{7,6},{8,9},{9,8},{10,11... | collective-permute-start | bytes 2555912 | tf_op jit(solution)/shard_map/ppermute | solution.py:584
  27.9 5.2 %collective-permute-start.10 = (bf16[8,16,128]{2,1,0:T(8,128)(2,1)S(1)}, bf16[8,16,128]{2,1,0:T(8,128)(2,1)S(1)}, u32[]{:S(2)}, u32[]{:S(2)}) collective-permute-start(bf16[8,16,128]{2,1,0:T(8,128)(2,1)S(1)} %get-tuple-element.48), channel_id=1, source_target_pairs={{0,8},{4,12},{8,0},{12,4},{1,9},{5,13},{9,1},{13,5},{2,10},{6,14},... | collective-permute-start | bytes 98312 | tf_op jit(solution)/shard_map/ppermute | solution.py:601
  28.0 5.8 %collective-permute-start.8 = (bf16[8,16,128]{2,1,0:T(8,128)(2,1)S(1)}, bf16[8,16,128]{2,1,0:T(8,128)(2,1)S(1)}, u32[]{:S(2)}, u32[]{:S(2)}) collective-permute-start(bf16[8,16,128]{2,1,0:T(8,128)(2,1)S(1)} %get-tuple-element.46), channel_id=1, source_target_pairs={{0,12},{4,8},{8,4},{12,0},{1,13},{5,9},{9,5},{13,1},{2,14},{6,10},... | collective-permute-start | bytes 98312 | tf_op jit(solution)/shard_map/ppermute | solution.py:601
  30.3 3.9 %collective-permute-start.9 = (bf16[8,16,128]{2,1,0:T(8,128)(2,1)S(1)}, bf16[8,16,128]{2,1,0:T(8,128)(2,1)S(1)}, u32[]{:S(2)}, u32[]{:S(2)}) collective-permute-start(bf16[8,16,128]{2,1,0:T(8,128)(2,1)S(1)} %get-tuple-element.47), channel_id=1, source_target_pairs={{0,4},{4,0},{8,12},{12,8},{1,5},{5,1},{9,13},{13,9},{2,6},{6,2},{1... | collective-permute-start | bytes 98312 | tf_op jit(solution)/shard_map/ppermute | solution.py:601

commit v11 on v10

--- a/solution.py
+++ b/solution.py
@@ -601,7 +601,7 @@
             received.append(lax.ppermute(sends[d], "tm", [(t, t ^ d) for t in range(slabs)]))
     else:
         received = [lax.all_to_all(sends[0], "tm", split_axis=0, concat_axis=0, tiled=True)]
-    turns = list((0, 3, 1, 2)) if crossed(slabs) else [0]
+    turns = list((0, 2, 1, 3)) if crossed(slabs) else [0]
     owned = pl.pallas_call(
         lambda *refs: merge_kernel(slabs, capacity, *[refs[turns.index(d)] for d in range(len(turns))], refs[-1]),
         out_shape=jax.ShapeDtypeStruct((slabs * capacity, part, width), BF16),

time: 35.1 us -> 35.1 us (level)
  starting transfers between devices: 11.4 us -> 12.3 us
  waiting for transfers between devices: 3.82 us -> 2.95 us
    ppermute x3, starting transfers between devices: 3.55 us -> 4.45 us  [shards(): lax.ppermute(sends[d], 'tm', [(t, t ^ d) for t in range(slabs)])]
    ppermute x3, waiting for transfers between devices: 2.76 us -> 1.89 us  [shards(): lax.ppermute(sends[d], 'tm', [(t, t ^ d) for t in range(slabs)])]
  transfers between devices with their start and end apart: 11 -> 11, of which waited for: 5 -> 4; matrix products, arithmetic and copies ran while one was open for 0% -> 0% of each run, Pallas kernels for 10% -> 10%
where the time goes in v11:
time: 35.1 us; the launch traced here: 34.9 us
  starting transfers between devices  12.3 us (35%)
  blocking collectives  10.2 us (29%)
  Pallas kernels  7.59 us (22%)
  waiting for transfers between devices  2.95 us (8%)
  local copies, waits for them, and re-layouts  1.73 us (5%)
    all_to_all x1, blocking collectives, shards(): lax.all_to_all(message, PART, split_axis=0, concat_axis=0, tiled=True)  10.2 us
    pallas_call x6, Pallas kernels, whole_call(): pl.pallas_call(turned, out_shape=out_shape, in_specs=[specs[n] for n in t...  6.92 us
    ppermute x4, starting transfers between devices, slab_swap(): return lax.ppermute(value, PART, flat_pairs(sizes, pairs))  4.67 us
    ppermute x3, starting transfers between devices, shards(): lax.ppermute(sends[d], 'tm', [(t, t ^ d) for t in range(slabs)])  4.45 us
    ppermute x1, starting transfers between devices, space_swap(): return lax.ppermute(value, PART, flat_pairs(sizes, pairs))  2.56 us
    ppermute x3, waiting for transfers between devices, shards(): lax.ppermute(sends[d], 'tm', [(t, t ^ d) for t in range(slabs)])  1.89 us
    unnamed x15, local copies, waits for them, and re-layouts  1.71 us
    ppermute x4, waiting for transfers between devices, slab_swap(): return lax.ppermute(value, PART, flat_pairs(sizes, pairs))  1.05 us
  transfers between devices with their start and end apart: 11, of which 4 were waited for; matrix products, arithmetic and copies ran while one was open for 0% of the time, Pallas kernels for 10%

profile of v11, /device:TPU:0, one launch (start us, length us, event | category | flops | bytes accessed | tf_op | source)
XLA Modules:
  0.0 34.9 jit_solution(1273112322821551439)
XLA Ops:
  0.0 1.0 %copy-done.1 = bf16[64,2,8,256]{3,2,1,0:T(8,128)(2,1)S(1)} copy-done((bf16[64,2,8,256]{3,2,1,0:T(8,128)(2,1)S(1)}, bf16[64,2,8,256]{3,2,1,0:T(8,128)(2,1)}, u32[]{:S(2)}) %copy-start.1) | copy-done | bytes 524312
  1.0 0.5 %shard_map.73 = (bf16[512,256]{1,0:T(8,128)(2,1)S(1)}, bf16[512,256]{1,0:T(8,128)(2,1)S(1)}, bf16[1024,256]{1,0:T(8,128)(2,1)S(1)}, bf16[128,256]{1,0:T(8,128)(2,1)S(1)}) custom-call(bf16[1024,256]{1,0:T(8,128)(2,1)S(1)} %bitcast.13), custom_call_target="tpu_custom_call" | custom-call | flops 3000000000 | bytes 7500000 | tf_op jit(solution)/shard_map/pallas_call | solution.py:64
  1.6 0.5 %collective-permute-start = (bf16[1024,256]{1,0:T(8,128)(2,1)S(1)}, bf16[1024,256]{1,0:T(8,128)(2,1)S(1)}, u32[]{:S(2)}, u32[]{:S(2)}) collective-permute-start(bf16[1024,256]{1,0:T(8,128)(2,1)S(1)} %get-tuple-element.27.refs_6_), channel_id=1, source_target_pairs={{0,1},{1,0},{2,3},{3,2},{4,5},{5,4},{6,7},{7,6},{8,9},{9,8},{10,11... | collective-permute-start | bytes 1572872 | tf_op jit(solution)/shard_map/ppermute | solution.py:549
  2.1 2.6 %collective-permute-start.1 = (bf16[128,256]{1,0:T(8,128)(2,1)S(1)}, bf16[128,256]{1,0:T(8,128)(2,1)S(1)}, u32[]{:S(2)}, u32[]{:S(2)}) collective-permute-start(bf16[128,256]{1,0:T(8,128)(2,1)S(1)} %get-tuple-element.34), channel_id=1, source_target_pairs={{0,2},{2,0},{1,3},{3,1},{4,6},{6,4},{5,7},{7,5},{8,10},{10,8},{9,1... | collective-permute-start | bytes 196616 | tf_op jit(solution)/shard_map/ppermute | solution.py:37
  4.7 0.2 collective-permute-start.3
  4.8 2.5 %collective-permute-start.4 = (bf16[512,256]{1,0:T(8,128)(2,1)S(1)}, bf16[512,256]{1,0:T(8,128)(2,1)S(1)}, u32[]{:S(2)}, u32[]{:S(2)}) collective-permute-start(bf16[512,256]{1,0:T(8,128)(2,1)S(1)} %get-tuple-element.32.refs_2_.refs_6_), channel_id=1, source_target_pairs={{0,5},{5,0},{4,9},{9,4},{8,13},{13,8},{1,3},{12,14},{2,7},{7,2},{6... | collective-permute-start | bytes 786440 | tf_op jit(solution)/shard_map/ppermute | solution.py:54
  7.4 0.6 %copy-done.3 = s32[2]{0:T(128)S(1)} copy-done((s32[2]{0:T(128)S(1)}, s32[2]{0:T(128)}, u32[]{:S(2)}) %copy-start.3) | copy-done | bytes 32
  8.0 1.1 %shard_map.74 = (bf16[384,768]{1,0:T(8,128)(2,1)S(1)}, bf16[2,384,384]{2,1,0:T(8,128)(2,1)S(1)}, bf16[384,384]{1,0:T(8,128)(2,1)S(1)}, f32[8,128]{1,0:T(8,128)S(1)}, bf16[32,512]{1,0:T(8,128)(2,1)S(1)}) custom-call(s32[1,2]{1,0:T(1,128)S(1)} %bitcast.15, s32[1,8]{1,0:T(1,128)S(1)} %bitcast.16, f32[1,128]{1,0:T(1,128)S(1)} %bitcast.17, ...), custom_call_target="tpu_custom_call" | custom-call | flops 4800000000 | bytes 12000000 | tf_op jit(solution)/shard_map/pallas_call | solution.py:64
  9.1 0.2 shard_map.75
  9.3 0.5 %collective-permute-start.5 = (bf16[80,256]{1,0:T(8,128)(2,1)S(1)}, bf16[80,256]{1,0:T(8,128)(2,1)S(1)}, u32[]{:S(2)}, u32[]{:S(2)}) collective-permute-start(bf16[80,256]{1,0:T(8,128)(2,1)S(1)} %get-tuple-element.39.refs_5_), channel_id=1, source_target_pairs={{1,5},{4,0},{5,9},{8,4},{9,13},{12,8},{13,12},{0,1},{3,7},{6,2},{7... | collective-permute-start | bytes 122888 | tf_op jit(solution)/shard_map/ppermute | solution.py:54
  9.8 1.5 %collective-permute-start.6 = (bf16[64,256]{1,0:T(8,128)(2,1)S(1)}, bf16[64,256]{1,0:T(8,128)(2,1)S(1)}, u32[]{:S(2)}, u32[]{:S(2)}) collective-permute-start(bf16[64,256]{1,0:T(8,128)(2,1)S(1)} %get-tuple-element.40), channel_id=1, source_target_pairs={{0,5},{5,0},{4,9},{9,4},{8,13},{13,8},{1,3},{12,14},{2,7},{7,2},{6... | collective-permute-start | bytes 98312 | tf_op jit(solution)/shard_map/ppermute | solution.py:54
  11.4 2.2 %shard_map.76 = (f32[8,128,256]{2,1,0:T(8,128)S(1)}, bf16[4,128,256]{2,1,0:T(8,128)(2,1)S(1)}, f32[8,128]{1,0:T(8,128)S(1)}) custom-call(bf16[384,768]{1,0:T(8,128)(2,1)S(1)} %get-tuple-element.30.refs_0_, bf16[384,384]{1,0:T(8,128)(2,1)S(1)} %get-tuple-element.31.refs_1_, bf16[512,256]{1,0:T(8,128)(2,1)S(1)} %get-tuple-element.32.refs_2_.refs_6_, ...), custom_call_target="tpu_custom_call" | custom-call | flops 1000000 | bytes 2500 | tf_op jit(solution)/shard_map/pallas_call | solution.py:64
  13.6 0.6 %collective-permute-done.4.refs_12_ = bf16[512,256]{1,0:T(8,128)(2,1)S(1)} collective-permute-done((bf16[512,256]{1,0:T(8,128)(2,1)S(1)}, bf16[512,256]{1,0:T(8,128)(2,1)S(1)}, u32[]{:S(2)}, u32[]{:S(2)}) %collective-permute-start.4) | collective-permute-done | bytes 262176 | tf_op jit(solution)/shard_map/ppermute | solution.py:54
  14.2 0.5 %collective-permute-done.6.refs_14_ = bf16[64,256]{1,0:T(8,128)(2,1)S(1)} collective-permute-done((bf16[64,256]{1,0:T(8,128)(2,1)S(1)}, bf16[64,256]{1,0:T(8,128)(2,1)S(1)}, u32[]{:S(2)}, u32[]{:S(2)}) %collective-permute-start.6) | collective-permute-done | bytes 32800 | tf_op jit(solution)/shard_map/ppermute | solution.py:54
  14.7 1.4 %shard_map.77 = (bf16[13,128,256]{2,1,0:T(8,128)(2,1)S(1)}, f32[16,256]{1,0:T(8,128)S(1)}, f32[8,128]{1,0:T(8,128)S(1)}) custom-call(f32[8,128]{1,0:T(8,128)S(1)} %get-tuple-element.28.refs_0_.refs_3_, bf16[2,384,384]{2,1,0:T(8,128)(2,1)S(1)} %get-tuple-element.29.refs_1_, f32[8,128,256]{2,1,0:T(8,128)S(1)} %get-tuple-element.36.refs_2_, ...), custom_call_target="tpu_custom_call" | custom-call | flops 1500000000 | bytes 3750000 | tf_op jit(solution)/shard_map/pallas_call | solution.py:64
  16.1 0.1 collective-permute-start.7
  16.2 10.2 %all_to_all.11 = f32[16,1,256]{2,1,0:T(1,128)S(1)} all-to-all(f32[16,1,256]{2,1,0:T(1,128)S(1)} %copy.8), channel_id=1, replica_groups=mesh['groups'=2,'tm'=4,'space'=2,'chan'=2] {'tm','space','chan'}, dimensions={0} | all-to-all | bytes 32768 | tf_op jit(solution)/shard_map/all_to_all | solution.py:585
  26.4 1.5 %shard_map.78 = (bf16[8,16,128]{2,1,0:T(8,128)(2,1)S(1)}, bf16[8,16,128]{2,1,0:T(8,128)(2,1)S(1)}, bf16[8,16,128]{2,1,0:T(8,128)(2,1)S(1)}, bf16[8,16,128]{2,1,0:T(8,128)(2,1)S(1)}) custom-call(f32[16,256]{1,0:T(8,128)S(1)} %get-tuple-element.41.refs_0_, f32[8,128]{1,0:T(8,128)S(1)} %get-tuple-element.42.refs_1_, f32[16,256]{1,0:T(8,128)S(1)} %bitcast.12, ...), custom_call_target="tpu_custom_call" | custom-call | tf_op jit(solution)/shard_map/pallas_call | solution.py:64
  27.9 0.1 collective-permute-start.10
  28.0 1.4 %collective-permute-start.8 = (bf16[8,16,128]{2,1,0:T(8,128)(2,1)S(1)}, bf16[8,16,128]{2,1,0:T(8,128)(2,1)S(1)}, u32[]{:S(2)}, u32[]{:S(2)}) collective-permute-start(bf16[8,16,128]{2,1,0:T(8,128)(2,1)S(1)} %get-tuple-element.46), channel_id=1, source_target_pairs={{0,8},{4,12},{8,0},{12,4},{1,9},{5,13},{9,1},{13,5},{2,10},{6,14},... | collective-permute-start | bytes 98312 | tf_op jit(solution)/shard_map/ppermute | solution.py:601
  29.4 2.9 %collective-permute-start.9 = (bf16[8,16,128]{2,1,0:T(8,128)(2,1)S(1)}, bf16[8,16,128]{2,1,0:T(8,128)(2,1)S(1)}, u32[]{:S(2)}, u32[]{:S(2)}) collective-permute-start(bf16[8,16,128]{2,1,0:T(8,128)(2,1)S(1)} %get-tuple-element.47), channel_id=1, source_target_pairs={{0,4},{4,0},{8,12},{12,8},{1,5},{5,1},{9,13},{13,9},{2,6},{6,2},{1... | collective-permute-start | bytes 98312 | tf_op jit(solution)/shard_map/ppermute | solution.py:601
  32.4 1.3 %collective-permute-done.10.refs_3_ = bf16[8,16,128]{2,1,0:T(8,128)(2,1)S(1)} collective-permute-done((bf16[8,16,128]{2,1,0:T(8,128)(2,1)S(1)}, bf16[8,16,128]{2,1,0:T(8,128)(2,1)S(1)}, u32[]{:S(2)}, u32[]{:S(2)}) %collective-permute-start.10) | collective-permute-done | bytes 32800 | tf_op jit(solution)/shard_map/ppermute | solution.py:601
  33.7 0.6 %collective-permute-done.9.refs_2_ = bf16[8,16,128]{2,1,0:T(8,128)(2,1)S(1)} collective-permute-done((bf16[8,16,128]{2,1,0:T(8,128)(2,1)S(1)}, bf16[8,16,128]{2,1,0:T(8,128)(2,1)S(1)}, u32[]{:S(2)}, u32[]{:S(2)}) %collective-permute-start.9) | collective-permute-done | bytes 32800 | tf_op jit(solution)/shard_map/ppermute | solution.py:601
  34.2 0.7 %shard_map.79 = bf16[16,16,128]{2,1,0:T(8,128)(2,1)} custom-call(bf16[8,16,128]{2,1,0:T(8,128)(2,1)S(1)} %get-tuple-element.45.refs_0_, bf16[8,16,128]{2,1,0:T(8,128)(2,1)S(1)} %collective-permute-done.8.refs_1_, bf16[8,16,128]{2,1,0:T(8,128)(2,1)S(1)} %collective-permute-done.9.refs_2_, bf16[8,16,128]{2,1,0:T(8,128)(2,1)S(1)} %collective-permute-done.10.refs_3_), custom_call_target="tpu_custom_call" | custom-call | tf_op jit(solution)/shard_map/pallas_call | solution.py:605
  (22 shorter events, 0.1 us)
Async XLA Ops:
  0.0 1.0 %copy-start.1 = (bf16[64,2,8,256]{3,2,1,0:T(8,128)(2,1)S(1)}, bf16[64,2,8,256]{3,2,1,0:T(8,128)(2,1)}, u32[]{:S(2)}) copy-start(bf16[64,2,8,256]{3,2,1,0:T(8,128)(2,1)} %param.7) | copy-start | bytes 1572868
  1.0 6.3 %copy-start = (bf16[3,3,3,128,128]{4,3,2,1,0:T(8,128)(2,1)S(1)}, bf16[3,3,3,128,128]{4,3,2,1,0:T(8,128)(2,1)}, u32[]{:S(2)}) copy-start(bf16[3,3,3,128,128]{4,3,2,1,0:T(8,128)(2,1)} %refs_5_.1) | copy-start | bytes 2654212
  1.0 6.3 %copy-start.2 = (bf16[2,2,128,32]{2,3,1,0:T(8,128)(2,1)S(1)}, bf16[2,2,128,32]{2,3,1,0:T(8,128)(2,1)}, u32[]{:S(2)}) copy-start(bf16[2,2,128,32]{2,3,1,0:T(8,128)(2,1)} %param.12) | copy-start | bytes 98308
  1.0 6.3 %copy-start.6 = (f32[128]{0:T(128)S(1)}, f32[128]{0:T(128)}, u32[]{:S(2)}) copy-start(f32[128]{0:T(128)} %param.11) | copy-start | bytes 1540
  1.6 7.5 %collective-permute-start = (bf16[1024,256]{1,0:T(8,128)(2,1)S(1)}, bf16[1024,256]{1,0:T(8,128)(2,1)S(1)}, u32[]{:S(2)}, u32[]{:S(2)}) collective-permute-start(bf16[1024,256]{1,0:T(8,128)(2,1)S(1)} %get-tuple-element.27.refs_6_), channel_id=1, source_target_pairs={{0,1},{1,0},{2,3},{3,2},{4,5},{5,4},{6,7},{7,6},{8,9},{9,8},{10,11... | collective-permute-start | bytes 1572872 | tf_op jit(solution)/shard_map/ppermute | solution.py:549
  2.1 7.0 %collective-permute-start.1 = (bf16[128,256]{1,0:T(8,128)(2,1)S(1)}, bf16[128,256]{1,0:T(8,128)(2,1)S(1)}, u32[]{:S(2)}, u32[]{:S(2)}) collective-permute-start(bf16[128,256]{1,0:T(8,128)(2,1)S(1)} %get-tuple-element.34), channel_id=1, source_target_pairs={{0,2},{2,0},{1,3},{3,1},{4,6},{6,4},{5,7},{7,5},{8,10},{10,8},{9,1... | collective-permute-start | bytes 196616 | tf_op jit(solution)/shard_map/ppermute | solution.py:37
  4.7 8.9 %collective-permute-start.3 = (bf16[512,256]{1,0:T(8,128)(2,1)S(1)}, bf16[512,256]{1,0:T(8,128)(2,1)S(1)}, u32[]{:S(2)}, u32[]{:S(2)}) collective-permute-start(bf16[512,256]{1,0:T(8,128)(2,1)S(1)} %get-tuple-element.33.refs_3_.refs_7_), channel_id=1, source_target_pairs={{1,5},{4,0},{5,9},{8,4},{9,13},{12,8},{13,12},{0,1},{3,7},{6,2},{7... | collective-permute-start | bytes 786440 | tf_op jit(solution)/shard_map/ppermute | solution.py:54
  4.8 9.3 %collective-permute-start.4 = (bf16[512,256]{1,0:T(8,128)(2,1)S(1)}, bf16[512,256]{1,0:T(8,128)(2,1)S(1)}, u32[]{:S(2)}, u32[]{:S(2)}) collective-permute-start(bf16[512,256]{1,0:T(8,128)(2,1)S(1)} %get-tuple-element.32.refs_2_.refs_6_), channel_id=1, source_target_pairs={{0,5},{5,0},{4,9},{9,4},{8,13},{13,8},{1,3},{12,14},{2,7},{7,2},{6... | collective-permute-start | bytes 786440 | tf_op jit(solution)/shard_map/ppermute | solution.py:54
  7.3 0.7 %copy-start.3 = (s32[2]{0:T(128)S(1)}, s32[2]{0:T(128)}, u32[]{:S(2)}) copy-start(s32[2]{0:T(128)} %param.8) | copy-start | bytes 28
  7.3 0.7 %copy-start.4 = (s32[1,8,1]{1,2,0:T(1,128)S(1)}, s32[1,8,1]{1,2,0:T(1,128)}, u32[]{:S(2)}) copy-start(s32[1,8,1]{1,2,0:T(1,128)} %param.13) | copy-start | bytes 100
  7.3 0.7 %copy-start.5 = (f32[128]{0:T(128)S(1)}, f32[128]{0:T(128)}, u32[]{:S(2)}) copy-start(f32[128]{0:T(128)} %param.10) | copy-start | bytes 1540
  9.3 2.1 %collective-permute-start.2 = (bf16[128,256]{1,0:T(8,128)(2,1)S(1)}, bf16[128,256]{1,0:T(8,128)(2,1)S(1)}, u32[]{:S(2)}, u32[]{:S(2)}) collective-permute-start(bf16[128,256]{1,0:T(8,128)(2,1)S(1)} %get-tuple-element.35.refs_5_.refs_9_), channel_id=1, source_target_pairs={{0,1},{1,0},{2,3},{3,2},{4,5},{5,4},{6,7},{7,6},{8,9},{9,8},{10,11... | collective-permute-start | bytes 196616 | tf_op jit(solution)/shard_map/ppermute | solution.py:556
  9.3 5.3 %collective-permute-start.5 = (bf16[80,256]{1,0:T(8,128)(2,1)S(1)}, bf16[80,256]{1,0:T(8,128)(2,1)S(1)}, u32[]{:S(2)}, u32[]{:S(2)}) collective-permute-start(bf16[80,256]{1,0:T(8,128)(2,1)S(1)} %get-tuple-element.39.refs_5_), channel_id=1, source_target_pairs={{1,5},{4,0},{5,9},{8,4},{9,13},{12,8},{13,12},{0,1},{3,7},{6,2},{7... | collective-permute-start | bytes 122888 | tf_op jit(solution)/shard_map/ppermute | solution.py:54
  9.8 4.8 %collective-permute-start.6 = (bf16[64,256]{1,0:T(8,128)(2,1)S(1)}, bf16[64,256]{1,0:T(8,128)(2,1)S(1)}, u32[]{:S(2)}, u32[]{:S(2)}) collective-permute-start(bf16[64,256]{1,0:T(8,128)(2,1)S(1)} %get-tuple-element.40), channel_id=1, source_target_pairs={{0,5},{5,0},{4,9},{9,4},{8,13},{13,8},{1,3},{12,14},{2,7},{7,2},{6... | collective-permute-start | bytes 98312 | tf_op jit(solution)/shard_map/ppermute | solution.py:54
  16.1 10.3 %collective-permute-start.7 = (bf16[13,128,256]{2,1,0:T(8,128)(2,1)S(1)}, bf16[13,128,256]{2,1,0:T(8,128)(2,1)S(1)}, u32[]{:S(2)}, u32[]{:S(2)}) collective-permute-start(bf16[13,128,256]{2,1,0:T(8,128)(2,1)S(1)} %get-tuple-element.44.refs_5_), channel_id=1, source_target_pairs={{0,1},{1,0},{2,3},{3,2},{4,5},{5,4},{6,7},{7,6},{8,9},{9,8},{10,11... | collective-permute-start | bytes 2555912 | tf_op jit(solution)/shard_map/ppermute | solution.py:584
  27.9 5.8 %collective-permute-start.10 = (bf16[8,16,128]{2,1,0:T(8,128)(2,1)S(1)}, bf16[8,16,128]{2,1,0:T(8,128)(2,1)S(1)}, u32[]{:S(2)}, u32[]{:S(2)}) collective-permute-start(bf16[8,16,128]{2,1,0:T(8,128)(2,1)S(1)} %get-tuple-element.48), channel_id=1, source_target_pairs={{0,12},{4,8},{8,4},{12,0},{1,13},{5,9},{9,5},{13,1},{2,14},{6,10},... | collective-permute-start | bytes 98312 | tf_op jit(solution)/shard_map/ppermute | solution.py:601
  28.0 5.7 %collective-permute-start.8 = (bf16[8,16,128]{2,1,0:T(8,128)(2,1)S(1)}, bf16[8,16,128]{2,1,0:T(8,128)(2,1)S(1)}, u32[]{:S(2)}, u32[]{:S(2)}) collective-permute-start(bf16[8,16,128]{2,1,0:T(8,128)(2,1)S(1)} %get-tuple-element.46), channel_id=1, source_target_pairs={{0,8},{4,12},{8,0},{12,4},{1,9},{5,13},{9,1},{13,5},{2,10},{6,14},... | collective-permute-start | bytes 98312 | tf_op jit(solution)/shard_map/ppermute | solution.py:601
  29.4 4.8 %collective-permute-start.9 = (bf16[8,16,128]{2,1,0:T(8,128)(2,1)S(1)}, bf16[8,16,128]{2,1,0:T(8,128)(2,1)S(1)}, u32[]{:S(2)}, u32[]{:S(2)}) collective-permute-start(bf16[8,16,128]{2,1,0:T(8,128)(2,1)S(1)} %get-tuple-element.47), channel_id=1, source_target_pairs={{0,4},{4,0},{8,12},{12,8},{1,5},{5,1},{9,13},{13,9},{2,6},{6,2},{1... | collective-permute-start | bytes 98312 | tf_op jit(solution)/shard_map/ppermute | solution.py:601
